TPU v7x, 32 devices: a whole 2x2x4 slice. The times are simulated.
32 devices in a mesh: dp: 2 (over x), expert: 16 (over z, y, core).
Axes of the slice: x: 2, y: 2, z: 4, core: 2. Of those that a mesh axis runs over, the one named last changes fastest.
Arguments:
- tokens: bfloat16 [2048, 3584], P('expert'), may hold values from -6 to 6
- expert_ids: int32 [2048, 8], P('expert'), may hold values from 0 to 15, all different within a row; in each aligned block of 128 rows (0 to 127, 128 to 255, ...) at most 96 rows name the same one
- route_weight: float32 [2048, 8], P('expert'), may hold values from 0.1 to 1
- pair_swap: int32 [8], replicated, may hold values from 0 to 1, as said below
- expert_gate: bfloat16 [16, 3584, 2048], P('expert', None, 'dp'), may hold values from -0.09375 to 0.09375
- expert_up: bfloat16 [16, 3584, 2048], P('expert', None, 'dp'), may hold values from -0.09375 to 0.09375
- expert_down: bfloat16 [16, 2048, 3584], P('expert', 'dp'), may hold values from -0.1875 to 0.1875
- shared_gate: bfloat16 [3584, 2048], P(None, 'dp'), may hold values from -0.09375 to 0.09375
- shared_up: bfloat16 [3584, 2048], P(None, 'dp'), may hold values from -0.09375 to 0.09375
- shared_down: bfloat16 [2048, 3584], P('dp'), may hold values from -0.1875 to 0.1875
Outputs:
- layer_out: bfloat16 [2048, 3584], P('expert', 'dp')
Inputs may be any that keep to these rules, and one draw needn't show every extreme that they name: `expert_ids`: each row names 8 different experts; within the rows of one device (aligned blocks of 128 rows) no expert is named more than 96 times, a bound that some block reaches. `pair_swap`: entry 0 is always 1; the other entries are 0 or 1.
All inputs are finite; a program needn't handle non-finite values.
Results may differ from a plain program's by a relative error of at most 0.012.
Values may be sent and summed in bfloat16 or wider, within the bound.
No kernel may reach another device: no remote copies, remote signals or barrier semaphores. Data moves between devices by JAX's collectives and lax.ppermute only.
A program may use at most 192 MiB of HBM per device.

v0:
```python
import jax
import jax.numpy as jnp
from jax import lax
from jax.sharding import PartitionSpec as P

routed_scale = 2.5


def from_partner(value, axis, stride):
    mask = 2**stride
    pairs = [(source, source ^ mask) for source in range(lax.axis_size(axis))]
    return lax.ppermute(value, axis, pairs)


def local(
    tokens,
    expert_ids,
    route_weight,
    pair_swap,
    expert_gate,
    expert_up,
    expert_down,
    shared_gate,
    shared_up,
    shared_down,
):
    tok_count, top_count = expert_ids.shape
    width = tokens.shape[1]
    experts = lax.axis_size("expert")
    half_axis = experts // 2
    capacity = 3 * tok_count * top_count // (2 * experts)
    column = lax.axis_index("expert")
    gate_block = expert_gate[0]
    up_block = expert_up[0]
    down_block = expert_down[0]
    swap_bit = experts.bit_length() - 2
    moved = from_partner((gate_block, up_block, down_block), "expert", swap_bit)
    keep_flag = pair_swap[column % half_axis] == 1
    gate_block = jnp.where(keep_flag, moved[0], gate_block)
    up_block = jnp.where(keep_flag, moved[1], up_block)
    down_block = jnp.where(keep_flag, moved[2], down_block)
    flat_target = expert_ids.reshape(-1)
    onehot = (flat_target[:, None] == jnp.arange(experts, dtype=jnp.int32)[None, :]).astype(
        jnp.int32
    )
    before = jnp.cumsum(onehot, axis=0) - onehot
    slot_index = jnp.sum(before * onehot, axis=1)
    position = flat_target * capacity + slot_index
    owner_row = jnp.arange(tok_count * top_count, dtype=jnp.int32) // top_count
    source_row = jnp.full((experts * capacity,), tok_count, jnp.int32).at[position].set(owner_row)
    padded = jnp.concatenate([tokens, jnp.zeros((1, width), tokens.dtype)], axis=0)
    mix = route_weight / jnp.sum(route_weight, axis=1, keepdims=True)
    shared_gv = jnp.dot(tokens, shared_gate, preferred_element_type=jnp.float32)
    shared_uv = jnp.dot(tokens, shared_up, preferred_element_type=jnp.float32)
    shared_act = (jax.nn.silu(shared_gv) * shared_uv).astype(jnp.bfloat16)
    shared_out = jnp.dot(shared_act, shared_down, preferred_element_type=jnp.float32)
    send_rows = jnp.take(padded, source_row, axis=0).reshape(experts, capacity, width)
    received = lax.all_to_all(send_rows, "expert", split_axis=0, concat_axis=0, tiled=True)
    sources, items, row_width = received.shape
    flat_rows = received.reshape(sources * items, row_width)
    gate_val = jnp.dot(flat_rows, gate_block, preferred_element_type=jnp.float32)
    up_val = jnp.dot(flat_rows, up_block, preferred_element_type=jnp.float32)
    act = (jax.nn.silu(gate_val) * up_val).astype(jnp.bfloat16)
    partial_out = jnp.dot(act, down_block, preferred_element_type=jnp.float32).astype(jnp.bfloat16)
    partial_out = partial_out.reshape(sources, items, row_width)
    returned = lax.all_to_all(partial_out, "expert", split_axis=0, concat_axis=0, tiled=True)
    back_rows = returned.reshape(experts * capacity, width)
    picked = jnp.take(back_rows, position, axis=0).reshape(tok_count, top_count, width)
    routed = jnp.zeros((tok_count, width), jnp.float32)
    for choice_index in range(top_count):
        routed = routed + mix[:, choice_index : choice_index + 1] * picked[:, choice_index].astype(
            jnp.float32
        )
    term = shared_out + routed_scale * routed
    summed = lax.psum_scatter(term, "dp", scatter_dimension=1, tiled=True)
    return summed.astype(jnp.bfloat16)


def solution(mesh):
    in_specs = (
        P("expert", None),
        P("expert", None),
        P("expert", None),
        P(),
        P("expert", None, "dp"),
        P("expert", None, "dp"),
        P("expert", "dp", None),
        P(None, "dp"),
        P(None, "dp"),
        P("dp", None),
    )
    out_specs = P("expert", "dp")
    return jax.shard_map(local, mesh=mesh, in_specs=in_specs, out_specs=out_specs, check_vma=False)
```

profile of v0, /device:TPU:8, one launch (start us, length us, event | category | flops | bytes accessed | tf_op | source)
XLA Modules:
  0.0 1574.4 jit_solution(8009057186696195412)
XLA Ops:
  6.5 0.8 copy.20
  7.3 0.1 eq.34
  7.4 0.1 reshape.102
  7.5 0.7 broadcast_multiply_fusion
  8.2 4.5 reduce-window.6
  12.8 0.1 copy.22
  13.0 0.1 broadcast_add_fusion
  13.1 0.1 copy.25
  13.2 0.1 mul.129
  13.4 4.3 scatter_custom_fusion
  17.8 1.2 concatenate.3
  19.1 9.1 gather_fusion
  28.2 9.9 broadcast_select_fusion
  38.1 6.4 all-to-all-start
  44.5 2.4 collective-permute-start.1
  47.0 0.6 collective-permute-start
  47.5 2.4 collective-permute-start.2
  49.9 0.6 dynamic_slice.3
  51.1 859.9 %collective-permute-done.1 = bf16[3584,1024]{1,0:T(8,128)(2,1)} collective-permute-done((bf16[3584,1024]{1,0:T(8,128)(2,1)}, bf16[3584,1024]{1,0:T(8,128)(2,1)}, u32[]{:S(2)}, u32[]{:S(2)}) %collective-permute-start.1) | collective-permute-done | bytes 7340064 | tf_op jit(solution)/shard_map/ppermute | solution.py:12
  911.1 19.8 %fusion.1 = f32[1536,1024]{1,0:T(8,128)} fusion(bf16[1536,3584]{1,0:T(8,128)(2,1)} %bitcast.6, bf16[3584,1024]{1,0:T(8,128)(2,1)} %collective-permute-done.1, pred[]{:T(512)} %bitcast.7, bf16[1,3584,1024]{2,1,0:T(8,128)(2,1)} %param.15), kind=kOutput, calls=%fused_computation.7 | convolution fusion | flops 11277959168 | bytes 31981568 | tf_op jit(solution)/shard_map/dot_general | solution.py:62
  930.8 137.5 %collective-permute-done = bf16[3584,1024]{1,0:T(8,128)(2,1)} collective-permute-done((bf16[3584,1024]{1,0:T(8,128)(2,1)}, bf16[3584,1024]{1,0:T(8,128)(2,1)}, u32[]{:S(2)}, u32[]{:S(2)}) %collective-permute-start) | collective-permute-done | bytes 7340064 | tf_op jit(solution)/shard_map/ppermute | solution.py:12
  1068.4 19.9 %fusion.3 = f32[1536,1024]{1,0:T(8,128)} fusion(bf16[1536,3584]{1,0:T(8,128)(2,1)} %bitcast.6, bf16[3584,1024]{1,0:T(8,128)(2,1)} %collective-permute-done, pred[]{:T(512)} %bitcast.7, bf16[1,3584,1024]{2,1,0:T(8,128)(2,1)} %param.14), kind=kOutput, calls=%fused_computation.9 | convolution fusion | flops 11277959168 | bytes 31981568 | tf_op jit(solution)/shard_map/dot_general | solution.py:61
  1088.3 136.9 %collective-permute-done.2 = bf16[1024,3584]{1,0:T(8,128)(2,1)} collective-permute-done((bf16[1024,3584]{1,0:T(8,128)(2,1)}, bf16[1024,3584]{1,0:T(8,128)(2,1)}, u32[]{:S(2)}, u32[]{:S(2)}) %collective-permute-start.2) | collective-permute-done | bytes 7340064 | tf_op jit(solution)/shard_map/ppermute | solution.py:12
  1225.2 22.8 %convolution_convert_fusion = bf16[1536,3584]{1,0:T(8,128)(2,1)} fusion(bf16[1024,3584]{1,0:T(8,128)(2,1)} %collective-permute-done.2, pred[]{:T(512)} %bitcast.7, f32[1536,1024]{1,0:T(8,128)} %fusion.1, f32[1536,1024]{1,0:T(8,128)} %fusion.3, bf16[1,1024,3584]{2,1,0:T(8,128)(2,1)} %param.16), kind=kOutput, calls=%fused_computation.3 | convolution fusion | flops 11292901376 | bytes 38273024 | tf_op jit(solution)/shard_map/dot_general | solution.py:64
  1248.0 8.2 all-to-all-start.1
  1256.5 4.2 fusion.38
  1260.8 232.4 %all-to-all-done.1 = bf16[16,96,3584]{2,1,0:T(8,128)(2,1)} async-done(((bf16[16,96,3584]{2,1,0:T(8,128)(2,1)}), bf16[16,96,3584]{2,1,0:T(8,128)(2,1)}, u32[]{:S(2)}, u32[]{:S(2)}) %all-to-all-start.1) | async-done | bytes 11010080 | tf_op jit(solution)/shard_map/all_to_all | solution.py:66
  1493.1 19.6 %gather_fusion.1 = bf16[1024,3584]{1,0:T(8,128)(2,1)} fusion(bf16[1536,3584]{1,0:T(8,128)(2,1)} %bitcast.12, s32[1024]{0:T(1024)S(1)} %broadcast_clamp_fusion), kind=kCustom, calls=%fused_computation.1 | custom fusion | bytes 14684160 | tf_op jit(solution)/shard_map/jit(_take)/gather | solution.py:68
  1512.7 10.8 copy_select_fusion
  1523.6 11.4 convolution_add_fusion
  1535.1 30.5 %reduce-scatter.2.cloned.1.call-done = f32[128,1792]{1,0:T(8,128)} async-done(((f32[128,3584]{1,0:T(8,128)}), f32[128,1792]{1,0:T(8,128)}) %reduce-scatter.2.cloned.1.call-update) | async-done | bytes 917520 | tf_op jit(solution)/shard_map/reduce_scatter | solution.py:75
  1565.6 2.0 convert_element_type.88
  (30 shorter events, 0.6 us)
Async XLA Ops:
  38.1 11.8 copy-start.3
  38.1 873.0 %all-to-all-start = ((bf16[16,96,3584]{2,1,0:T(8,128)(2,1)}), bf16[16,96,3584]{2,1,0:T(8,128)(2,1)}, u32[]{:S(2)}, u32[]{:S(2)}) async-start(bf16[16,96,3584]{2,1,0:T(8,128)(2,1)} %broadcast_select_fusion), calls=%async_computation | async-start | bytes 22020096 | tf_op jit(solution)/shard_map/all_to_all | solution.py:58
  44.5 866.5 %collective-permute-start.1 = (bf16[3584,1024]{1,0:T(8,128)(2,1)}, bf16[3584,1024]{1,0:T(8,128)(2,1)}, u32[]{:S(2)}, u32[]{:S(2)}) collective-permute-start(bf16[3584,1024]{1,0:T(8,128)(2,1)} %bitcast.112), channel_id=1, source_target_pairs={{0,8},{1,9},{2,10},{3,11},{4,12},{5,13},{6,14},{7,15},{8,0},{9,1},... | collective-permute-start | bytes 22020104 | tf_op jit(solution)/shard_map/ppermute | solution.py:12
  47.0 1021.4 %collective-permute-start = (bf16[3584,1024]{1,0:T(8,128)(2,1)}, bf16[3584,1024]{1,0:T(8,128)(2,1)}, u32[]{:S(2)}, u32[]{:S(2)}) collective-permute-start(bf16[3584,1024]{1,0:T(8,128)(2,1)} %bitcast.113), channel_id=1, source_target_pairs={{0,8},{1,9},{2,10},{3,11},{4,12},{5,13},{6,14},{7,15},{8,0},{9,1},... | collective-permute-start | bytes 22020104 | tf_op jit(solution)/shard_map/ppermute | solution.py:12
  47.5 1177.7 %collective-permute-start.2 = (bf16[1024,3584]{1,0:T(8,128)(2,1)}, bf16[1024,3584]{1,0:T(8,128)(2,1)}, u32[]{:S(2)}, u32[]{:S(2)}) collective-permute-start(bf16[1024,3584]{1,0:T(8,128)(2,1)} %bitcast.114), channel_id=1, source_target_pairs={{0,8},{1,9},{2,10},{3,11},{4,12},{5,13},{6,14},{7,15},{8,0},{9,1},... | collective-permute-start | bytes 22020104 | tf_op jit(solution)/shard_map/ppermute | solution.py:12
  1248.0 8.4 copy-start.2
  1248.0 8.5 copy-start.1
  1248.0 8.5 copy-start
  1248.0 245.1 %all-to-all-start.1 = ((bf16[16,96,3584]{2,1,0:T(8,128)(2,1)}), bf16[16,96,3584]{2,1,0:T(8,128)(2,1)}, u32[]{:S(2)}, u32[]{:S(2)}) async-start(bf16[16,96,3584]{2,1,0:T(8,128)(2,1)} %bitcast.106), calls=%async_computation.1 | async-start | bytes 22020096 | tf_op jit(solution)/shard_map/all_to_all | solution.py:66
  1256.2 309.3 %reduce-scatter.2.cloned.1.call-start = ((), (), s32[]{:S(2)}) async-start(), calls=%async_computation.3 | async-start | bytes 2752512 | tf_op jit(solution)/shard_map/reduce_scatter | solution.py:75
Sparse Core Ops, SparseCore 0:
  1535.2 30.3 reduce-scatter.1
where the time goes:
time: 1580 us; the launch traced here: 1570 us
  waiting for transfers between devices  1400 us (89%)
  matrix products  78.2 us (5%)
  local copies, waits for them, and re-layouts  36.5 us (2%)
  other arithmetic  28.2 us (2%)
  starting transfers between devices  20 us (1%)
    ppermute x3, waiting for transfers between devices, from_partner(): return lax.ppermute(value, axis, pairs)  1130 us
    all_to_all x1, waiting for transfers between devices, local(): lax.all_to_all(partial_out, 'expert', split_axis=0, concat_axis=0, tiled=...  232 us
  transfers between devices with their start and end apart: 6, of which 5 were waited for; matrix products, arithmetic and copies ran while one was open for 3% of the time, Pallas kernels for 0%

commit v1 on v0

v1 whole, which is shorter than its diff:
```python
import functools

import jax
import jax.numpy as jnp
from jax import lax
from jax.experimental import pallas as pl
from jax.experimental.pallas import tpu as pltpu
from jax.sharding import PartitionSpec as P

routed_scale = 2.5
LANES = 128
TILE = 256
VMEM = 52 * 1024 * 1024


def exchange(value, axis, mask):
    pairs = [(source, source ^ mask) for source in range(lax.axis_size(axis))]
    return lax.ppermute(value, axis, pairs)


def widen_body(experts, share, n_dp, info, tokens, ids, weight, rows, carried):
    count, width = tokens.shape
    rates = weight[...]
    rates = routed_scale * rates / jnp.sum(rates, axis=1, keepdims=True)
    lane = lax.broadcasted_iota(jnp.int32, (count, LANES), 1)
    total = jnp.zeros((count, LANES), jnp.float32)
    for choice in range(ids.shape[1]):
        total += jnp.where(ids[:, choice : choice + 1] == lane % experts, rates[:, choice : choice + 1], 0.0)
    high = total.astype(jnp.bfloat16).astype(jnp.float32)
    middle = (total - high).astype(jnp.bfloat16).astype(jnp.float32)
    low = total - high - middle
    term = lane // experts
    held = jnp.where(term == 0, high, jnp.where(term == 1, middle, jnp.where(term == 2, low, 0.0)))
    rows[:, :width] = tokens[...]
    rows[:, width:] = held.astype(jnp.bfloat16)
    if carried is not None:
        start = pl.multiple_of(info[0] * share, 16)
        carried[:share, :] = rows[pl.ds(start, share), :]
        carried[share:, :] = rows[n_dp * share :, :]


def widen(tokens, ids, weight, info, experts, share, n_dp):
    count, width = tokens.shape
    shapes = [jax.ShapeDtypeStruct((count, width + LANES), tokens.dtype)]
    if share:
        shapes.append(jax.ShapeDtypeStruct((count - (n_dp - 1) * share, width + LANES), tokens.dtype))

    def body(info_ref, tokens_ref, ids_ref, weight_ref, *outs):
        widen_body(experts, share, n_dp, info_ref, tokens_ref, ids_ref, weight_ref, outs[0], outs[1] if share else None)

    out = pl.pallas_call(
        body,
        out_shape=shapes,
        in_specs=[pl.BlockSpec(memory_space=pltpu.SMEM)] + [pl.BlockSpec(memory_space=pltpu.VMEM)] * 3,
        out_specs=[pl.BlockSpec(memory_space=pltpu.VMEM)] * len(shapes),
        compiler_params=pltpu.CompilerParams(vmem_limit_bytes=16 * 1024 * 1024),
        name="widen",
    )(info, tokens, ids, weight)
    return out[0], out[1] if share else out[0]


def ffn_body(layout, experts, blocks, out_rows, scaled, n_in, n_out, *refs):
    info = refs[0]
    inputs = refs[1 : 1 + n_in]
    gate, up, down = refs[1 + n_in : 4 + n_in]
    outs = refs[4 + n_in : 4 + n_in + n_out]
    x, gate_v, up_v, down_v, act, result, x_sem, gate_sem, up_sem, down_sem, out_sem = refs[4 + n_in + n_out :]
    width, hidden = gate.shape
    steps = hidden // TILE
    per_block = width // blocks // TILE
    dp = info[0]

    copies = []
    for number, (which, source, size, fixed, unit, flip) in enumerate(layout):
        start = fixed
        if unit:
            start = pl.multiple_of(fixed + (dp ^ flip) * unit, 16)
        copies.append(
            pltpu.make_async_copy(
                inputs[which].at[pl.ds(source, size), :], x.at[pl.ds(start, size), :], x_sem.at[number]
            )
        )

    def side(weights, held, sems, j):
        return pltpu.make_async_copy(
            weights.at[:, pl.ds(pl.multiple_of(j * TILE, TILE), TILE)], held.at[j], sems.at[j]
        )

    def lower(i):
        column = ((i // per_block) ^ dp if blocks > 1 else 0) * (width // blocks) + (i % per_block) * TILE
        return pltpu.make_async_copy(
            down.at[:, pl.ds(pl.multiple_of(column, TILE), TILE)], down_v.at[i], down_sem.at[i]
        )

    def leave(i):
        given = []
        for number, (first, count) in enumerate(out_rows):
            given.append(
                pltpu.make_async_copy(
                    result.at[i, pl.ds(first, count), :],
                    outs[number].at[i // per_block, :, pl.ds(pl.multiple_of((i % per_block) * TILE, TILE), TILE)],
                    out_sem.at[i, number],
                )
            )
        return given

    for copy in copies:
        copy.start()
    for j in range(steps):
        side(gate, gate_v, gate_sem, j).start()
        side(up, up_v, up_sem, j).start()
    for i in range(blocks * per_block):
        lower(i).start()
    for copy in copies:
        copy.wait()

    def first(j, carry):
        side(gate, gate_v, gate_sem, j).wait()
        side(up, up_v, up_sem, j).wait()
        rows = x[:, :width]
        gate_val = jnp.dot(rows, gate_v[j], preferred_element_type=jnp.float32)
        up_val = jnp.dot(rows, up_v[j], preferred_element_type=jnp.float32)
        value = gate_val / (1.0 + jnp.exp(-gate_val)) * up_val
        act[:, pl.ds(pl.multiple_of(j * TILE, TILE), TILE)] = value.astype(act.dtype)
        return carry

    lax.fori_loop(0, steps, first, 0)

    if scaled:
        held = x[:, width:].astype(jnp.float32)
        lane = lax.broadcasted_iota(jnp.int32, held.shape, 1)
        factor = jnp.sum(jnp.where(lane % experts == info[1], held, 0.0), axis=1, keepdims=True)

    def second(i, carry):
        lower(i).wait()
        value = jnp.dot(act[...], down_v[i], preferred_element_type=jnp.float32)
        if scaled:
            value = value * factor
        result[i] = value.astype(result.dtype)
        for copy in leave(i):
            copy.start()
        return carry

    lax.fori_loop(0, blocks * per_block, second, 0)

    def finish(i, carry):
        for copy in leave(i):
            copy.wait()
        return carry

    lax.fori_loop(0, blocks * per_block, finish, 0)


def ffn(info, inputs, layout, gate, up, down, experts, blocks, out_rows, scaled, dtype, name):
    width, hidden = gate.shape
    row_width = inputs[0].shape[1]
    rows = sum(count for _, count in out_rows)
    tiles = width // TILE
    steps = hidden // TILE
    flops = 6 * rows * width * hidden
    body = functools.partial(ffn_body, layout, experts, blocks, out_rows, scaled, len(inputs), len(out_rows))
    return pl.pallas_call(
        body,
        out_shape=[jax.ShapeDtypeStruct((blocks, count, width // blocks), dtype) for _, count in out_rows],
        in_specs=[pl.BlockSpec(memory_space=pltpu.SMEM)] + [pl.BlockSpec(memory_space=pl.ANY)] * (len(inputs) + 3),
        out_specs=[pl.BlockSpec(memory_space=pl.ANY)] * len(out_rows),
        scratch_shapes=[
            pltpu.VMEM((rows, row_width), jnp.bfloat16),
            pltpu.VMEM((steps, width, TILE), jnp.bfloat16),
            pltpu.VMEM((steps, width, TILE), jnp.bfloat16),
            pltpu.VMEM((tiles, hidden, TILE), jnp.bfloat16),
            pltpu.VMEM((rows, hidden), jnp.bfloat16),
            pltpu.VMEM((tiles, rows, TILE), dtype),
            pltpu.SemaphoreType.DMA((len(layout),)),
            pltpu.SemaphoreType.DMA((steps,)),
            pltpu.SemaphoreType.DMA((steps,)),
            pltpu.SemaphoreType.DMA((tiles,)),
            pltpu.SemaphoreType.DMA((tiles, len(out_rows))),
        ],
        compiler_params=pltpu.CompilerParams(vmem_limit_bytes=VMEM),
        cost_estimate=pl.CostEstimate(
            flops=flops, bytes_accessed=6 * width * hidden + 4 * rows * width, transcendentals=rows * hidden
        ),
        name=name,
    )(info, *inputs, gate, up, down)


def local(
    tokens,
    expert_ids,
    route_weight,
    pair_swap,
    expert_gate,
    expert_up,
    expert_down,
    shared_gate,
    shared_up,
    shared_down,
):
    count, width = tokens.shape
    experts = lax.axis_size("expert")
    n_dp = lax.axis_size("dp")
    half_axis = experts // 2
    column = lax.axis_index("expert")
    dp = lax.axis_index("dp")
    mine = jnp.where(pair_swap[column % half_axis] == 1, (column + half_axis) % experts, column)
    info = jnp.stack([dp, mine]).astype(jnp.int32)
    share = 3 * count // (4 * n_dp) // 16 * 16
    blocks = n_dp if (width // n_dp) % TILE == 0 else 1
    f32, bf16 = jnp.float32, jnp.bfloat16
    wide, carried = widen(tokens, expert_ids, route_weight, info, experts, share, n_dp)

    def by_dp(value):
        if blocks == n_dp:
            return value
        rows = value.shape[1]
        parts = value.reshape(rows, n_dp, width // n_dp)
        return jnp.take(parts, dp ^ jnp.arange(n_dp), axis=1).transpose(1, 0, 2)

    weights = (expert_gate[0], expert_up[0], expert_down[0])
    kept_rows = ((0, 2 * count), (2 * count, 2 * count))

    def gathered(distance):
        if distance == 0:
            across = exchange(wide, "expert", 2)
            inputs = [wide, across, exchange(wide, "expert", 1), exchange(across, "expert", 1)]
            layout = tuple((which, 0, count, which * count, 0, 0) for which in range(4))
            return inputs, layout
        mine_rows = exchange(carried, "expert", 4 * distance)
        across = exchange(mine_rows, "expert", 2)
        parts = [mine_rows, across]
        if share:
            both = jnp.concatenate([mine_rows[:share], across[:share]], axis=0)
            for flip in range(1, n_dp):
                parts.append(exchange(both, "dp", flip))
        own = jnp.concatenate(parts, axis=0)
        other = exchange(own, "expert", 1)
        held = carried.shape[0]
        layout = []
        for which in range(2):
            for shard in range(2):
                base = (2 * which + shard) * count
                at = shard * held
                if share:
                    layout.append((which, at, share, base, share, 0))
                if held > share:
                    layout.append((which, at + share, held - share, base + n_dp * share, 0, 0))
                for flip in range(1, n_dp if share else 1):
                    layout.append((which, 2 * held + (2 * flip - 2 + shard) * share, share, base, share, flip))
        return [own, other], tuple(layout)

    def spread(kept, sent, extra, across_first):
        kept, met = by_dp(kept), exchange(by_dp(sent), "expert", 1)
        if across_first:
            outer = (kept[:, count:].astype(f32) + met[:, count:].astype(f32)).astype(bf16)
            came = exchange(outer, "expert", 2)
            total = kept[:, :count].astype(f32) + met[:, :count].astype(f32) + came.astype(f32)
            if extra is not None:
                total = total + by_dp(extra)
            result = total[0]
            for flip in range(1, n_dp):
                result = result + exchange(total[flip].astype(bf16), "dp", flip).astype(f32)
            return result
        total = kept[0].astype(f32) + met[0].astype(f32)
        for flip in range(1, n_dp):
            outer = (kept[flip].astype(f32) + met[flip].astype(f32)).astype(bf16)
            total = total + exchange(outer, "dp", flip).astype(f32)
        came = exchange(total[count:].astype(bf16), "expert", 2)
        return total[:count] + came.astype(f32)

    shared_part = ffn(
        info,
        [tokens],
        ((0, 0, count, 0, 0, 0),),
        shared_gate,
        shared_up,
        shared_down,
        experts,
        blocks,
        ((0, count),),
        False,
        f32,
        "shared_expert",
    )[0]
    answer = None
    for distance in range(experts // 4):
        inputs, layout = gathered(distance)
        kept, sent = ffn(
            info, inputs, layout, *weights, experts, blocks, kept_rows, True, bf16, "routed_expert"
        )
        part = spread(kept, sent, shared_part if distance == 0 else None, distance % 2 == 0)
        if distance:
            part = exchange(part.astype(bf16), "expert", 4 * distance).astype(f32)
        answer = part if answer is None else answer + part
    return answer.astype(bf16)


def solution(mesh):
    in_specs = (
        P("expert", None),
        P("expert", None),
        P("expert", None),
        P(),
        P("expert", None, "dp"),
        P("expert", None, "dp"),
        P("expert", "dp", None),
        P(None, "dp"),
        P(None, "dp"),
        P("dp", None),
    )
    out_specs = P("expert", "dp")
    return jax.shard_map(local, mesh=mesh, in_specs=in_specs, out_specs=out_specs, check_vma=False)
```

time: 1580 us -> 293 us (0.19)
  waiting for transfers between devices: 1400 us -> 133 us
  Pallas kernels: 0 us -> 110 us
  matrix products: 78.2 us -> 0 us
  local copies, waits for them, and re-layouts: 36.5 us -> 11.5 us
  other arithmetic: 28.2 us -> 9.54 us
    ppermute x3 -> x30, waiting for transfers between devices: 1130 us -> 133 us  [exchange(): return lax.ppermute(value, axis, pairs)]
    all_to_all x2 -> x0, waiting for transfers between devices: 232 us -> none  [the longest x1 232 us: local(): lax.all_to_all(partial_out, 'expert', split_axis=0, concat_axis=0, tiled=...]
    pallas_call x0 -> x6, Pallas kernels: none -> 110 us  [the longest x5 109 us: ffn(): pl.pallas_call(body, out_shape=[jax.ShapeDtypeStruct((blocks, count, widt...]
    dot_general x5 -> x0, matrix products: 78.2 us -> none  [the longest x1 22.8 us: local(): jnp.dot(act, down_block, preferred_element_type=jnp.float32)]
    reduce_scatter x1 -> x0, waiting for transfers between devices: 30.5 us -> none  [local(): summed = lax.psum_scatter(term, 'dp', scatter_dimension=1, tiled=True)]
    gather x2 -> x0, local copies, waits for them, and re-layouts: 28.7 us -> none  [the longest x1 19.6 us: local(): jnp.take(back_rows, position, axis=0).reshape(tok_count, top_count, width)]
    ppermute x3 -> x30, starting transfers between devices: 5.35 us -> 27.6 us  [exchange(): return lax.ppermute(value, axis, pairs)]
    select_n x5 -> x0, other arithmetic: 20.8 us -> none  [the longest x2 10.9 us: local(): jnp.take(back_rows, position, axis=0).reshape(tok_count, top_count, width)]
  transfers between devices with their start and end apart: 6 -> 30, of which waited for: 5 -> 12; matrix products, arithmetic and copies ran while one was open for 3% -> 4% of each run, Pallas kernels for 0% -> 37%
where the time goes in v1:
time: 293 us
  waiting for transfers between devices  133 us (45%)
  Pallas kernels  110 us (38%)
  starting transfers between devices  27.6 us (9%)
  local copies, waits for them, and re-layouts  11.5 us (4%)
  other arithmetic  9.54 us (3%)
    ppermute x30, waiting for transfers between devices, exchange(): return lax.ppermute(value, axis, pairs)  133 us
    pallas_call x5, Pallas kernels, ffn(): pl.pallas_call(body, out_shape=[jax.ShapeDtypeStruct((blocks, count, widt...  109 us
    ppermute x30, starting transfers between devices, exchange(): return lax.ppermute(value, axis, pairs)  27.6 us
    unnamed x28, local copies, waits for them, and re-layouts  8.91 us
  transfers between devices with their start and end apart: 30, of which 12 were waited for; matrix products, arithmetic and copies ran while one was open for 4% of the time, Pallas kernels for 37%

profile of v1, /device:TPU:8, one launch (start us, length us, event | category | flops | bytes accessed | tf_op | source)
XLA Modules:
  0.0 292.8 jit_solution(6716709229308342578)
XLA Ops:
  5.9 3.0 %collective-permute-start.14 = (bf16[80,3712]{1,0:T(8,128)(2,1)S(1)}, bf16[80,3712]{1,0:T(8,128)(2,1)S(1)}, u32[]{:S(2)}, u32[]{:S(2)}) collective-permute-start(bf16[80,3712]{1,0:T(8,128)(2,1)S(1)} %get-tuple-element.18), channel_id=1, source_target_pairs={{0,8},{1,9},{2,10},{3,11},{4,12},{5,13},{6,14},{7,15},{8,0},{9,1},... | collective-permute-start | bytes 1781768 | tf_op jit(solution)/shard_map/ppermute | solution.py:18
  9.3 1.5 collective-permute-start
  12.0 13.2 %shared_expert.1 = f32[2,128,1792]{2,1,0:T(8,128)} custom-call(s32[2]{0:T(128)S(1)} %pad_add_fusion.info_ref.refs_0_, bf16[128,3584]{1,0:T(8,128)(2,1)S(1)} %copy-done.1, bf16[3584,1024]{1,0:T(8,128)(2,1)} %refs_2_.1, bf16[3584,1024]{1,0:T(8,128)(2,1)} %refs_3_.1, bf16[1024,3584]{1,0:T(8,128)(2,1)} %refs_4_.1), custom_call_target="tpu_custom_call" | custom-call | flops 2818572288 | bytes 23855104 | tf_op jit(solution)/shard_map/shared_expert/pallas_call | solution.py:162
  25.3 5.5 %collective-permute-done.6 = bf16[80,3712]{1,0:T(8,128)(2,1)S(1)} collective-permute-done((bf16[80,3712]{1,0:T(8,128)(2,1)S(1)}, bf16[80,3712]{1,0:T(8,128)(2,1)S(1)}, u32[]{:S(2)}, u32[]{:S(2)}) %collective-permute-start.6) | collective-permute-done | bytes 593952 | tf_op jit(solution)/shard_map/ppermute | solution.py:18
  30.8 1.7 collective-permute-start.7
  32.6 15.6 %collective-permute-done.14 = bf16[80,3712]{1,0:T(8,128)(2,1)S(1)} collective-permute-done((bf16[80,3712]{1,0:T(8,128)(2,1)S(1)}, bf16[80,3712]{1,0:T(8,128)(2,1)S(1)}, u32[]{:S(2)}, u32[]{:S(2)}) %collective-permute-start.14) | collective-permute-done | bytes 593952 | tf_op jit(solution)/shard_map/ppermute | solution.py:18
  48.2 1.6 collective-permute-start.15
  49.8 10.6 %collective-permute-done.22 = bf16[80,3712]{1,0:T(8,128)(2,1)S(1)} collective-permute-done((bf16[80,3712]{1,0:T(8,128)(2,1)S(1)}, bf16[80,3712]{1,0:T(8,128)(2,1)S(1)}, u32[]{:S(2)}, u32[]{:S(2)}) %collective-permute-start.22) | collective-permute-done | bytes 593952 | tf_op jit(solution)/shard_map/ppermute | solution.py:18
  61.4 1.6 collective-permute-start.23
  63.2 1.6 collective-permute-start.8
  65.4 10.0 %collective-permute-done.23 = bf16[80,3712]{1,0:T(8,128)(2,1)S(1)} collective-permute-done((bf16[80,3712]{1,0:T(8,128)(2,1)S(1)}, bf16[80,3712]{1,0:T(8,128)(2,1)S(1)}, u32[]{:S(2)}, u32[]{:S(2)}) %collective-permute-start.23) | collective-permute-done | bytes 593952 | tf_op jit(solution)/shard_map/ppermute | solution.py:18
  75.5 1.6 collective-permute-start.24
  79.5 23.8 %routed_expert.4 = (bf16[2,256,1792]{2,1,0:T(8,128)(2,1)}, bf16[2,256,1792]{2,1,0:T(8,128)(2,1)}) custom-call(s32[2]{0:T(128)S(1)} %pad_add_fusion.info_ref.refs_0_, bf16[128,3712]{1,0:T(8,128)(2,1)S(1)} %get-tuple-element.15.refs_1_, bf16[128,3712]{1,0:T(8,128)(2,1)S(1)} %collective-permute-done.refs_2_, bf16[128,3712]{1,0:T(8,128)(2,1)} %copy-done.8, ...), custom_call_target="tpu_custom_call" | custom-call | flops 11274289152 | bytes 29360128 | tf_op jit(solution)/shard_map/routed_expert/pallas_call | solution.py:162
  105.9 6.2 %collective-permute-done.24 = bf16[96,3712]{1,0:T(8,128)(2,1)S(1)} collective-permute-done((bf16[96,3712]{1,0:T(8,128)(2,1)S(1)}, bf16[96,3712]{1,0:T(8,128)(2,1)S(1)}, u32[]{:S(2)}, u32[]{:S(2)}) %collective-permute-start.24) | collective-permute-done | bytes 712736 | tf_op jit(solution)/shard_map/ppermute | solution.py:18
  114.7 24.1 %routed_expert.5 = (bf16[2,256,1792]{2,1,0:T(8,128)(2,1)S(1)}, bf16[2,256,1792]{2,1,0:T(8,128)(2,1)}) custom-call(s32[2]{0:T(128)S(1)} %pad_add_fusion.info_ref.refs_0_, bf16[256,3712]{1,0:T(8,128)(2,1)} %copy-done.4, bf16[256,3712]{1,0:T(8,128)(2,1)} %collective-permute-done.9.refs_2_, bf16[3584,1024]{1,0:T(8,128)(2,1)} %bitcast.37, ...), custom_call_target="tpu_custom_call" | custom-call | flops 11274289152 | bytes 29360128 | tf_op jit(solution)/shard_map/routed_expert/pallas_call | solution.py:162
  139.1 24.1 %routed_expert.6 = (bf16[2,256,1792]{2,1,0:T(8,128)(2,1)S(1)}, bf16[2,256,1792]{2,1,0:T(8,128)(2,1)}) custom-call(s32[2]{0:T(128)S(1)} %pad_add_fusion.info_ref.refs_0_, bf16[256,3712]{1,0:T(8,128)(2,1)} %copy-done.7, bf16[256,3712]{1,0:T(8,128)(2,1)} %collective-permute-done.17.refs_2_, bf16[3584,1024]{1,0:T(8,128)(2,1)} %bitcast.38, ...), custom_call_target="tpu_custom_call" | custom-call | flops 11274289152 | bytes 29360128 | tf_op jit(solution)/shard_map/routed_expert/pallas_call | solution.py:162
  163.6 24.1 %routed_expert.7 = (bf16[2,256,1792]{2,1,0:T(8,128)(2,1)S(1)}, bf16[2,256,1792]{2,1,0:T(8,128)(2,1)}) custom-call(s32[2]{0:T(128)S(1)} %pad_add_fusion.info_ref.refs_0_, bf16[256,3712]{1,0:T(8,128)(2,1)} %constant_dynamic-update-slice_fusion.6.refs_1_, bf16[256,3712]{1,0:T(8,128)(2,1)} %collective-permute-done.25.refs_2_, bf16[3584,1024]{1,0:T(8,128)(2,1)} %bitcast.39, ...), custom_call_target="tpu_custom_call" | custom-call | flops 11274289152 | bytes 29360128 | tf_op jit(solution)/shard_map/routed_expert/pallas_call | solution.py:162
  188.4 1.6 collective-permute-start.5
  193.4 1.6 collective-permute-start.19
  195.2 1.6 collective-permute-start.27
  196.8 24.7 %collective-permute-done.11 = bf16[256,1792]{1,0:T(8,128)(2,1)S(1)} collective-permute-done((bf16[256,1792]{1,0:T(8,128)(2,1)S(1)}, bf16[256,1792]{1,0:T(8,128)(2,1)S(1)}, u32[]{:S(2)}, u32[]{:S(2)}) %collective-permute-start.11) | collective-permute-done | bytes 917536 | tf_op jit(solution)/shard_map/ppermute | solution.py:18
  221.5 1.6 bitcast_add_fusion.1
  223.1 1.6 collective-permute-start.12
  224.7 1.5 convert_add_fusion
  226.2 1.6 collective-permute-start.20
  227.8 13.3 %collective-permute-done.27 = bf16[256,1792]{1,0:T(8,128)(2,1)S(1)} collective-permute-done((bf16[256,1792]{1,0:T(8,128)(2,1)S(1)}, bf16[256,1792]{1,0:T(8,128)(2,1)S(1)}, u32[]{:S(2)}, u32[]{:S(2)}) %collective-permute-start.27) | collective-permute-done | bytes 917536 | tf_op jit(solution)/shard_map/ppermute | solution.py:18
  241.5 1.6 collective-permute-start.28
  243.3 7.1 %collective-permute-done.20 = bf16[128,1792]{1,0:T(8,128)(2,1)S(1)} collective-permute-done((bf16[128,1792]{1,0:T(8,128)(2,1)S(1)}, bf16[128,1792]{1,0:T(8,128)(2,1)S(1)}, u32[]{:S(2)}, u32[]{:S(2)}) %collective-permute-start.20) | collective-permute-done | bytes 458784 | tf_op jit(solution)/shard_map/ppermute | solution.py:18
  250.5 2.3 collective-permute-done.28
  253.0 1.6 collective-permute-start.29
  254.9 26.2 %collective-permute-done.21 = bf16[128,1792]{1,0:T(8,128)(2,1)S(1)} collective-permute-done((bf16[128,1792]{1,0:T(8,128)(2,1)S(1)}, bf16[128,1792]{1,0:T(8,128)(2,1)S(1)}, u32[]{:S(2)}, u32[]{:S(2)}) %collective-permute-start.21) | collective-permute-done | bytes 458784 | tf_op jit(solution)/shard_map/ppermute | solution.py:18
  281.1 10.6 %collective-permute-done.29 = bf16[128,1792]{1,0:T(8,128)(2,1)S(1)} collective-permute-done((bf16[128,1792]{1,0:T(8,128)(2,1)S(1)}, bf16[128,1792]{1,0:T(8,128)(2,1)S(1)}, u32[]{:S(2)}, u32[]{:S(2)}) %collective-permute-start.29) | collective-permute-done | bytes 458784 | tf_op jit(solution)/shard_map/ppermute | solution.py:18
  (92 shorter events, 23.5 us)
Async XLA Ops:
  5.8 25.0 %collective-permute-start.6 = (bf16[80,3712]{1,0:T(8,128)(2,1)S(1)}, bf16[80,3712]{1,0:T(8,128)(2,1)S(1)}, u32[]{:S(2)}, u32[]{:S(2)}) collective-permute-start(bf16[80,3712]{1,0:T(8,128)(2,1)S(1)} %get-tuple-element.18), channel_id=1, source_target_pairs={{0,4},{1,5},{2,6},{3,7},{4,0},{5,1},{6,2},{7,3},{8,12},{9,13},{10,... | collective-permute-start | bytes 1781768 | tf_op jit(solution)/shard_map/ppermute | solution.py:18
  5.9 42.3 %collective-permute-start.14 = (bf16[80,3712]{1,0:T(8,128)(2,1)S(1)}, bf16[80,3712]{1,0:T(8,128)(2,1)S(1)}, u32[]{:S(2)}, u32[]{:S(2)}) collective-permute-start(bf16[80,3712]{1,0:T(8,128)(2,1)S(1)} %get-tuple-element.18), channel_id=1, source_target_pairs={{0,8},{1,9},{2,10},{3,11},{4,12},{5,13},{6,14},{7,15},{8,0},{9,1},... | collective-permute-start | bytes 1781768 | tf_op jit(solution)/shard_map/ppermute | solution.py:18
  8.9 51.5 %collective-permute-start.22 = (bf16[80,3712]{1,0:T(8,128)(2,1)S(1)}, bf16[80,3712]{1,0:T(8,128)(2,1)S(1)}, u32[]{:S(2)}, u32[]{:S(2)}) collective-permute-start(bf16[80,3712]{1,0:T(8,128)(2,1)S(1)} %get-tuple-element.18), channel_id=1, source_target_pairs={{0,12},{1,13},{2,14},{3,15},{4,8},{5,9},{6,10},{7,11},{8,4},{9,5},... | collective-permute-start | bytes 1781768 | tf_op jit(solution)/shard_map/ppermute | solution.py:18
  9.3 53.6 %collective-permute-start = (bf16[128,3712]{1,0:T(8,128)(2,1)S(1)}, bf16[128,3712]{1,0:T(8,128)(2,1)S(1)}, u32[]{:S(2)}, u32[]{:S(2)}) collective-permute-start(bf16[128,3712]{1,0:T(8,128)(2,1)S(1)} %get-tuple-element.15.refs_1_), channel_id=1, source_target_pairs={{0,2},{1,3},{2,0},{3,1},{4,6},{5,7},{6,4},{7,5},{8,10},{9,11},{10,... | collective-permute-start | bytes 2850824 | tf_op jit(solution)/shard_map/ppermute | solution.py:18
  10.8 66.4 %collective-permute-start.1 = (bf16[128,3712]{1,0:T(8,128)(2,1)S(1)}, bf16[128,3712]{1,0:T(8,128)(2,1)S(1)}, u32[]{:S(2)}, u32[]{:S(2)}) collective-permute-start(bf16[128,3712]{1,0:T(8,128)(2,1)S(1)} %get-tuple-element.15.refs_1_), channel_id=1, source_target_pairs={{0,1},{1,0},{2,3},{3,2},{4,5},{5,4},{6,7},{7,6},{8,9},{9,8},{10,11... | collective-permute-start | bytes 2850824 | tf_op jit(solution)/shard_map/ppermute | solution.py:18
  30.8 32.3 %collective-permute-start.7 = (bf16[80,3712]{1,0:T(8,128)(2,1)S(1)}, bf16[80,3712]{1,0:T(8,128)(2,1)S(1)}, u32[]{:S(2)}, u32[]{:S(2)}) collective-permute-start(bf16[80,3712]{1,0:T(8,128)(2,1)S(1)} %collective-permute-done.6), channel_id=1, source_target_pairs={{0,2},{1,3},{2,0},{3,1},{4,6},{5,7},{6,4},{7,5},{8,10},{9,11},{10,... | collective-permute-start | bytes 1781768 | tf_op jit(solution)/shard_map/ppermute | solution.py:18
  48.2 16.5 %collective-permute-start.15 = (bf16[80,3712]{1,0:T(8,128)(2,1)S(1)}, bf16[80,3712]{1,0:T(8,128)(2,1)S(1)}, u32[]{:S(2)}, u32[]{:S(2)}) collective-permute-start(bf16[80,3712]{1,0:T(8,128)(2,1)S(1)} %collective-permute-done.14), channel_id=1, source_target_pairs={{0,2},{1,3},{2,0},{3,1},{4,6},{5,7},{6,4},{7,5},{8,10},{9,11},{10,... | collective-permute-start | bytes 1781768 | tf_op jit(solution)/shard_map/ppermute | solution.py:18
  61.4 14.1 %collective-permute-start.23 = (bf16[80,3712]{1,0:T(8,128)(2,1)S(1)}, bf16[80,3712]{1,0:T(8,128)(2,1)S(1)}, u32[]{:S(2)}, u32[]{:S(2)}) collective-permute-start(bf16[80,3712]{1,0:T(8,128)(2,1)S(1)} %collective-permute-done.22), channel_id=1, source_target_pairs={{0,2},{1,3},{2,0},{3,1},{4,6},{5,7},{6,4},{7,5},{8,10},{9,11},{10,... | collective-permute-start | bytes 1781768 | tf_op jit(solution)/shard_map/ppermute | solution.py:18
  63.0 14.3 %collective-permute-start.2 = (bf16[128,3712]{1,0:T(8,128)(2,1)S(1)}, bf16[128,3712]{1,0:T(8,128)(2,1)S(1)}, u32[]{:S(2)}, u32[]{:S(2)}) collective-permute-start(bf16[128,3712]{1,0:T(8,128)(2,1)S(1)} %collective-permute-done.refs_2_), channel_id=1, source_target_pairs={{0,1},{1,0},{2,3},{3,2},{4,5},{5,4},{6,7},{7,6},{8,9},{9,8},{10,11... | collective-permute-start | bytes 2850824 | tf_op jit(solution)/shard_map/ppermute | solution.py:18
  63.2 40.2 %collective-permute-start.8 = (bf16[96,3712]{1,0:T(8,128)(2,1)S(1)}, bf16[96,3712]{1,0:T(8,128)(2,1)S(1)}, u32[]{:S(2)}, u32[]{:S(2)}) collective-permute-start(bf16[96,3712]{1,0:T(8,128)(2,1)S(1)} %pad_maximum_fusion), channel_id=1, source_target_pairs={{0,16},{16,0},{1,17},{17,1},{2,18},{18,2},{3,19},{19,3},{4,20},{20... | collective-permute-start | bytes 2138120 | tf_op jit(solution)/shard_map/ppermute | solution.py:18
  64.8 40.1 %collective-permute-start.16 = (bf16[96,3712]{1,0:T(8,128)(2,1)S(1)}, bf16[96,3712]{1,0:T(8,128)(2,1)S(1)}, u32[]{:S(2)}, u32[]{:S(2)}) collective-permute-start(bf16[96,3712]{1,0:T(8,128)(2,1)S(1)} %pad_maximum_fusion.1), channel_id=1, source_target_pairs={{0,16},{16,0},{1,17},{17,1},{2,18},{18,2},{3,19},{19,3},{4,20},{20... | collective-permute-start | bytes 2138120 | tf_op jit(solution)/shard_map/ppermute | solution.py:18
  75.5 36.6 %collective-permute-start.24 = (bf16[96,3712]{1,0:T(8,128)(2,1)S(1)}, bf16[96,3712]{1,0:T(8,128)(2,1)S(1)}, u32[]{:S(2)}, u32[]{:S(2)}) collective-permute-start(bf16[96,3712]{1,0:T(8,128)(2,1)S(1)} %pad_maximum_fusion.2), channel_id=1, source_target_pairs={{0,16},{16,0},{1,17},{17,1},{2,18},{18,2},{3,19},{19,3},{4,20},{20... | collective-permute-start | bytes 2138120 | tf_op jit(solution)/shard_map/ppermute | solution.py:18
  103.3 9.7 %collective-permute-start.3 = (bf16[2,256,1792]{2,1,0:T(8,128)(2,1)}, bf16[2,256,1792]{2,1,0:T(8,128)(2,1)S(1)}, u32[]{:S(2)}, u32[]{:S(2)}) collective-permute-start(bf16[2,256,1792]{2,1,0:T(8,128)(2,1)} %get-tuple-element.17), channel_id=1, source_target_pairs={{0,1},{1,0},{2,3},{3,2},{4,5},{5,4},{6,7},{7,6},{8,9},{9,8},{10,11... | collective-permute-start | bytes 5505032 | tf_op jit(solution)/shard_map/ppermute | solution.py:18
  103.5 11.2 %collective-permute-start.9 = (bf16[256,3712]{1,0:T(8,128)(2,1)S(1)}, bf16[256,3712]{1,0:T(8,128)(2,1)}, u32[]{:S(2)}, u32[]{:S(2)}) collective-permute-start(bf16[256,3712]{1,0:T(8,128)(2,1)S(1)} %constant_dynamic-update-slice_fusion.refs_1_), channel_id=1, source_target_pairs={{0,1},{1,0},{2,3},{3,2},{4,5},{5,4},{6,7},{7,6},{8,9},{9,8},{10,11... | collective-permute-start | bytes 5701640 | tf_op jit(solution)/shard_map/ppermute | solution.py:18
  105.8 33.0 %copy-start.7 = (bf16[256,3712]{1,0:T(8,128)(2,1)}, bf16[256,3712]{1,0:T(8,128)(2,1)S(1)}, u32[]{:S(2)}) copy-start(bf16[256,3712]{1,0:T(8,128)(2,1)S(1)} %constant_dynamic-update-slice_fusion.3.refs_1_) | copy-start | bytes 5701636
  105.8 33.3 %collective-permute-start.17 = (bf16[256,3712]{1,0:T(8,128)(2,1)S(1)}, bf16[256,3712]{1,0:T(8,128)(2,1)}, u32[]{:S(2)}, u32[]{:S(2)}) collective-permute-start(bf16[256,3712]{1,0:T(8,128)(2,1)S(1)} %constant_dynamic-update-slice_fusion.3.refs_1_), channel_id=1, source_target_pairs={{0,1},{1,0},{2,3},{3,2},{4,5},{5,4},{6,7},{7,6},{8,9},{9,8},{10,11... | collective-permute-start | bytes 5701640 | tf_op jit(solution)/shard_map/ppermute | solution.py:18
  113.0 50.6 %collective-permute-start.25 = (bf16[256,3712]{1,0:T(8,128)(2,1)}, bf16[256,3712]{1,0:T(8,128)(2,1)}, u32[]{:S(2)}, u32[]{:S(2)}) collective-permute-start(bf16[256,3712]{1,0:T(8,128)(2,1)} %constant_dynamic-update-slice_fusion.6.refs_1_), channel_id=1, source_target_pairs={{0,1},{1,0},{2,3},{3,2},{4,5},{5,4},{6,7},{7,6},{8,9},{9,8},{10,11... | collective-permute-start | bytes 5701640 | tf_op jit(solution)/shard_map/ppermute | solution.py:18
  114.2 73.8 %collective-permute-start.4 = (bf16[2,128,1792]{2,1,0:T(8,128)(2,1)}, bf16[2,128,1792]{2,1,0:T(8,128)(2,1)S(1)}, u32[]{:S(2)}, u32[]{:S(2)}) collective-permute-start(bf16[2,128,1792]{2,1,0:T(8,128)(2,1)} %add_convert_fusion.3), channel_id=1, source_target_pairs={{0,2},{1,3},{2,0},{3,1},{4,6},{5,7},{6,4},{7,5},{8,10},{9,11},{10,... | collective-permute-start | bytes 2752520 | tf_op jit(solution)/shard_map/ppermute | solution.py:18
  138.8 51.1 %collective-permute-start.10 = (bf16[2,256,1792]{2,1,0:T(8,128)(2,1)}, bf16[2,256,1792]{2,1,0:T(8,128)(2,1)}, u32[]{:S(2)}, u32[]{:S(2)}) collective-permute-start(bf16[2,256,1792]{2,1,0:T(8,128)(2,1)} %get-tuple-element.20), channel_id=1, source_target_pairs={{0,1},{1,0},{2,3},{3,2},{4,5},{5,4},{6,7},{7,6},{8,9},{9,8},{10,11... | collective-permute-start | bytes 5505032 | tf_op jit(solution)/shard_map/ppermute | solution.py:18
  163.2 24.8 %copy-start.2 = (f32[2,128,1792]{2,1,0:T(8,128)S(1)}, f32[2,128,1792]{2,1,0:T(8,128)}, u32[]{:S(2)}) copy-start(f32[2,128,1792]{2,1,0:T(8,128)} %shared_expert.1) | copy-start | bytes 5505028
  163.2 28.8 %collective-permute-start.18 = (bf16[2,256,1792]{2,1,0:T(8,128)(2,1)}, bf16[2,256,1792]{2,1,0:T(8,128)(2,1)}, u32[]{:S(2)}, u32[]{:S(2)}) collective-permute-start(bf16[2,256,1792]{2,1,0:T(8,128)(2,1)} %get-tuple-element.22), channel_id=1, source_target_pairs={{0,1},{1,0},{2,3},{3,2},{4,5},{5,4},{6,7},{7,6},{8,9},{9,8},{10,11... | collective-permute-start | bytes 5505032 | tf_op jit(solution)/shard_map/ppermute | solution.py:18
  187.7 7.3 %collective-permute-start.26 = (bf16[2,256,1792]{2,1,0:T(8,128)(2,1)}, bf16[2,256,1792]{2,1,0:T(8,128)(2,1)S(1)}, u32[]{:S(2)}, u32[]{:S(2)}) collective-permute-start(bf16[2,256,1792]{2,1,0:T(8,128)(2,1)} %get-tuple-element.24), channel_id=1, source_target_pairs={{0,1},{1,0},{2,3},{3,2},{4,5},{5,4},{6,7},{7,6},{8,9},{9,8},{10,11... | collective-permute-start | bytes 5505032 | tf_op jit(solution)/shard_map/ppermute | solution.py:18
  188.4 66.1 %collective-permute-start.5 = (bf16[128,1792]{1,0:T(8,128)(2,1)S(1)}, bf16[128,1792]{1,0:T(8,128)(2,1)S(1)}, u32[]{:S(2)}, u32[]{:S(2)}) collective-permute-start(bf16[128,1792]{1,0:T(8,128)(2,1)S(1)} %fusion.11), channel_id=1, source_target_pairs={{0,16},{16,0},{1,17},{17,1},{2,18},{18,2},{3,19},{19,3},{4,20},{20... | collective-permute-start | bytes 1376264 | tf_op jit(solution)/shard_map/ppermute | solution.py:18
  191.4 30.1 %collective-permute-start.11 = (bf16[256,1792]{1,0:T(8,128)(2,1)S(1)}, bf16[256,1792]{1,0:T(8,128)(2,1)S(1)}, u32[]{:S(2)}, u32[]{:S(2)}) collective-permute-start(bf16[256,1792]{1,0:T(8,128)(2,1)S(1)} %fusion), channel_id=1, source_target_pairs={{0,16},{16,0},{1,17},{17,1},{2,18},{18,2},{3,19},{19,3},{4,20},{20... | collective-permute-start | bytes 2752520 | tf_op jit(solution)/shard_map/ppermute | solution.py:18
  193.4 31.3 %collective-permute-start.19 = (bf16[2,128,1792]{2,1,0:T(8,128)(2,1)S(1)}, bf16[2,128,1792]{2,1,0:T(8,128)(2,1)S(1)}, u32[]{:S(2)}, u32[]{:S(2)}) collective-permute-start(bf16[2,128,1792]{2,1,0:T(8,128)(2,1)S(1)} %add_convert_fusion.1), channel_id=1, source_target_pairs={{0,2},{1,3},{2,0},{3,1},{4,6},{5,7},{6,4},{7,5},{8,10},{9,11},{10,... | collective-permute-start | bytes 2752520 | tf_op jit(solution)/shard_map/ppermute | solution.py:18
  195.2 45.9 %collective-permute-start.27 = (bf16[256,1792]{1,0:T(8,128)(2,1)S(1)}, bf16[256,1792]{1,0:T(8,128)(2,1)S(1)}, u32[]{:S(2)}, u32[]{:S(2)}) collective-permute-start(bf16[256,1792]{1,0:T(8,128)(2,1)S(1)} %fusion.1), channel_id=1, source_target_pairs={{0,16},{16,0},{1,17},{17,1},{2,18},{18,2},{3,19},{19,3},{4,20},{20... | collective-permute-start | bytes 2752520 | tf_op jit(solution)/shard_map/ppermute | solution.py:18
  223.1 20.0 %collective-permute-start.12 = (bf16[128,1792]{1,0:T(8,128)(2,1)S(1)}, bf16[128,1792]{1,0:T(8,128)(2,1)S(1)}, u32[]{:S(2)}, u32[]{:S(2)}) collective-permute-start(bf16[128,1792]{1,0:T(8,128)(2,1)S(1)} %slice.193), channel_id=1, source_target_pairs={{0,2},{1,3},{2,0},{3,1},{4,6},{5,7},{6,4},{7,5},{8,10},{9,11},{10,... | collective-permute-start | bytes 1376264 | tf_op jit(solution)/shard_map/ppermute | solution.py:18
  226.2 24.1 %collective-permute-start.20 = (bf16[128,1792]{1,0:T(8,128)(2,1)S(1)}, bf16[128,1792]{1,0:T(8,128)(2,1)S(1)}, u32[]{:S(2)}, u32[]{:S(2)}) collective-permute-start(bf16[128,1792]{1,0:T(8,128)(2,1)S(1)} %fusion.12), channel_id=1, source_target_pairs={{0,16},{16,0},{1,17},{17,1},{2,18},{18,2},{3,19},{19,3},{4,20},{20... | collective-permute-start | bytes 1376264 | tf_op jit(solution)/shard_map/ppermute | solution.py:18
  241.5 11.4 %collective-permute-start.28 = (bf16[128,1792]{1,0:T(8,128)(2,1)S(1)}, bf16[128,1792]{1,0:T(8,128)(2,1)S(1)}, u32[]{:S(2)}, u32[]{:S(2)}) collective-permute-start(bf16[128,1792]{1,0:T(8,128)(2,1)S(1)} %slice.192), channel_id=1, source_target_pairs={{0,2},{1,3},{2,0},{3,1},{4,6},{5,7},{6,4},{7,5},{8,10},{9,11},{10,... | collective-permute-start | bytes 1376264 | tf_op jit(solution)/shard_map/ppermute | solution.py:18
  243.2 11.7 %collective-permute-start.13 = (bf16[128,1792]{1,0:T(8,128)(2,1)S(1)}, bf16[128,1792]{1,0:T(8,128)(2,1)S(1)}, u32[]{:S(2)}, u32[]{:S(2)}) collective-permute-start(bf16[128,1792]{1,0:T(8,128)(2,1)S(1)} %fusion.5), channel_id=1, source_target_pairs={{0,4},{1,5},{2,6},{3,7},{4,0},{5,1},{6,2},{7,3},{8,12},{9,13},{10,... | collective-permute-start | bytes 1376264 | tf_op jit(solution)/shard_map/ppermute | solution.py:18
  250.5 30.7 %collective-permute-start.21 = (bf16[128,1792]{1,0:T(8,128)(2,1)S(1)}, bf16[128,1792]{1,0:T(8,128)(2,1)S(1)}, u32[]{:S(2)}, u32[]{:S(2)}) collective-permute-start(bf16[128,1792]{1,0:T(8,128)(2,1)S(1)} %fusion.4), channel_id=1, source_target_pairs={{0,8},{1,9},{2,10},{3,11},{4,12},{5,13},{6,14},{7,15},{8,0},{9,1},... | collective-permute-start | bytes 1376264 | tf_op jit(solution)/shard_map/ppermute | solution.py:18
  253.0 38.8 %collective-permute-start.29 = (bf16[128,1792]{1,0:T(8,128)(2,1)S(1)}, bf16[128,1792]{1,0:T(8,128)(2,1)S(1)}, u32[]{:S(2)}, u32[]{:S(2)}) collective-permute-start(bf16[128,1792]{1,0:T(8,128)(2,1)S(1)} %fusion.2), channel_id=1, source_target_pairs={{0,12},{1,13},{2,14},{3,15},{4,8},{5,9},{6,10},{7,11},{8,4},{9,5},... | collective-permute-start | bytes 1376264 | tf_op jit(solution)/shard_map/ppermute | solution.py:18
  (8 other events, 28.3 us)

commit v2 on v1

v2 whole, which is shorter than its diff:
```python
import functools

import jax
import jax.numpy as jnp
from jax import lax
from jax.experimental import pallas as pl
from jax.experimental.pallas import tpu as pltpu
from jax.sharding import PartitionSpec as P

routed_scale = 2.5
LANES = 128
SIDE = 256
AHEAD = 2
VMEM = 52 * 1024 * 1024


def exchange(value, axis, mask):
    pairs = [(source, source ^ mask) for source in range(lax.axis_size(axis))]
    return lax.ppermute(value, axis, pairs)


def widen_body(experts, tokens, ids, weight, rows):
    count, width = tokens.shape
    rates = weight[...]
    rates = routed_scale * rates / jnp.sum(rates, axis=1, keepdims=True)
    lane = lax.broadcasted_iota(jnp.int32, (count, LANES), 1)
    total = jnp.zeros((count, LANES), jnp.float32)
    for choice in range(ids.shape[1]):
        total += jnp.where(ids[:, choice : choice + 1] == lane % experts, rates[:, choice : choice + 1], 0.0)
    high = total.astype(jnp.bfloat16).astype(jnp.float32)
    middle = (total - high).astype(jnp.bfloat16).astype(jnp.float32)
    low = total - high - middle
    term = lane // experts
    held = jnp.where(term == 0, high, jnp.where(term == 1, middle, jnp.where(term == 2, low, 0.0)))
    rows[:, :width] = tokens[...]
    rows[:, width:] = held.astype(jnp.bfloat16)


def widen(tokens, ids, weight, experts):
    count, width = tokens.shape
    return pl.pallas_call(
        functools.partial(widen_body, experts),
        out_shape=jax.ShapeDtypeStruct((count, width + LANES), tokens.dtype),
        in_specs=[pl.BlockSpec(memory_space=pltpu.VMEM)] * 3,
        out_specs=pl.BlockSpec(memory_space=pltpu.VMEM),
        compiler_params=pltpu.CompilerParams(vmem_limit_bytes=16 * 1024 * 1024),
        name="widen",
    )(tokens, ids, weight)


def ffn_body(experts, blocks, out_rows, scaled, added, n_in, n_out, *refs):
    info = refs[0]
    inputs = refs[1 : 1 + n_in]
    gate, up, down = refs[1 + n_in : 4 + n_in]
    extra = refs[4 + n_in] if added else None
    refs = refs[4 + n_in + added :]
    outs = refs[:n_out]
    x, gate_v, up_v, down_v, act, factor, result, x_sem, gate_sem, up_sem, down_sem, out_sem = refs[n_out : n_out + 12]
    width, hidden = gate.shape
    steps = hidden // SIDE
    tile = result.shape[2]
    per_block = width // blocks // tile
    dp = info[0]

    copies = []
    for number, source in enumerate(inputs):
        size = source.shape[0]
        copies.append(pltpu.make_async_copy(source, x.at[pl.ds(number * size, size), :], x_sem.at[number]))
    if added:
        extra_v, extra_sem = refs[n_out + 12 :]
        count = extra.shape[1]
        more = pltpu.make_async_copy(extra, extra_v, extra_sem.at[0])

    def side(weights, held, sems, j):
        return pltpu.make_async_copy(
            weights.at[:, pl.ds(pl.multiple_of(j * SIDE, SIDE), SIDE)], held.at[j], sems.at[j]
        )

    def lower(i):
        column = ((i // per_block) ^ dp if blocks > 1 else 0) * (width // blocks) + (i % per_block) * tile
        return pltpu.make_async_copy(
            down.at[:, pl.ds(pl.multiple_of(column, LANES), tile)], down_v.at[i], down_sem.at[i]
        )

    def leave(i):
        given = []
        for number, (first, count) in enumerate(out_rows):
            given.append(
                pltpu.make_async_copy(
                    result.at[i, pl.ds(first, count), :],
                    outs[number].at[i // per_block, :, pl.ds(pl.multiple_of((i % per_block) * tile, LANES), tile)],
                    out_sem.at[i, number],
                )
            )
        return given

    for copy in copies:
        copy.start()
    for j in range(min(AHEAD, steps)):
        side(gate, gate_v, gate_sem, j).start()
        side(up, up_v, up_sem, j).start()
    for copy in copies:
        copy.wait()

    if scaled:
        held = x[:, width:].astype(jnp.float32)
        lane = lax.broadcasted_iota(jnp.int32, held.shape, 1)
        chosen = jnp.sum(jnp.where(lane % experts == info[1], held, 0.0), axis=1, keepdims=True)
        factor[...] = jnp.broadcast_to(chosen, factor.shape)

    def lowers():
        for i in range(blocks * per_block):
            lower(i).start()

    if steps <= AHEAD:
        lowers()
    if added:
        more.start()

    def first(j, carry):
        side(gate, gate_v, gate_sem, j).wait()
        side(up, up_v, up_sem, j).wait()

        @pl.when(j + AHEAD < steps)
        def _():
            side(gate, gate_v, gate_sem, j + AHEAD).start()
            side(up, up_v, up_sem, j + AHEAD).start()

        @pl.when(j + AHEAD == steps - 1)
        def _():
            lowers()

        rows = x[:, :width]
        gate_val = jnp.dot(rows, gate_v[j], preferred_element_type=jnp.float32)
        up_val = jnp.dot(rows, up_v[j], preferred_element_type=jnp.float32)
        value = gate_val / (1.0 + jnp.exp(-gate_val)) * up_val
        if scaled:
            value = value * factor[...]
        act[:, pl.ds(pl.multiple_of(j * SIDE, SIDE), SIDE)] = value.astype(act.dtype)
        return carry

    lax.fori_loop(0, steps, first, 0)

    if added:
        more.wait()

    def second(i, carry):
        lower(i).wait()
        value = jnp.dot(act[...], down_v[i], preferred_element_type=jnp.float32)
        if added:
            result[i, :count, :] = (value[:count] + extra_v[i]).astype(result.dtype)
            result[i, count:, :] = value[count:].astype(result.dtype)
        else:
            result[i] = value.astype(result.dtype)
        for copy in leave(i):
            copy.start()
        return carry

    lax.fori_loop(0, blocks * per_block, second, 0)

    def finish(i, carry):
        for copy in leave(i):
            copy.wait()
        return carry

    lax.fori_loop(0, blocks * per_block, finish, 0)


def ffn(info, inputs, gate, up, down, extra, experts, blocks, out_rows, scaled, dtype, name):
    width, hidden = gate.shape
    row_width = inputs[0].shape[1]
    rows = sum(count for _, count in out_rows)
    tiles = max(blocks, 2)
    tile = width // tiles
    steps = hidden // SIDE
    flops = 6 * rows * width * hidden
    added = 0 if extra is None else 1
    body = functools.partial(ffn_body, experts, blocks, out_rows, scaled, added, len(inputs), len(out_rows))
    scratch = [
        pltpu.VMEM((rows, row_width), jnp.bfloat16),
        pltpu.VMEM((steps, width, SIDE), jnp.bfloat16),
        pltpu.VMEM((steps, width, SIDE), jnp.bfloat16),
        pltpu.VMEM((tiles, hidden, tile), jnp.bfloat16),
        pltpu.VMEM((rows, hidden), jnp.bfloat16),
        pltpu.VMEM((rows, SIDE), jnp.float32),
        pltpu.VMEM((tiles, rows, tile), dtype),
        pltpu.SemaphoreType.DMA((len(inputs),)),
        pltpu.SemaphoreType.DMA((steps,)),
        pltpu.SemaphoreType.DMA((steps,)),
        pltpu.SemaphoreType.DMA((tiles,)),
        pltpu.SemaphoreType.DMA((tiles, len(out_rows))),
    ]
    if added:
        scratch += [pltpu.VMEM((tiles, extra.shape[1], tile), jnp.float32), pltpu.SemaphoreType.DMA((1,))]
    return pl.pallas_call(
        body,
        out_shape=[jax.ShapeDtypeStruct((blocks, count, width // blocks), dtype) for _, count in out_rows],
        in_specs=[pl.BlockSpec(memory_space=pltpu.SMEM)]
        + [pl.BlockSpec(memory_space=pltpu.HBM)] * (len(inputs) + 3 + added),
        out_specs=[pl.BlockSpec(memory_space=pltpu.HBM)] * len(out_rows),
        scratch_shapes=scratch,
        compiler_params=pltpu.CompilerParams(vmem_limit_bytes=VMEM),
        cost_estimate=pl.CostEstimate(
            flops=flops, bytes_accessed=6 * width * hidden + 4 * rows * width, transcendentals=rows * hidden
        ),
        name=name,
    )(info, *inputs, gate, up, down, *([extra] if added else []))


def local(
    tokens,
    expert_ids,
    route_weight,
    pair_swap,
    expert_gate,
    expert_up,
    expert_down,
    shared_gate,
    shared_up,
    shared_down,
):
    count, width = tokens.shape
    experts = lax.axis_size("expert")
    n_dp = lax.axis_size("dp")
    half_axis = experts // 2
    column = lax.axis_index("expert")
    dp = lax.axis_index("dp")
    mine = jnp.where(pair_swap[column % half_axis] == 1, (column + half_axis) % experts, column)
    info = jnp.stack([dp, mine]).astype(jnp.int32)
    blocks = n_dp if (width // n_dp) % LANES == 0 else 1
    planes = experts // 4
    plane = column // 4
    f32, bf16 = jnp.float32, jnp.bfloat16
    weights = (expert_gate[0], expert_up[0], expert_down[0])
    def over_core(value):
        return exchange(value, "expert", 1)

    def over_row(value):
        return exchange(value, "expert", 2)

    def over_dp(sends):
        return [exchange(send, "dp", k + 1) for k, send in enumerate(sends)]

    def over_planes(value, pairs):
        return lax.ppermute(value, "expert", [(4 * s + k, 4 * t + k) for s, t in pairs for k in range(4)])

    def by_dp(value):
        if blocks == n_dp:
            return value
        rows = value.shape[1]
        parts = value.transpose(1, 0, 2).reshape(rows, n_dp, width // n_dp)
        return jnp.take(parts, dp ^ jnp.arange(n_dp), axis=1).transpose(1, 0, 2)

    def routed(inputs, extra=None):
        half = len(inputs) // 2 * count
        halves = ((0, half), (half, half))
        kept, sent = ffn(info, inputs, *weights, extra, experts, blocks, halves, True, bf16, "routed_expert")
        return by_dp(kept), by_dp(sent)

    def to_dp(kept, met):
        return [(kept[k].astype(f32) + met[k].astype(f32)).astype(bf16) for k in range(1, n_dp)]

    def owned(kept, met, came):
        whole = kept[0].astype(f32) + met[0].astype(f32)
        for value in came:
            whole = whole + value.astype(f32)
        return whole

    def together(*values):
        return lax.optimization_barrier(values)

    wide = widen(tokens, expert_ids, route_weight, experts)
    shared_part = ffn(
        info,
        [tokens],
        shared_gate,
        shared_up,
        shared_down,
        None,
        experts,
        blocks,
        ((0, count),),
        False,
        f32,
        "shared_expert",
    )[0]
    if blocks == 1:
        shared_part = shared_part.reshape(count, 2, width // 2).transpose(1, 0, 2)

    if planes == 4:
        inner = (plane == 1) | (plane == 2)
        middle, outward = ((1, 2), (2, 1)), ((1, 0), (2, 3))
        row_own = over_row(wide)
        near = over_planes(wide, ((0, 1), (1, 0), (2, 3), (3, 2)))
        opposite = over_planes(wide, middle)
        kept_0, sent_0 = routed([wide, over_core(wide)], shared_part)
        kept_0, sent_0, row_own, near, opposite = together(kept_0, sent_0, row_own, near, opposite)

        inputs = [row_own, near, over_core(row_own), over_core(near)]
        row_near = over_row(near)
        from_outer, from_inner = over_planes(opposite, outward), over_planes(near, middle)
        met_0 = over_core(sent_0)
        came_0 = over_dp(to_dp(kept_0, met_0))
        kept_1, sent_1 = routed(inputs)
        kept_1, sent_1, row_near, from_outer, from_inner, *came_0 = together(
            kept_1, sent_1, row_near, from_outer, from_inner, *came_0
        )

        next_ = jnp.where(inner, from_inner, from_outer)
        inputs = [row_near, next_, over_core(row_near), over_core(next_)]
        row_next = over_row(next_)
        last = over_planes(from_inner, outward)
        met_1 = over_core(sent_1)
        came_1 = over_dp(to_dp(kept_1, met_1))
        kept_2, sent_2 = routed(inputs)
        kept_2, sent_2, row_next, last, *came_1 = together(kept_2, sent_2, row_next, last, *came_1)

        far = jnp.where(inner, opposite, last)
        inputs = [row_next, far, over_core(row_next), over_core(far)]
        row_far = over_row(far)
        met_2 = over_core(sent_2)
        whole_1 = owned(kept_1, met_1, came_1)
        back_0 = over_row(whole_1[:count].astype(bf16))
        came_2 = over_dp(to_dp(kept_2, met_2))
        kept_3, sent_3 = routed(inputs)
        kept_3, sent_3, row_far, back_0, *came_2 = together(kept_3, sent_3, row_far, back_0, *came_2)

        inputs = [row_far, over_core(row_far)]
        met_3 = over_core(sent_3)
        whole_2 = owned(kept_2, met_2, came_2)
        back_1 = over_row(whole_2[:count].astype(bf16))
        came_3 = over_dp(to_dp(kept_3, met_3))
        kept_4, sent_4 = routed(inputs)
        kept_4, sent_4, back_1, *came_3 = together(kept_4, sent_4, back_1, *came_3)

        met_4 = over_core(sent_4)
        whole_3 = owned(kept_3, met_3, came_3)
        back_2 = over_row(whole_3[:count].astype(bf16))
        came_4 = over_dp(to_dp(kept_4, met_4))
        back_3 = over_row(owned(kept_4, met_4, came_4).astype(bf16))
        totals = [
            owned(kept_0, met_0, came_0) + back_0.astype(f32),
            whole_1[count:] + back_1.astype(f32),
            whole_2[count:] + back_2.astype(f32),
            whole_3[count:] + back_3.astype(f32),
        ]
    else:
        totals = []
        for s in range(planes):
            here = exchange(wide, "expert", 4 * s) if s else wide
            across = over_row(here)
            kept, sent = routed([here, across, over_core(here), over_core(across)], None if s else shared_part)
            met = over_core(sent)
            whole = owned(kept, met, over_dp(to_dp(kept, met)))
            totals.append(whole[:count] + over_row(whole[count:].astype(bf16)).astype(f32))
    answer = totals[0]
    for s in range(1, planes):
        answer = answer + exchange(totals[s].astype(bf16), "expert", 4 * s).astype(f32)
    return answer.astype(bf16)


def solution(mesh):
    in_specs = (
        P("expert", None),
        P("expert", None),
        P("expert", None),
        P(),
        P("expert", None, "dp"),
        P("expert", None, "dp"),
        P("expert", "dp", None),
        P(None, "dp"),
        P(None, "dp"),
        P("dp", None),
    )
    out_specs = P("expert", "dp")
    return jax.shard_map(local, mesh=mesh, in_specs=in_specs, out_specs=out_specs, check_vma=False)
```

time: 293 us -> 219 us (0.75)
  waiting for transfers between devices: 133 us -> 74.5 us
  Pallas kernels: 110 us -> 86.8 us
  starting transfers between devices: 27.6 us -> 32.8 us
  other arithmetic: 9.54 us -> 13.4 us
    ppermute x30 -> x29, waiting for transfers between devices: 133 us -> 73.5 us  [exchange(): return lax.ppermute(value, axis, pairs)]
    pallas_call x5 -> x6, Pallas kernels: 109 us -> 86.4 us  [ffn(): pl.pallas_call(body, out_shape=[jax.ShapeDtypeStruct((blocks, count, widt...]
    ppermute x0 -> x5, starting transfers between devices: none -> 12.5 us  [over_planes(): lax.ppermute(value, 'expert', [(4 * s + k, 4 * t + k) for s, t in pairs f...]
    ppermute x30 -> x29, starting transfers between devices: 27.6 us -> 20.2 us  [exchange(): return lax.ppermute(value, axis, pairs)]
    unnamed x28 -> x50, local copies, waits for them, and re-layouts: 8.91 us -> 8.7 us
  transfers between devices with their start and end apart: 30 -> 34, of which waited for: 12 -> 13; matrix products, arithmetic and copies ran while one was open for 4% -> 6% of each run, Pallas kernels for 37% -> 39%
where the time goes in v2:
time: 219 us
  Pallas kernels  86.8 us (40%)
  waiting for transfers between devices  74.5 us (34%)
  starting transfers between devices  32.8 us (15%)
  other arithmetic  13.4 us (6%)
  local copies, waits for them, and re-layouts  10.2 us (5%)
    pallas_call x6, Pallas kernels, ffn(): pl.pallas_call(body, out_shape=[jax.ShapeDtypeStruct((blocks, count, widt...  86.4 us
    ppermute x29, waiting for transfers between devices, exchange(): return lax.ppermute(value, axis, pairs)  73.5 us
    ppermute x29, starting transfers between devices, exchange(): return lax.ppermute(value, axis, pairs)  20.2 us
    ppermute x5, starting transfers between devices, over_planes(): lax.ppermute(value, 'expert', [(4 * s + k, 4 * t + k) for s, t in pairs f...  12.5 us
    unnamed x50, local copies, waits for them, and re-layouts  8.7 us
    add x3, other arithmetic, owned(): whole = whole + value.astype(f32)  4.64 us
  transfers between devices with their start and end apart: 34, of which 13 were waited for; matrix products, arithmetic and copies ran while one was open for 6% of the time, Pallas kernels for 39%

profile of v2, /device:TPU:8, one launch (start us, length us, event | category | flops | bytes accessed | tf_op | source)
XLA Modules:
  0.0 218.8 jit_solution(10026121070601113209)
XLA Ops:
  3.3 1.6 collective-permute-start.1
  5.3 4.6 %collective-permute-start.3 = (bf16[128,3712]{1,0:T(8,128)(2,1)S(1)}, bf16[128,3712]{1,0:T(8,128)(2,1)}, u32[]{:S(2)}, u32[]{:S(2)}) collective-permute-start(bf16[128,3712]{1,0:T(8,128)(2,1)S(1)} %widen.1.refs_1_), channel_id=1, source_target_pairs={{4,8},{5,9},{6,10},{7,11},{8,4},{9,5},{10,6},{11,7},{20,24},{21,25... | collective-permute-start | bytes 2850824 | tf_op jit(solution)/shard_map/ppermute | solution.py:245
  11.3 10.2 %shared_expert.1.refs_6_ = f32[2,128,1792]{2,1,0:T(8,128)} custom-call(s32[2]{0:T(128)S(1)} %pad_add_fusion.refs_0_, bf16[128,3584]{1,0:T(8,128)(2,1)S(1)} %copy-done.2, bf16[3584,1024]{1,0:T(8,128)(2,1)} %refs_2_.1, bf16[3584,1024]{1,0:T(8,128)(2,1)} %refs_3_.1, bf16[1024,3584]{1,0:T(8,128)(2,1)} %refs_4_.1), custom_call_target="tpu_custom_call" | custom-call | flops 2818572288 | bytes 23855104 | tf_op jit(solution)/shard_map/shared_expert/pallas_call | solution.py:195
  21.6 11.9 %routed_expert.5 = (bf16[2,128,1792]{2,1,0:T(8,128)(2,1)S(1)}, bf16[2,128,1792]{2,1,0:T(8,128)(2,1)S(1)}) custom-call(s32[2]{0:T(128)S(1)} %pad_add_fusion.refs_0_, bf16[128,3712]{1,0:T(8,128)(2,1)} %copy-done, bf16[128,3712]{1,0:T(8,128)(2,1)} %collective-permute-done.refs_2_, bf16[3584,1024]{1,0:T(8,128)(2,1)} %bitcast.38, bf16[3584,1024]{1,0:T(8,128)(2,1)} %bitcast.43, ...), custom_call_target="tpu_custom_call" | custom-call | flops 5637144576 | bytes 25690112 | tf_op jit(solution)/shard_map/routed_expert/pallas_call | solution.py:195
  34.7 1.9 collective-permute-start.9
  38.6 1.5 collective-permute-start.10
  41.1 17.5 %routed_expert.6 = (bf16[2,256,1792]{2,1,0:T(8,128)(2,1)}, bf16[2,256,1792]{2,1,0:T(8,128)(2,1)}) custom-call(s32[2]{0:T(128)S(1)} %pad_add_fusion.refs_0_, bf16[128,3712]{1,0:T(8,128)(2,1)} %collective-permute-done.1.refs_1_, bf16[128,3712]{1,0:T(8,128)(2,1)S(1)} %collective-permute-done.2.refs_2_, bf16[128,3712]{1,0:T(8,128)(2,1)} %copy-done.20, ...), custom_call_target="tpu_custom_call" | custom-call | flops 11274289152 | bytes 29360128 | tf_op jit(solution)/shard_map/routed_expert/pallas_call | solution.py:195
  62.8 1.5 collective-permute-start.13
  64.3 4.2 %collective-permute-start.14 = (bf16[128,3712]{1,0:T(8,128)(2,1)S(1)}, bf16[128,3712]{1,0:T(8,128)(2,1)S(1)}, u32[]{:S(2)}, u32[]{:S(2)}) collective-permute-start(bf16[128,3712]{1,0:T(8,128)(2,1)S(1)} %copy-done.9), channel_id=1, source_target_pairs={{4,0},{5,1},{6,2},{7,3},{8,12},{9,13},{10,14},{11,15},{20,16},{21,... | collective-permute-start | bytes 2850824 | tf_op jit(solution)/shard_map/ppermute | solution.py:245
  69.9 1.6 collective-permute-start.16
  72.5 17.7 %routed_expert.7 = (bf16[2,256,1792]{2,1,0:T(8,128)(2,1)}, bf16[2,256,1792]{2,1,0:T(8,128)(2,1)}) custom-call(s32[2]{0:T(128)S(1)} %pad_add_fusion.refs_0_, bf16[128,3712]{1,0:T(8,128)(2,1)S(1)} %collective-permute-done.7.refs_1_, bf16[128,3712]{1,0:T(8,128)(2,1)S(1)} %broadcast_select_fusion.1.refs_2_, bf16[128,3712]{1,0:T(8,128)(2,1)} %collective-permute-done.11.refs_3_, ...), custom_call_target="tpu_custom_call" | custom-call | flops 11274289152 | bytes 29360128 | tf_op jit(solution)/shard_map/routed_expert/pallas_call | solution.py:195
  90.2 1.9 collective-permute-done.16
  95.5 1.6 bitcast_add_fusion.2
  97.9 1.5 collective-permute-start.20
  99.7 1.6 collective-permute-start.22
  102.2 17.7 %routed_expert.8 = (bf16[2,256,1792]{2,1,0:T(8,128)(2,1)}, bf16[2,256,1792]{2,1,0:T(8,128)(2,1)}) custom-call(s32[2]{0:T(128)S(1)} %pad_add_fusion.refs_0_, bf16[128,3712]{1,0:T(8,128)(2,1)S(1)} %collective-permute-done.13.refs_1_, bf16[128,3712]{1,0:T(8,128)(2,1)S(1)} %broadcast_select_fusion.refs_2_, bf16[128,3712]{1,0:T(8,128)(2,1)} %collective-permute-done.17.refs_3_, ...), custom_call_target="tpu_custom_call" | custom-call | flops 11274289152 | bytes 29360128 | tf_op jit(solution)/shard_map/routed_expert/pallas_call | solution.py:195
  119.9 8.0 %collective-permute-done.20 = bf16[128,1792]{1,0:T(8,128)(2,1)S(1)} collective-permute-done((bf16[128,1792]{1,0:T(8,128)(2,1)}, bf16[128,1792]{1,0:T(8,128)(2,1)S(1)}, u32[]{:S(2)}, u32[]{:S(2)}) %collective-permute-start.20) | collective-permute-done | bytes 458784 | tf_op jit(solution)/shard_map/ppermute | solution.py:19
  128.5 4.8 %collective-permute-done.25 = bf16[2,256,1792]{2,1,0:T(8,128)(2,1)S(1)} collective-permute-done((bf16[2,256,1792]{2,1,0:T(8,128)(2,1)}, bf16[2,256,1792]{2,1,0:T(8,128)(2,1)S(1)}, u32[]{:S(2)}, u32[]{:S(2)}) %collective-permute-start.25) | collective-permute-done | bytes 1835040 | tf_op jit(solution)/shard_map/ppermute | solution.py:19
  133.3 2.3 %fusion.2 = bf16[256,1792]{1,0:T(8,128)(2,1)} fusion(bf16[2,256,1792]{2,1,0:T(8,128)(2,1)S(1)} %collective-permute-done.25, bf16[2,256,1792]{2,1,0:T(8,128)(2,1)} %get-tuple-element.69), kind=kLoop, calls=%fused_computation.10 | loop fusion | flops 1835008 | bytes 2752512 | tf_op jit(solution)/shard_map/convert_element_type | solution.py:261
  135.7 1.5 collective-permute-start.26
  137.2 1.5 bitcast_add_fusion.1
  140.2 11.4 %routed_expert.9 = (bf16[2,128,1792]{2,1,0:T(8,128)(2,1)S(1)}, bf16[2,128,1792]{2,1,0:T(8,128)(2,1)S(1)}) custom-call(s32[2]{0:T(128)S(1)} %pad_add_fusion.refs_0_, bf16[128,3712]{1,0:T(8,128)(2,1)} %copy-done.12, bf16[128,3712]{1,0:T(8,128)(2,1)} %copy-done.13, bf16[3584,1024]{1,0:T(8,128)(2,1)} %bitcast.42, bf16[3584,1024]{1,0:T(8,128)(2,1)} %bitcast.47, ...), custom_call_target="tpu_custom_call" | custom-call | flops 5637144576 | bytes 25690112 | tf_op jit(solution)/shard_map/routed_expert/pallas_call | solution.py:195
  151.6 6.7 %collective-permute-done.26 = bf16[256,1792]{1,0:T(8,128)(2,1)} collective-permute-done((bf16[256,1792]{1,0:T(8,128)(2,1)}, bf16[256,1792]{1,0:T(8,128)(2,1)}, u32[]{:S(2)}, u32[]{:S(2)}) %collective-permute-start.26) | collective-permute-done | bytes 917536 | tf_op jit(solution)/shard_map/ppermute | solution.py:19
  158.5 2.3 %collective-permute-done.30 = bf16[2,128,1792]{2,1,0:T(8,128)(2,1)S(1)} collective-permute-done((bf16[2,128,1792]{2,1,0:T(8,128)(2,1)S(1)}, bf16[2,128,1792]{2,1,0:T(8,128)(2,1)S(1)}, u32[]{:S(2)}, u32[]{:S(2)}) %collective-permute-start.30) | collective-permute-done | bytes 917536 | tf_op jit(solution)/shard_map/ppermute | solution.py:19
  161.0 1.6 collective-permute-start.31
  162.6 1.6 bitcast_add_fusion
  164.8 8.8 %collective-permute-done.31 = bf16[128,1792]{1,0:T(8,128)(2,1)S(1)} collective-permute-done((bf16[128,1792]{1,0:T(8,128)(2,1)S(1)}, bf16[128,1792]{1,0:T(8,128)(2,1)S(1)}, u32[]{:S(2)}, u32[]{:S(2)}) %collective-permute-start.31) | collective-permute-done | bytes 458784 | tf_op jit(solution)/shard_map/ppermute | solution.py:19
  174.4 2.8 %collective-permute-done.28 = bf16[128,1792]{1,0:T(8,128)(2,1)S(1)} collective-permute-done((bf16[128,1792]{1,0:T(8,128)(2,1)S(1)}, bf16[128,1792]{1,0:T(8,128)(2,1)S(1)}, u32[]{:S(2)}, u32[]{:S(2)}) %collective-permute-start.28) | collective-permute-done | bytes 458784 | tf_op jit(solution)/shard_map/ppermute | solution.py:19
  178.3 8.1 %collective-permute-done.32 = bf16[128,1792]{1,0:T(8,128)(2,1)S(1)} collective-permute-done((bf16[128,1792]{1,0:T(8,128)(2,1)S(1)}, bf16[128,1792]{1,0:T(8,128)(2,1)S(1)}, u32[]{:S(2)}, u32[]{:S(2)}) %collective-permute-start.32) | collective-permute-done | bytes 458784 | tf_op jit(solution)/shard_map/ppermute | solution.py:19
  186.5 1.8 collective-permute-start.33
  188.3 19.8 %collective-permute-done.29 = bf16[128,1792]{1,0:T(8,128)(2,1)S(1)} collective-permute-done((bf16[128,1792]{1,0:T(8,128)(2,1)S(1)}, bf16[128,1792]{1,0:T(8,128)(2,1)S(1)}, u32[]{:S(2)}, u32[]{:S(2)}) %collective-permute-start.29) | collective-permute-done | bytes 458784 | tf_op jit(solution)/shard_map/ppermute | solution.py:19
  208.1 9.5 %collective-permute-done.33 = bf16[128,1792]{1,0:T(8,128)(2,1)S(1)} collective-permute-done((bf16[128,1792]{1,0:T(8,128)(2,1)S(1)}, bf16[128,1792]{1,0:T(8,128)(2,1)S(1)}, u32[]{:S(2)}, u32[]{:S(2)}) %collective-permute-start.33) | collective-permute-done | bytes 458784 | tf_op jit(solution)/shard_map/ppermute | solution.py:19
  (113 shorter events, 26.6 us)
Async XLA Ops:
  3.2 18.3 %collective-permute-start = (bf16[128,3712]{1,0:T(8,128)(2,1)S(1)}, bf16[128,3712]{1,0:T(8,128)(2,1)}, u32[]{:S(2)}, u32[]{:S(2)}) collective-permute-start(bf16[128,3712]{1,0:T(8,128)(2,1)S(1)} %widen.1.refs_1_), channel_id=1, source_target_pairs={{0,1},{1,0},{2,3},{3,2},{4,5},{5,4},{6,7},{7,6},{8,9},{9,8},{10,11... | collective-permute-start | bytes 2850824 | tf_op jit(solution)/shard_map/ppermute | solution.py:19
  3.3 30.2 %collective-permute-start.1 = (bf16[128,3712]{1,0:T(8,128)(2,1)S(1)}, bf16[128,3712]{1,0:T(8,128)(2,1)}, u32[]{:S(2)}, u32[]{:S(2)}) collective-permute-start(bf16[128,3712]{1,0:T(8,128)(2,1)S(1)} %widen.1.refs_1_), channel_id=1, source_target_pairs={{0,2},{1,3},{2,0},{3,1},{4,6},{5,7},{6,4},{7,5},{8,10},{9,11},{10,... | collective-permute-start | bytes 2850824 | tf_op jit(solution)/shard_map/ppermute | solution.py:19
  4.9 28.6 %collective-permute-start.2 = (bf16[128,3712]{1,0:T(8,128)(2,1)S(1)}, bf16[128,3712]{1,0:T(8,128)(2,1)S(1)}, u32[]{:S(2)}, u32[]{:S(2)}) collective-permute-start(bf16[128,3712]{1,0:T(8,128)(2,1)S(1)} %widen.1.refs_1_), channel_id=1, source_target_pairs={{0,4},{1,5},{2,6},{3,7},{4,0},{5,1},{6,2},{7,3},{8,12},{9,13},{10,... | collective-permute-start | bytes 2850824 | tf_op jit(solution)/shard_map/ppermute | solution.py:245
  5.3 28.1 %collective-permute-start.3 = (bf16[128,3712]{1,0:T(8,128)(2,1)S(1)}, bf16[128,3712]{1,0:T(8,128)(2,1)}, u32[]{:S(2)}, u32[]{:S(2)}) collective-permute-start(bf16[128,3712]{1,0:T(8,128)(2,1)S(1)} %widen.1.refs_1_), channel_id=1, source_target_pairs={{4,8},{5,9},{6,10},{7,11},{8,4},{9,5},{10,6},{11,7},{20,24},{21,25... | collective-permute-start | bytes 2850824 | tf_op jit(solution)/shard_map/ppermute | solution.py:245
  33.6 5.0 %collective-permute-start.5 = (bf16[128,3712]{1,0:T(8,128)(2,1)}, bf16[128,3712]{1,0:T(8,128)(2,1)S(1)}, u32[]{:S(2)}, u32[]{:S(2)}) collective-permute-start(bf16[128,3712]{1,0:T(8,128)(2,1)} %collective-permute-done.1.refs_1_), channel_id=1, source_target_pairs={{0,1},{1,0},{2,3},{3,2},{4,5},{5,4},{6,7},{7,6},{8,9},{9,8},{10,11... | collective-permute-start | bytes 2850824 | tf_op jit(solution)/shard_map/ppermute | solution.py:19
  34.1 6.0 %collective-permute-start.6 = (bf16[128,3712]{1,0:T(8,128)(2,1)S(1)}, bf16[128,3712]{1,0:T(8,128)(2,1)S(1)}, u32[]{:S(2)}, u32[]{:S(2)}) collective-permute-start(bf16[128,3712]{1,0:T(8,128)(2,1)S(1)} %collective-permute-done.2.refs_2_), channel_id=1, source_target_pairs={{0,1},{1,0},{2,3},{3,2},{4,5},{5,4},{6,7},{7,6},{8,9},{9,8},{10,11... | collective-permute-start | bytes 2850824 | tf_op jit(solution)/shard_map/ppermute | solution.py:19
  34.2 24.5 %collective-permute-start.7 = (bf16[128,3712]{1,0:T(8,128)(2,1)S(1)}, bf16[128,3712]{1,0:T(8,128)(2,1)S(1)}, u32[]{:S(2)}, u32[]{:S(2)}) collective-permute-start(bf16[128,3712]{1,0:T(8,128)(2,1)S(1)} %collective-permute-done.2.refs_2_), channel_id=1, source_target_pairs={{0,2},{1,3},{2,0},{3,1},{4,6},{5,7},{6,4},{7,5},{8,10},{9,11},{10,... | collective-permute-start | bytes 2850824 | tf_op jit(solution)/shard_map/ppermute | solution.py:19
  34.7 25.0 %collective-permute-start.9 = (bf16[128,3712]{1,0:T(8,128)(2,1)S(1)}, bf16[128,3712]{1,0:T(8,128)(2,1)S(1)}, u32[]{:S(2)}, u32[]{:S(2)}) collective-permute-start(bf16[128,3712]{1,0:T(8,128)(2,1)S(1)} %collective-permute-done.2.refs_2_), channel_id=1, source_target_pairs={{4,8},{5,9},{6,10},{7,11},{8,4},{9,5},{10,6},{11,7},{20,24},{21,25... | collective-permute-start | bytes 2850824 | tf_op jit(solution)/shard_map/ppermute | solution.py:245
  36.6 22.5 %collective-permute-start.8 = (bf16[128,3712]{1,0:T(8,128)(2,1)}, bf16[128,3712]{1,0:T(8,128)(2,1)S(1)}, u32[]{:S(2)}, u32[]{:S(2)}) collective-permute-start(bf16[128,3712]{1,0:T(8,128)(2,1)} %collective-permute-done.3), channel_id=1, source_target_pairs={{4,0},{5,1},{6,2},{7,3},{8,12},{9,13},{10,14},{11,15},{20,16},{21,... | collective-permute-start | bytes 2850824 | tf_op jit(solution)/shard_map/ppermute | solution.py:245
  38.6 22.1 %collective-permute-start.10 = (bf16[128,1792]{1,0:T(8,128)(2,1)S(1)}, bf16[128,1792]{1,0:T(8,128)(2,1)S(1)}, u32[]{:S(2)}, u32[]{:S(2)}) collective-permute-start(bf16[128,1792]{1,0:T(8,128)(2,1)S(1)} %fusion.12), channel_id=1, source_target_pairs={{0,16},{16,0},{1,17},{17,1},{2,18},{18,2},{3,19},{19,3},{4,20},{20... | collective-permute-start | bytes 1376264 | tf_op jit(solution)/shard_map/ppermute | solution.py:19
  60.7 7.9 %collective-permute-start.15 = (bf16[2,256,1792]{2,1,0:T(8,128)(2,1)}, bf16[2,256,1792]{2,1,0:T(8,128)(2,1)}, u32[]{:S(2)}, u32[]{:S(2)}) collective-permute-start(bf16[2,256,1792]{2,1,0:T(8,128)(2,1)} %get-tuple-element.56), channel_id=1, source_target_pairs={{0,1},{1,0},{2,3},{3,2},{4,5},{5,4},{6,7},{7,6},{8,9},{9,8},{10,11... | collective-permute-start | bytes 5505032 | tf_op jit(solution)/shard_map/ppermute | solution.py:19
  62.2 9.3 %collective-permute-start.12 = (bf16[128,3712]{1,0:T(8,128)(2,1)S(1)}, bf16[128,3712]{1,0:T(8,128)(2,1)S(1)}, u32[]{:S(2)}, u32[]{:S(2)}) collective-permute-start(bf16[128,3712]{1,0:T(8,128)(2,1)S(1)} %broadcast_select_fusion.1.refs_2_), channel_id=1, source_target_pairs={{0,1},{1,0},{2,3},{3,2},{4,5},{5,4},{6,7},{7,6},{8,9},{9,8},{10,11... | collective-permute-start | bytes 2850824 | tf_op jit(solution)/shard_map/ppermute | solution.py:19
  62.7 8.8 %collective-permute-start.11 = (bf16[128,3712]{1,0:T(8,128)(2,1)S(1)}, bf16[128,3712]{1,0:T(8,128)(2,1)}, u32[]{:S(2)}, u32[]{:S(2)}) collective-permute-start(bf16[128,3712]{1,0:T(8,128)(2,1)S(1)} %collective-permute-done.7.refs_1_), channel_id=1, source_target_pairs={{0,1},{1,0},{2,3},{3,2},{4,5},{5,4},{6,7},{7,6},{8,9},{9,8},{10,11... | collective-permute-start | bytes 2850824 | tf_op jit(solution)/shard_map/ppermute | solution.py:19
  62.8 27.4 %collective-permute-start.13 = (bf16[128,3712]{1,0:T(8,128)(2,1)S(1)}, bf16[128,3712]{1,0:T(8,128)(2,1)S(1)}, u32[]{:S(2)}, u32[]{:S(2)}) collective-permute-start(bf16[128,3712]{1,0:T(8,128)(2,1)S(1)} %broadcast_select_fusion.1.refs_2_), channel_id=1, source_target_pairs={{0,2},{1,3},{2,0},{3,1},{4,6},{5,7},{6,4},{7,5},{8,10},{9,11},{10,... | collective-permute-start | bytes 2850824 | tf_op jit(solution)/shard_map/ppermute | solution.py:19
  64.3 25.9 %collective-permute-start.14 = (bf16[128,3712]{1,0:T(8,128)(2,1)S(1)}, bf16[128,3712]{1,0:T(8,128)(2,1)S(1)}, u32[]{:S(2)}, u32[]{:S(2)}) collective-permute-start(bf16[128,3712]{1,0:T(8,128)(2,1)S(1)} %copy-done.9), channel_id=1, source_target_pairs={{4,0},{5,1},{6,2},{7,3},{8,12},{9,13},{10,14},{11,15},{20,16},{21,... | collective-permute-start | bytes 2850824 | tf_op jit(solution)/shard_map/ppermute | solution.py:245
  69.9 22.2 %collective-permute-start.16 = (bf16[256,1792]{1,0:T(8,128)(2,1)S(1)}, bf16[256,1792]{1,0:T(8,128)(2,1)S(1)}, u32[]{:S(2)}, u32[]{:S(2)}) collective-permute-start(bf16[256,1792]{1,0:T(8,128)(2,1)S(1)} %fusion), channel_id=1, source_target_pairs={{0,16},{16,0},{1,17},{17,1},{2,18},{18,2},{3,19},{19,3},{4,20},{20... | collective-permute-start | bytes 2752520 | tf_op jit(solution)/shard_map/ppermute | solution.py:19
  93.1 6.3 %collective-permute-start.21 = (bf16[2,256,1792]{2,1,0:T(8,128)(2,1)}, bf16[2,256,1792]{2,1,0:T(8,128)(2,1)S(1)}, u32[]{:S(2)}, u32[]{:S(2)}) collective-permute-start(bf16[2,256,1792]{2,1,0:T(8,128)(2,1)} %get-tuple-element.63), channel_id=1, source_target_pairs={{0,1},{1,0},{2,3},{3,2},{4,5},{5,4},{6,7},{7,6},{8,9},{9,8},{10,11... | collective-permute-start | bytes 5505032 | tf_op jit(solution)/shard_map/ppermute | solution.py:19
  94.5 6.7 %collective-permute-start.18 = (bf16[128,3712]{1,0:T(8,128)(2,1)S(1)}, bf16[128,3712]{1,0:T(8,128)(2,1)S(1)}, u32[]{:S(2)}, u32[]{:S(2)}) collective-permute-start(bf16[128,3712]{1,0:T(8,128)(2,1)S(1)} %broadcast_select_fusion.refs_2_), channel_id=1, source_target_pairs={{0,1},{1,0},{2,3},{3,2},{4,5},{5,4},{6,7},{7,6},{8,9},{9,8},{10,11... | collective-permute-start | bytes 2850824 | tf_op jit(solution)/shard_map/ppermute | solution.py:19
  95.0 32.9 %collective-permute-start.19 = (bf16[128,3712]{1,0:T(8,128)(2,1)S(1)}, bf16[128,3712]{1,0:T(8,128)(2,1)S(1)}, u32[]{:S(2)}, u32[]{:S(2)}) collective-permute-start(bf16[128,3712]{1,0:T(8,128)(2,1)S(1)} %broadcast_select_fusion.refs_2_), channel_id=1, source_target_pairs={{0,2},{1,3},{2,0},{3,1},{4,6},{5,7},{6,4},{7,5},{8,10},{9,11},{10,... | collective-permute-start | bytes 2850824 | tf_op jit(solution)/shard_map/ppermute | solution.py:19
  95.5 6.7 %collective-permute-start.17 = (bf16[128,3712]{1,0:T(8,128)(2,1)S(1)}, bf16[128,3712]{1,0:T(8,128)(2,1)}, u32[]{:S(2)}, u32[]{:S(2)}) collective-permute-start(bf16[128,3712]{1,0:T(8,128)(2,1)S(1)} %collective-permute-done.13.refs_1_), channel_id=1, source_target_pairs={{0,1},{1,0},{2,3},{3,2},{4,5},{5,4},{6,7},{7,6},{8,9},{9,8},{10,11... | collective-permute-start | bytes 2850824 | tf_op jit(solution)/shard_map/ppermute | solution.py:19
  97.9 30.0 %collective-permute-start.20 = (bf16[128,1792]{1,0:T(8,128)(2,1)}, bf16[128,1792]{1,0:T(8,128)(2,1)S(1)}, u32[]{:S(2)}, u32[]{:S(2)}) collective-permute-start(bf16[128,1792]{1,0:T(8,128)(2,1)} %slice.157), channel_id=1, source_target_pairs={{0,2},{1,3},{2,0},{3,1},{4,6},{5,7},{6,4},{7,5},{8,10},{9,11},{10,... | collective-permute-start | bytes 1376264 | tf_op jit(solution)/shard_map/ppermute | solution.py:19
  99.7 28.2 %collective-permute-start.22 = (bf16[256,1792]{1,0:T(8,128)(2,1)S(1)}, bf16[256,1792]{1,0:T(8,128)(2,1)S(1)}, u32[]{:S(2)}, u32[]{:S(2)}) collective-permute-start(bf16[256,1792]{1,0:T(8,128)(2,1)S(1)} %fusion.1), channel_id=1, source_target_pairs={{0,16},{16,0},{1,17},{17,1},{2,18},{18,2},{3,19},{19,3},{4,20},{20... | collective-permute-start | bytes 2752520 | tf_op jit(solution)/shard_map/ppermute | solution.py:19
  127.9 5.4 %collective-permute-start.25 = (bf16[2,256,1792]{2,1,0:T(8,128)(2,1)}, bf16[2,256,1792]{2,1,0:T(8,128)(2,1)S(1)}, u32[]{:S(2)}, u32[]{:S(2)}) collective-permute-start(bf16[2,256,1792]{2,1,0:T(8,128)(2,1)} %get-tuple-element.70), channel_id=1, source_target_pairs={{0,1},{1,0},{2,3},{3,2},{4,5},{5,4},{6,7},{7,6},{8,9},{9,8},{10,11... | collective-permute-start | bytes 5505032 | tf_op jit(solution)/shard_map/ppermute | solution.py:19
  128.0 11.3 %collective-permute-start.23 = (bf16[128,3712]{1,0:T(8,128)(2,1)S(1)}, bf16[128,3712]{1,0:T(8,128)(2,1)S(1)}, u32[]{:S(2)}, u32[]{:S(2)}) collective-permute-start(bf16[128,3712]{1,0:T(8,128)(2,1)S(1)} %collective-permute-done.19.refs_1_), channel_id=1, source_target_pairs={{0,1},{1,0},{2,3},{3,2},{4,5},{5,4},{6,7},{7,6},{8,9},{9,8},{10,11... | collective-permute-start | bytes 2850824 | tf_op jit(solution)/shard_map/ppermute | solution.py:19
  135.7 22.7 %collective-permute-start.26 = (bf16[256,1792]{1,0:T(8,128)(2,1)}, bf16[256,1792]{1,0:T(8,128)(2,1)}, u32[]{:S(2)}, u32[]{:S(2)}) collective-permute-start(bf16[256,1792]{1,0:T(8,128)(2,1)} %fusion.2), channel_id=1, source_target_pairs={{0,16},{16,0},{1,17},{17,1},{2,18},{18,2},{3,19},{19,3},{4,20},{20... | collective-permute-start | bytes 2752520 | tf_op jit(solution)/shard_map/ppermute | solution.py:19
  138.7 12.9 %collective-permute-start.24 = (bf16[128,1792]{1,0:T(8,128)(2,1)S(1)}, bf16[128,1792]{1,0:T(8,128)(2,1)S(1)}, u32[]{:S(2)}, u32[]{:S(2)}) collective-permute-start(bf16[128,1792]{1,0:T(8,128)(2,1)S(1)} %slice.156), channel_id=1, source_target_pairs={{0,2},{1,3},{2,0},{3,1},{4,6},{5,7},{6,4},{7,5},{8,10},{9,11},{10,... | collective-permute-start | bytes 1376264 | tf_op jit(solution)/shard_map/ppermute | solution.py:19
  158.5 29.8 %collective-permute-start.27 = (bf16[128,1792]{1,0:T(8,128)(2,1)S(1)}, bf16[128,1792]{1,0:T(8,128)(2,1)S(1)}, u32[]{:S(2)}, u32[]{:S(2)}) collective-permute-start(bf16[128,1792]{1,0:T(8,128)(2,1)S(1)} %fusion.5), channel_id=1, source_target_pairs={{0,4},{1,5},{2,6},{3,7},{4,0},{5,1},{6,2},{7,3},{8,12},{9,13},{10,... | collective-permute-start | bytes 1376264 | tf_op jit(solution)/shard_map/ppermute | solution.py:19
  161.0 12.6 %collective-permute-start.31 = (bf16[128,1792]{1,0:T(8,128)(2,1)S(1)}, bf16[128,1792]{1,0:T(8,128)(2,1)S(1)}, u32[]{:S(2)}, u32[]{:S(2)}) collective-permute-start(bf16[128,1792]{1,0:T(8,128)(2,1)S(1)} %fusion.13), channel_id=1, source_target_pairs={{0,16},{16,0},{1,17},{17,1},{2,18},{18,2},{3,19},{19,3},{4,20},{20... | collective-permute-start | bytes 1376264 | tf_op jit(solution)/shard_map/ppermute | solution.py:19
  164.2 13.0 %collective-permute-start.28 = (bf16[128,1792]{1,0:T(8,128)(2,1)S(1)}, bf16[128,1792]{1,0:T(8,128)(2,1)S(1)}, u32[]{:S(2)}, u32[]{:S(2)}) collective-permute-start(bf16[128,1792]{1,0:T(8,128)(2,1)S(1)} %slice.155), channel_id=1, source_target_pairs={{0,2},{1,3},{2,0},{3,1},{4,6},{5,7},{6,4},{7,5},{8,10},{9,11},{10,... | collective-permute-start | bytes 1376264 | tf_op jit(solution)/shard_map/ppermute | solution.py:19
  173.8 12.6 %collective-permute-start.32 = (bf16[128,1792]{1,0:T(8,128)(2,1)S(1)}, bf16[128,1792]{1,0:T(8,128)(2,1)S(1)}, u32[]{:S(2)}, u32[]{:S(2)}) collective-permute-start(bf16[128,1792]{1,0:T(8,128)(2,1)S(1)} %fusion.6), channel_id=1, source_target_pairs={{0,2},{1,3},{2,0},{3,1},{4,6},{5,7},{6,4},{7,5},{8,10},{9,11},{10,... | collective-permute-start | bytes 1376264 | tf_op jit(solution)/shard_map/ppermute | solution.py:19
  177.3 30.8 %collective-permute-start.29 = (bf16[128,1792]{1,0:T(8,128)(2,1)S(1)}, bf16[128,1792]{1,0:T(8,128)(2,1)S(1)}, u32[]{:S(2)}, u32[]{:S(2)}) collective-permute-start(bf16[128,1792]{1,0:T(8,128)(2,1)S(1)} %fusion.4), channel_id=1, source_target_pairs={{0,8},{1,9},{2,10},{3,11},{4,12},{5,13},{6,14},{7,15},{8,0},{9,1},... | collective-permute-start | bytes 1376264 | tf_op jit(solution)/shard_map/ppermute | solution.py:19
  186.5 31.1 %collective-permute-start.33 = (bf16[128,1792]{1,0:T(8,128)(2,1)S(1)}, bf16[128,1792]{1,0:T(8,128)(2,1)S(1)}, u32[]{:S(2)}, u32[]{:S(2)}) collective-permute-start(bf16[128,1792]{1,0:T(8,128)(2,1)S(1)} %fusion.3), channel_id=1, source_target_pairs={{0,12},{1,13},{2,14},{3,15},{4,8},{5,9},{6,10},{7,11},{8,4},{9,5},... | collective-permute-start | bytes 1376264 | tf_op jit(solution)/shard_map/ppermute | solution.py:19
  (26 other events, 167.9 us)

commit v3 on v2

--- a/solution.py
+++ b/solution.py
@@ -11,7 +11,7 @@
 LANES = 128
 SIDE = 256
 AHEAD = 2
-VMEM = 52 * 1024 * 1024
+VMEM = 42 * 1024 * 1024
 
 
 def exchange(value, axis, mask):
@@ -21,7 +21,8 @@
 
 def widen_body(experts, tokens, ids, weight, rows):
     count, width = tokens.shape
-    rates = weight[...]
+    ids = jnp.transpose(ids[...])
+    rates = jnp.transpose(weight[...])
     rates = routed_scale * rates / jnp.sum(rates, axis=1, keepdims=True)
     lane = lax.broadcasted_iota(jnp.int32, (count, LANES), 1)
     total = jnp.zeros((count, LANES), jnp.float32)
@@ -41,21 +42,21 @@
     return pl.pallas_call(
         functools.partial(widen_body, experts),
         out_shape=jax.ShapeDtypeStruct((count, width + LANES), tokens.dtype),
-        in_specs=[pl.BlockSpec(memory_space=pltpu.VMEM)] * 3,
-        out_specs=pl.BlockSpec(memory_space=pltpu.VMEM),
+        grid=(1,),
+        in_specs=[pl.BlockSpec(array.shape, lambda i: (0, 0)) for array in (tokens, ids.T, weight.T)],
+        out_specs=pl.BlockSpec((count, width + LANES), lambda i: (0, 0)),
         compiler_params=pltpu.CompilerParams(vmem_limit_bytes=16 * 1024 * 1024),
         name="widen",
-    )(tokens, ids, weight)
-
-
-def ffn_body(experts, blocks, out_rows, scaled, added, n_in, n_out, *refs):
+    )(tokens, ids.T, weight.T)
+
+
+def ffn_body(experts, blocks, out_rows, scaled, n_in, n_out, *refs):
     info = refs[0]
     inputs = refs[1 : 1 + n_in]
     gate, up, down = refs[1 + n_in : 4 + n_in]
-    extra = refs[4 + n_in] if added else None
-    refs = refs[4 + n_in + added :]
+    refs = refs[4 + n_in :]
     outs = refs[:n_out]
-    x, gate_v, up_v, down_v, act, factor, result, x_sem, gate_sem, up_sem, down_sem, out_sem = refs[n_out : n_out + 12]
+    x, gate_v, up_v, down_v, act, factor, result, x_sem, gate_sem, up_sem, down_sem, out_sem = refs[n_out:]
     width, hidden = gate.shape
     steps = hidden // SIDE
     tile = result.shape[2]
@@ -66,11 +67,6 @@
     for number, source in enumerate(inputs):
         size = source.shape[0]
         copies.append(pltpu.make_async_copy(source, x.at[pl.ds(number * size, size), :], x_sem.at[number]))
-    if added:
-        extra_v, extra_sem = refs[n_out + 12 :]
-        count = extra.shape[1]
-        more = pltpu.make_async_copy(extra, extra_v, extra_sem.at[0])
-
     def side(weights, held, sems, j):
         return pltpu.make_async_copy(
             weights.at[:, pl.ds(pl.multiple_of(j * SIDE, SIDE), SIDE)], held.at[j], sems.at[j]
@@ -114,8 +110,6 @@
 
     if steps <= AHEAD:
         lowers()
-    if added:
-        more.start()
 
     def first(j, carry):
         side(gate, gate_v, gate_sem, j).wait()
@@ -141,17 +135,10 @@
 
     lax.fori_loop(0, steps, first, 0)
 
-    if added:
-        more.wait()
-
     def second(i, carry):
         lower(i).wait()
         value = jnp.dot(act[...], down_v[i], preferred_element_type=jnp.float32)
-        if added:
-            result[i, :count, :] = (value[:count] + extra_v[i]).astype(result.dtype)
-            result[i, count:, :] = value[count:].astype(result.dtype)
-        else:
-            result[i] = value.astype(result.dtype)
+        result[i] = value.astype(result.dtype)
         for copy in leave(i):
             copy.start()
         return carry
@@ -166,7 +153,7 @@
     lax.fori_loop(0, blocks * per_block, finish, 0)
 
 
-def ffn(info, inputs, gate, up, down, extra, experts, blocks, out_rows, scaled, dtype, name):
+def ffn(info, inputs, gate, up, down, experts, blocks, out_rows, scaled, dtype, name):
     width, hidden = gate.shape
     row_width = inputs[0].shape[1]
     rows = sum(count for _, count in out_rows)
@@ -174,8 +161,7 @@
     tile = width // tiles
     steps = hidden // SIDE
     flops = 6 * rows * width * hidden
-    added = 0 if extra is None else 1
-    body = functools.partial(ffn_body, experts, blocks, out_rows, scaled, added, len(inputs), len(out_rows))
+    body = functools.partial(ffn_body, experts, blocks, out_rows, scaled, len(inputs), len(out_rows))
     scratch = [
         pltpu.VMEM((rows, row_width), jnp.bfloat16),
         pltpu.VMEM((steps, width, SIDE), jnp.bfloat16),
@@ -190,21 +176,19 @@
         pltpu.SemaphoreType.DMA((tiles,)),
         pltpu.SemaphoreType.DMA((tiles, len(out_rows))),
     ]
-    if added:
-        scratch += [pltpu.VMEM((tiles, extra.shape[1], tile), jnp.float32), pltpu.SemaphoreType.DMA((1,))]
     return pl.pallas_call(
         body,
         out_shape=[jax.ShapeDtypeStruct((blocks, count, width // blocks), dtype) for _, count in out_rows],
         in_specs=[pl.BlockSpec(memory_space=pltpu.SMEM)]
-        + [pl.BlockSpec(memory_space=pltpu.HBM)] * (len(inputs) + 3 + added),
-        out_specs=[pl.BlockSpec(memory_space=pltpu.HBM)] * len(out_rows),
+        + [pl.BlockSpec(memory_space=pl.ANY)] * (len(inputs) + 3),
+        out_specs=[pl.BlockSpec(memory_space=pl.ANY)] * len(out_rows),
         scratch_shapes=scratch,
         compiler_params=pltpu.CompilerParams(vmem_limit_bytes=VMEM),
         cost_estimate=pl.CostEstimate(
             flops=flops, bytes_accessed=6 * width * hidden + 4 * rows * width, transcendentals=rows * hidden
         ),
         name=name,
-    )(info, *inputs, gate, up, down, *([extra] if added else []))
+    )(info, *inputs, *[pltpu.with_memory_space_constraint(array, pltpu.HBM) for array in (gate, up, down)])
 
 
 def local(
@@ -241,6 +225,10 @@
     def over_dp(sends):
         return [exchange(send, "dp", k + 1) for k, send in enumerate(sends)]
 
+    def across_both(value, k):
+        pairs = [(d * experts + e, (d ^ k) * experts + (e ^ 2)) for d in range(n_dp) for e in range(experts)]
+        return lax.ppermute(value, ("dp", "expert"), pairs)
+
     def over_planes(value, pairs):
         return lax.ppermute(value, "expert", [(4 * s + k, 4 * t + k) for s, t in pairs for k in range(4)])
 
@@ -251,60 +239,55 @@
         parts = value.transpose(1, 0, 2).reshape(rows, n_dp, width // n_dp)
         return jnp.take(parts, dp ^ jnp.arange(n_dp), axis=1).transpose(1, 0, 2)
 
-    def routed(inputs, extra=None):
+    def routed(inputs):
         half = len(inputs) // 2 * count
         halves = ((0, half), (half, half))
-        kept, sent = ffn(info, inputs, *weights, extra, experts, blocks, halves, True, bf16, "routed_expert")
+        kept, sent = ffn(info, inputs, *weights, experts, blocks, halves, True, bf16, "routed_expert")
         return by_dp(kept), by_dp(sent)
 
-    def to_dp(kept, met):
-        return [(kept[k].astype(f32) + met[k].astype(f32)).astype(bf16) for k in range(1, n_dp)]
-
-    def owned(kept, met, came):
-        whole = kept[0].astype(f32) + met[0].astype(f32)
+    def shared(rows):
+        halves = ((0, count),)
+        out = ffn(info, [rows], shared_gate, shared_up, shared_down, experts, blocks, halves, False, f32, "shared_expert")
+        return by_dp(out[0])
+
+    def to_dp(kept, met, part=slice(None)):
+        return [(kept[k, part].astype(f32) + met[k, part].astype(f32)).astype(bf16) for k in range(1, n_dp)]
+
+    def owned(kept, met, came, part=slice(None)):
+        whole = kept[0, part].astype(f32) + met[0, part].astype(f32)
         for value in came:
             whole = whole + value.astype(f32)
         return whole
 
+    def of(values, part):
+        return [value[part] for value in values]
+
     def together(*values):
         return lax.optimization_barrier(values)
 
+    upper, lower = slice(None, count), slice(count, None)
     wide = widen(tokens, expert_ids, route_weight, experts)
-    shared_part = ffn(
-        info,
-        [tokens],
-        shared_gate,
-        shared_up,
-        shared_down,
-        None,
-        experts,
-        blocks,
-        ((0, count),),
-        False,
-        f32,
-        "shared_expert",
-    )[0]
-    if blocks == 1:
-        shared_part = shared_part.reshape(count, 2, width // 2).transpose(1, 0, 2)
-
     if planes == 4:
         inner = (plane == 1) | (plane == 2)
+        cut = count * 3 // 4
         middle, outward = ((1, 2), (2, 1)), ((1, 0), (2, 3))
         row_own = over_row(wide)
         near = over_planes(wide, ((0, 1), (1, 0), (2, 3), (3, 2)))
         opposite = over_planes(wide, middle)
-        kept_0, sent_0 = routed([wide, over_core(wide)], shared_part)
-        kept_0, sent_0, row_own, near, opposite = together(kept_0, sent_0, row_own, near, opposite)
+        shared_part = shared(tokens)
+        kept_0, sent_0 = routed([wide, over_core(wide)])
+        kept_0, near, opposite = together(kept_0, near, opposite)
+        kept_0, sent_0, row_own, shared_part = together(kept_0, sent_0, row_own, shared_part)
 
         inputs = [row_own, near, over_core(row_own), over_core(near)]
         row_near = over_row(near)
         from_outer, from_inner = over_planes(opposite, outward), over_planes(near, middle)
         met_0 = over_core(sent_0)
-        came_0 = over_dp(to_dp(kept_0, met_0))
+        own = kept_0.astype(f32) + met_0.astype(f32) + shared_part
+        came_0 = over_dp([own[k].astype(bf16) for k in range(1, n_dp)])
         kept_1, sent_1 = routed(inputs)
-        kept_1, sent_1, row_near, from_outer, from_inner, *came_0 = together(
-            kept_1, sent_1, row_near, from_outer, from_inner, *came_0
-        )
+        kept_1, sent_1, row_near, *came_0 = together(kept_1, sent_1, row_near, *came_0)
+        kept_1, from_outer, from_inner = together(kept_1, from_outer, from_inner)
 
         next_ = jnp.where(inner, from_inner, from_outer)
         inputs = [row_near, next_, over_core(row_near), over_core(next_)]
@@ -313,49 +296,60 @@
         met_1 = over_core(sent_1)
         came_1 = over_dp(to_dp(kept_1, met_1))
         kept_2, sent_2 = routed(inputs)
-        kept_2, sent_2, row_next, last, *came_1 = together(kept_2, sent_2, row_next, last, *came_1)
+        kept_2, sent_2, row_next, *came_1 = together(kept_2, sent_2, row_next, *came_1)
+        kept_2, last = together(kept_2, last)
 
         far = jnp.where(inner, opposite, last)
         inputs = [row_next, far, over_core(row_next), over_core(far)]
         row_far = over_row(far)
         met_2 = over_core(sent_2)
-        whole_1 = owned(kept_1, met_1, came_1)
-        back_0 = over_row(whole_1[:count].astype(bf16))
+        home_1 = exchange(owned(kept_1, met_1, of(came_1, lower), lower).astype(bf16), "expert", 4)
         came_2 = over_dp(to_dp(kept_2, met_2))
         kept_3, sent_3 = routed(inputs)
-        kept_3, sent_3, row_far, back_0, *came_2 = together(kept_3, sent_3, row_far, back_0, *came_2)
+        kept_3, sent_3, row_far, home_1, *came_2 = together(kept_3, sent_3, row_far, home_1, *came_2)
 
         inputs = [row_far, over_core(row_far)]
         met_3 = over_core(sent_3)
-        whole_2 = owned(kept_2, met_2, came_2)
-        back_1 = over_row(whole_2[:count].astype(bf16))
-        came_3 = over_dp(to_dp(kept_3, met_3))
+        cross_1 = exchange(owned(kept_2, met_2, of(came_2, upper), upper).astype(bf16), "expert", 4)
+        total_2 = owned(kept_2, met_2, of(came_2, lower), lower).astype(bf16)
+        home_2 = exchange(total_2[:cut], "expert", 8)
+        came_3 = over_dp(to_dp(kept_3, met_3, upper))
         kept_4, sent_4 = routed(inputs)
-        kept_4, sent_4, back_1, *came_3 = together(kept_4, sent_4, back_1, *came_3)
+        kept_4, sent_4, home_2, *came_3 = together(kept_4, sent_4, home_2, *came_3)
 
         met_4 = over_core(sent_4)
-        whole_3 = owned(kept_3, met_3, came_3)
-        back_2 = over_row(whole_3[:count].astype(bf16))
-        came_4 = over_dp(to_dp(kept_4, met_4))
-        back_3 = over_row(owned(kept_4, met_4, came_4).astype(bf16))
-        totals = [
-            owned(kept_0, met_0, came_0) + back_0.astype(f32),
-            whole_1[count:] + back_1.astype(f32),
-            whole_2[count:] + back_2.astype(f32),
-            whole_3[count:] + back_3.astype(f32),
-        ]
+        sends = [(kept_4[k].astype(f32) + met_4[k].astype(f32)).astype(bf16) for k in range(n_dp)]
+        back_3 = [over_row(sends[0])] + [across_both(send, k) for k, send in enumerate(sends) if k]
+        cross_2 = owned(kept_3, met_3, came_3, upper).astype(bf16)
+        cross_2 = exchange(jnp.concatenate([cross_2, total_2[cut:]], axis=0), "expert", 8)
+        *sends, _ = together(*to_dp(kept_3, met_3, lower), sends[0])
+        came_far = over_dp(sends)
+        back_3[0], back_3[1], cross_1, cross_2, *came_far = together(*back_3[:2], cross_1, cross_2, *came_far)
+        total_3 = owned(kept_3, met_3, came_far + back_3, lower)
+        home_3 = exchange(total_3.astype(bf16), "expert", 12)
+        cross = cross_1.astype(f32) + cross_2[:count].astype(f32)
+        back_0 = over_row((owned(kept_1, met_1, of(came_1, upper), upper) + cross).astype(bf16))
+        home_2 = jnp.concatenate([home_2, cross_2[count:]], axis=0)
+        homes = [home_1, home_2, home_3]
+        answer = own[0] + back_0.astype(f32)
+        for value in came_0:
+            answer = answer + value.astype(f32)
     else:
         totals = []
         for s in range(planes):
             here = exchange(wide, "expert", 4 * s) if s else wide
             across = over_row(here)
-            kept, sent = routed([here, across, over_core(here), over_core(across)], None if s else shared_part)
+            kept, sent = routed([here, across, over_core(here), over_core(across)])
             met = over_core(sent)
             whole = owned(kept, met, over_dp(to_dp(kept, met)))
             totals.append(whole[:count] + over_row(whole[count:].astype(bf16)).astype(f32))
-    answer = totals[0]
-    for s in range(1, planes):
-        answer = answer + exchange(totals[s].astype(bf16), "expert", 4 * s).astype(f32)
+        homes = [exchange(totals[s].astype(bf16), "expert", 4 * s) for s in range(1, planes)]
+        shared_part = shared(tokens)
+        answer = totals[0] + shared_part[0]
+        for value in over_dp([shared_part[k].astype(bf16) for k in range(1, n_dp)]):
+            answer = answer + value.astype(f32)
+    for value in homes:
+        answer = answer + value.astype(f32)
     return answer.astype(bf16)
 
 

time: 219 us -> 188 us (0.86)
  waiting for transfers between devices: 74.5 us -> 49.8 us
  local copies, waits for them, and re-layouts: 10.2 us -> 3.25 us
  starting transfers between devices: 32.8 us -> 39.4 us
  other arithmetic: 13.4 us -> 9.57 us
    ppermute x29, waiting for transfers between devices: 73.5 us -> 48.8 us  [exchange(): return lax.ppermute(value, axis, pairs)]
    unnamed x50 -> x14, local copies, waits for them, and re-layouts: 8.7 us -> 2.58 us
    add x3 -> x1, other arithmetic: 4.64 us -> 0.28 us  [local(): own = kept_0.astype(f32) + met_0.astype(f32) + shared_part]
    ppermute x29, starting transfers between devices: 20.2 us -> 23.8 us  [exchange(): return lax.ppermute(value, axis, pairs)]
    pallas_call x6, Pallas kernels: 86.4 us -> 84 us  [ffn(): pl.pallas_call(body, out_shape=[jax.ShapeDtypeStruct((blocks, count, widt...]
  transfers between devices with their start and end apart: 34 -> 35, of which waited for: 13 -> 10; matrix products, arithmetic and copies ran while one was open for 6% -> 5% of each run, Pallas kernels for 39% -> 45%
where the time goes in v3:
time: 188 us
  Pallas kernels  84.9 us (45%)
  waiting for transfers between devices  49.8 us (26%)
  starting transfers between devices  39.4 us (21%)
  other arithmetic  9.57 us (5%)
  local copies, waits for them, and re-layouts  3.25 us (2%)
    pallas_call x6, Pallas kernels, ffn(): pl.pallas_call(body, out_shape=[jax.ShapeDtypeStruct((blocks, count, widt...  84 us
    ppermute x29, waiting for transfers between devices, exchange(): return lax.ppermute(value, axis, pairs)  48.8 us
    ppermute x29, starting transfers between devices, exchange(): return lax.ppermute(value, axis, pairs)  23.8 us
    ppermute x5, starting transfers between devices, over_planes(): lax.ppermute(value, 'expert', [(4 * s + k, 4 * t + k) for s, t in pairs f...  14 us
  transfers between devices with their start and end apart: 35, of which 10 were waited for; matrix products, arithmetic and copies ran while one was open for 5% of the time, Pallas kernels for 45%

profile of v3, /device:TPU:8, one launch (start us, length us, event | category | flops | bytes accessed | tf_op | source)
XLA Modules:
  0.0 187.8 jit_solution(4520723265434636350)
XLA Ops:
  3.6 5.0 %collective-permute-start.2 = (bf16[128,3712]{1,0:T(8,128)(2,1)S(1)}, bf16[128,3712]{1,0:T(8,128)(2,1)}, u32[]{:S(2)}, u32[]{:S(2)}) collective-permute-start(bf16[128,3712]{1,0:T(8,128)(2,1)S(1)} %widen.1.refs_1_), channel_id=1, source_target_pairs={{4,8},{5,9},{6,10},{7,11},{8,4},{9,5},{10,6},{11,7},{20,24},{21,25... | collective-permute-start | bytes 2850824 | tf_op jit(solution)/shard_map/ppermute | solution.py:233
  8.7 1.6 collective-permute-start.3
  11.6 9.5 %shared_expert.1 = f32[2,128,1792]{2,1,0:T(8,128)S(1)} custom-call(s32[2]{0:T(128)S(1)} %pad_add_fusion.refs_0_, bf16[128,3584]{1,0:T(8,128)(2,1)S(1)} %copy-done.1, bf16[3584,1024]{1,0:T(8,128)(2,1)} %refs_2_.1, bf16[3584,1024]{1,0:T(8,128)(2,1)} %refs_3_.1, bf16[1024,3584]{1,0:T(8,128)(2,1)} %refs_4_.1), custom_call_target="tpu_custom_call" | custom-call | flops 2818572288 | bytes 23855104 | tf_op jit(solution)/shard_map/shared_expert/pallas_call | solution.py:179
  21.1 11.3 %routed_expert.5 = (bf16[2,128,1792]{2,1,0:T(8,128)(2,1)S(1)}, bf16[2,128,1792]{2,1,0:T(8,128)(2,1)S(1)}) custom-call(s32[2]{0:T(128)S(1)} %pad_add_fusion.refs_0_, bf16[128,3712]{1,0:T(8,128)(2,1)S(1)} %widen.1.refs_1_, bf16[128,3712]{1,0:T(8,128)(2,1)S(1)} %collective-permute-done.refs_2_, bf16[3584,1024]{1,0:T(8,128)(2,1)} %bitcast.68, ...), custom_call_target="tpu_custom_call" | custom-call | flops 5637144576 | bytes 25690112 | tf_op jit(solution)/shard_map/routed_expert/pallas_call | solution.py:179
  33.7 2.2 %collective-permute-start.10 = (bf16[128,3712]{1,0:T(8,128)(2,1)}, bf16[128,3712]{1,0:T(8,128)(2,1)}, u32[]{:S(2)}, u32[]{:S(2)}) collective-permute-start(bf16[128,3712]{1,0:T(8,128)(2,1)} %collective-permute-done.1.refs_2_), channel_id=1, source_target_pairs={{4,8},{5,9},{6,10},{7,11},{8,4},{9,5},{10,6},{11,7},{20,24},{21,25... | collective-permute-start | bytes 2850824 | tf_op jit(solution)/shard_map/ppermute | solution.py:233
  36.0 2.2 %collective-permute-start.9 = (bf16[128,3712]{1,0:T(8,128)(2,1)}, bf16[128,3712]{1,0:T(8,128)(2,1)}, u32[]{:S(2)}, u32[]{:S(2)}) collective-permute-start(bf16[128,3712]{1,0:T(8,128)(2,1)} %collective-permute-done.2), channel_id=1, source_target_pairs={{4,0},{5,1},{6,2},{7,3},{8,12},{9,13},{10,14},{11,15},{20,16},{21,... | collective-permute-start | bytes 2850824 | tf_op jit(solution)/shard_map/ppermute | solution.py:233
  38.7 1.5 collective-permute-start.8
  40.2 17.4 %routed_expert.6 = (bf16[2,256,1792]{2,1,0:T(8,128)(2,1)S(1)}, bf16[2,256,1792]{2,1,0:T(8,128)(2,1)}) custom-call(s32[2]{0:T(128)S(1)} %pad_add_fusion.refs_0_, bf16[128,3712]{1,0:T(8,128)(2,1)} %collective-permute-done.3.refs_1_, bf16[128,3712]{1,0:T(8,128)(2,1)} %collective-permute-done.1.refs_2_, bf16[128,3712]{1,0:T(8,128)(2,1)S(1)} %collective-permute-done.5.refs_3_, ...), custom_call_target="tpu_custom_call" | custom-call | flops 11274289152 | bytes 29360128 | tf_op jit(solution)/shard_map/routed_expert/pallas_call | solution.py:179
  58.8 1.3 broadcast_select_fusion.1.refs_2_
  60.7 1.2 collective-permute-start.14
  61.9 4.5 %collective-permute-start.16 = (bf16[128,3712]{1,0:T(8,128)(2,1)}, bf16[128,3712]{1,0:T(8,128)(2,1)S(1)}, u32[]{:S(2)}, u32[]{:S(2)}) collective-permute-start(bf16[128,3712]{1,0:T(8,128)(2,1)} %collective-permute-done.10), channel_id=1, source_target_pairs={{4,0},{5,1},{6,2},{7,3},{8,12},{9,13},{10,14},{11,15},{20,16},{21,... | collective-permute-start | bytes 2850824 | tf_op jit(solution)/shard_map/ppermute | solution.py:233
  66.4 1.4 fusion
  67.8 1.6 collective-permute-start.15
  69.4 17.2 %routed_expert.7 = (bf16[2,256,1792]{2,1,0:T(8,128)(2,1)S(1)}, bf16[2,256,1792]{2,1,0:T(8,128)(2,1)S(1)}) custom-call(s32[2]{0:T(128)S(1)} %pad_add_fusion.refs_0_, bf16[128,3712]{1,0:T(8,128)(2,1)S(1)} %collective-permute-done.7.refs_1_, bf16[128,3712]{1,0:T(8,128)(2,1)S(1)} %broadcast_select_fusion.1.refs_2_, ...), custom_call_target="tpu_custom_call" | custom-call | flops 11274289152 | bytes 29360128 | tf_op jit(solution)/shard_map/routed_expert/pallas_call | solution.py:179
  86.6 3.0 %collective-permute-done.15 = bf16[256,1792]{1,0:T(8,128)(2,1)S(1)} collective-permute-done((bf16[256,1792]{1,0:T(8,128)(2,1)S(1)}, bf16[256,1792]{1,0:T(8,128)(2,1)S(1)}, u32[]{:S(2)}, u32[]{:S(2)}) %collective-permute-start.15) | collective-permute-done | bytes 917536 | tf_op jit(solution)/shard_map/ppermute | solution.py:19
  89.7 1.4 broadcast_select_fusion.refs_2_
  94.0 1.6 collective-permute-start.22
  96.2 17.2 %routed_expert.8 = (bf16[2,256,1792]{2,1,0:T(8,128)(2,1)S(1)}, bf16[2,256,1792]{2,1,0:T(8,128)(2,1)S(1)}) custom-call(s32[2]{0:T(128)S(1)} %pad_add_fusion.refs_0_, bf16[128,3712]{1,0:T(8,128)(2,1)S(1)} %collective-permute-done.14.refs_1_, bf16[128,3712]{1,0:T(8,128)(2,1)S(1)} %broadcast_select_fusion.refs_2_, ...), custom_call_target="tpu_custom_call" | custom-call | flops 11274289152 | bytes 29360128 | tf_op jit(solution)/shard_map/routed_expert/pallas_call | solution.py:179
  113.4 1.2 collective-permute-done.19.refs_1_
  114.6 2.2 %collective-permute-done.22 = bf16[256,1792]{1,0:T(8,128)(2,1)S(1)} collective-permute-done((bf16[256,1792]{1,0:T(8,128)(2,1)S(1)}, bf16[256,1792]{1,0:T(8,128)(2,1)S(1)}, u32[]{:S(2)}, u32[]{:S(2)}) %collective-permute-start.22) | collective-permute-done | bytes 917536 | tf_op jit(solution)/shard_map/ppermute | solution.py:19
  117.7 3.0 %collective-permute-start.24 = (bf16[96,1792]{1,0:T(8,128)(2,1)S(1)}, bf16[96,1792]{1,0:T(8,128)(2,1)S(1)}, u32[]{:S(2)}, u32[]{:S(2)}) collective-permute-start(bf16[96,1792]{1,0:T(8,128)(2,1)S(1)} %slice.144), channel_id=1, source_target_pairs={{0,8},{1,9},{2,10},{3,11},{4,12},{5,13},{6,14},{7,15},{8,0},{9,1},... | collective-permute-start | bytes 1032200 | tf_op jit(solution)/shard_map/ppermute | solution.py:19
  120.9 1.6 collective-permute-start.26
  122.5 11.3 %routed_expert.9 = (bf16[2,128,1792]{2,1,0:T(8,128)(2,1)S(1)}, bf16[2,128,1792]{2,1,0:T(8,128)(2,1)S(1)}) custom-call(s32[2]{0:T(128)S(1)} %pad_add_fusion.refs_0_, bf16[128,3712]{1,0:T(8,128)(2,1)S(1)} %collective-permute-done.19.refs_1_, bf16[128,3712]{1,0:T(8,128)(2,1)S(1)} %collective-permute-done.23.refs_2_, bf16[3584,1024]{1,0:T(8,128)(2,1)} %bitcast.72, ...), custom_call_target="tpu_custom_call" | custom-call | flops 5637144576 | bytes 25690112 | tf_op jit(solution)/shard_map/routed_expert/pallas_call | solution.py:179
  133.8 1.5 collective-permute-done.24
  135.3 2.5 %collective-permute-start.30 = (bf16[128,1792]{1,0:T(8,128)(2,1)S(1)}, bf16[128,1792]{1,0:T(8,128)(2,1)S(1)}, u32[]{:S(2)}, u32[]{:S(2)}) collective-permute-start(bf16[128,1792]{1,0:T(8,128)(2,1)S(1)} %get-tuple-element.95), channel_id=1, source_target_pairs={{0,4},{1,5},{2,6},{3,7},{4,0},{5,1},{6,2},{7,3},{8,12},{9,13},{10,... | collective-permute-start | bytes 1376264 | tf_op jit(solution)/shard_map/ppermute | solution.py:19
  139.3 1.5 collective-permute-start.28
  140.8 1.6 collective-permute-start.29
  142.9 14.8 %collective-permute-done.30 = bf16[128,1792]{1,0:T(8,128)(2,1)S(1)} collective-permute-done((bf16[128,1792]{1,0:T(8,128)(2,1)S(1)}, bf16[128,1792]{1,0:T(8,128)(2,1)S(1)}, u32[]{:S(2)}, u32[]{:S(2)}) %collective-permute-start.30) | collective-permute-done | bytes 458784 | tf_op jit(solution)/shard_map/ppermute | solution.py:19
  157.6 6.7 %collective-permute-done.31 = bf16[160,1792]{1,0:T(8,128)(2,1)S(1)} collective-permute-done((bf16[160,1792]{1,0:T(8,128)(2,1)S(1)}, bf16[160,1792]{1,0:T(8,128)(2,1)S(1)}, u32[]{:S(2)}, u32[]{:S(2)}) %collective-permute-start.31) | collective-permute-done | bytes 573472 | tf_op jit(solution)/shard_map/ppermute | solution.py:19
  165.3 1.3 fusion.16
  166.6 1.5 collective-permute-start.33
  168.1 18.6 %collective-permute-done.34 = bf16[128,1792]{1,0:T(8,128)(2,1)S(1)} collective-permute-done((bf16[128,1792]{1,0:T(8,128)(2,1)S(1)}, bf16[128,1792]{1,0:T(8,128)(2,1)S(1)}, u32[]{:S(2)}, u32[]{:S(2)}) %collective-permute-start.34) | collective-permute-done | bytes 458784 | tf_op jit(solution)/shard_map/ppermute | solution.py:19
  (79 shorter events, 16.6 us)
Async XLA Ops:
  3.5 17.6 %collective-permute-start = (bf16[128,3712]{1,0:T(8,128)(2,1)S(1)}, bf16[128,3712]{1,0:T(8,128)(2,1)S(1)}, u32[]{:S(2)}, u32[]{:S(2)}) collective-permute-start(bf16[128,3712]{1,0:T(8,128)(2,1)S(1)} %widen.1.refs_1_), channel_id=1, source_target_pairs={{0,1},{1,0},{2,3},{3,2},{4,5},{5,4},{6,7},{7,6},{8,9},{9,8},{10,11... | collective-permute-start | bytes 2850824 | tf_op jit(solution)/shard_map/ppermute | solution.py:19
  3.5 28.9 %collective-permute-start.1 = (bf16[128,3712]{1,0:T(8,128)(2,1)S(1)}, bf16[128,3712]{1,0:T(8,128)(2,1)}, u32[]{:S(2)}, u32[]{:S(2)}) collective-permute-start(bf16[128,3712]{1,0:T(8,128)(2,1)S(1)} %widen.1.refs_1_), channel_id=1, source_target_pairs={{0,4},{1,5},{2,6},{3,7},{4,0},{5,1},{6,2},{7,3},{8,12},{9,13},{10,... | collective-permute-start | bytes 2850824 | tf_op jit(solution)/shard_map/ppermute | solution.py:233
  3.6 28.9 %collective-permute-start.2 = (bf16[128,3712]{1,0:T(8,128)(2,1)S(1)}, bf16[128,3712]{1,0:T(8,128)(2,1)}, u32[]{:S(2)}, u32[]{:S(2)}) collective-permute-start(bf16[128,3712]{1,0:T(8,128)(2,1)S(1)} %widen.1.refs_1_), channel_id=1, source_target_pairs={{4,8},{5,9},{6,10},{7,11},{8,4},{9,5},{10,6},{11,7},{20,24},{21,25... | collective-permute-start | bytes 2850824 | tf_op jit(solution)/shard_map/ppermute | solution.py:233
  8.7 23.8 %collective-permute-start.3 = (bf16[128,3712]{1,0:T(8,128)(2,1)S(1)}, bf16[128,3712]{1,0:T(8,128)(2,1)}, u32[]{:S(2)}, u32[]{:S(2)}) collective-permute-start(bf16[128,3712]{1,0:T(8,128)(2,1)S(1)} %widen.1.refs_1_), channel_id=1, source_target_pairs={{0,2},{1,3},{2,0},{3,1},{4,6},{5,7},{6,4},{7,5},{8,10},{9,11},{10,... | collective-permute-start | bytes 2850824 | tf_op jit(solution)/shard_map/ppermute | solution.py:19
  32.6 7.6 %collective-permute-start.6 = (bf16[128,3712]{1,0:T(8,128)(2,1)}, bf16[128,3712]{1,0:T(8,128)(2,1)S(1)}, u32[]{:S(2)}, u32[]{:S(2)}) collective-permute-start(bf16[128,3712]{1,0:T(8,128)(2,1)} %collective-permute-done.1.refs_2_), channel_id=1, source_target_pairs={{0,1},{1,0},{2,3},{3,2},{4,5},{5,4},{6,7},{7,6},{8,9},{9,8},{10,11... | collective-permute-start | bytes 2850824 | tf_op jit(solution)/shard_map/ppermute | solution.py:19
  33.1 24.5 %collective-permute-start.7 = (bf16[128,3712]{1,0:T(8,128)(2,1)}, bf16[128,3712]{1,0:T(8,128)(2,1)S(1)}, u32[]{:S(2)}, u32[]{:S(2)}) collective-permute-start(bf16[128,3712]{1,0:T(8,128)(2,1)} %collective-permute-done.1.refs_2_), channel_id=1, source_target_pairs={{0,2},{1,3},{2,0},{3,1},{4,6},{5,7},{6,4},{7,5},{8,10},{9,11},{10,... | collective-permute-start | bytes 2850824 | tf_op jit(solution)/shard_map/ppermute | solution.py:19
  33.7 25.1 %collective-permute-start.10 = (bf16[128,3712]{1,0:T(8,128)(2,1)}, bf16[128,3712]{1,0:T(8,128)(2,1)}, u32[]{:S(2)}, u32[]{:S(2)}) collective-permute-start(bf16[128,3712]{1,0:T(8,128)(2,1)} %collective-permute-done.1.refs_2_), channel_id=1, source_target_pairs={{4,8},{5,9},{6,10},{7,11},{8,4},{9,5},{10,6},{11,7},{20,24},{21,25... | collective-permute-start | bytes 2850824 | tf_op jit(solution)/shard_map/ppermute | solution.py:233
  36.0 22.8 %collective-permute-start.9 = (bf16[128,3712]{1,0:T(8,128)(2,1)}, bf16[128,3712]{1,0:T(8,128)(2,1)}, u32[]{:S(2)}, u32[]{:S(2)}) collective-permute-start(bf16[128,3712]{1,0:T(8,128)(2,1)} %collective-permute-done.2), channel_id=1, source_target_pairs={{4,0},{5,1},{6,2},{7,3},{8,12},{9,13},{10,14},{11,15},{20,16},{21,... | collective-permute-start | bytes 2850824 | tf_op jit(solution)/shard_map/ppermute | solution.py:233
  38.7 18.9 %collective-permute-start.8 = (bf16[128,1792]{1,0:T(8,128)(2,1)S(1)}, bf16[128,1792]{1,0:T(8,128)(2,1)S(1)}, u32[]{:S(2)}, u32[]{:S(2)}) collective-permute-start(bf16[128,1792]{1,0:T(8,128)(2,1)S(1)} %fusion.21), channel_id=1, source_target_pairs={{0,16},{16,0},{1,17},{17,1},{2,18},{18,2},{3,19},{19,3},{4,20},{20... | collective-permute-start | bytes 1376264 | tf_op jit(solution)/shard_map/ppermute | solution.py:19
  57.6 8.8 %collective-permute-start.11 = (bf16[2,256,1792]{2,1,0:T(8,128)(2,1)}, bf16[2,256,1792]{2,1,0:T(8,128)(2,1)}, u32[]{:S(2)}, u32[]{:S(2)}) collective-permute-start(bf16[2,256,1792]{2,1,0:T(8,128)(2,1)} %get-tuple-element.63), channel_id=1, source_target_pairs={{0,1},{1,0},{2,3},{3,2},{4,5},{5,4},{6,7},{7,6},{8,9},{9,8},{10,11... | collective-permute-start | bytes 5505032 | tf_op jit(solution)/shard_map/ppermute | solution.py:19
  58.8 10.6 %collective-permute-start.12 = (bf16[128,3712]{1,0:T(8,128)(2,1)S(1)}, bf16[128,3712]{1,0:T(8,128)(2,1)S(1)}, u32[]{:S(2)}, u32[]{:S(2)}) collective-permute-start(bf16[128,3712]{1,0:T(8,128)(2,1)S(1)} %collective-permute-done.7.refs_1_), channel_id=1, source_target_pairs={{0,1},{1,0},{2,3},{3,2},{4,5},{5,4},{6,7},{7,6},{8,9},{9,8},{10,11... | collective-permute-start | bytes 2850824 | tf_op jit(solution)/shard_map/ppermute | solution.py:19
  60.1 9.3 %collective-permute-start.13 = (bf16[128,3712]{1,0:T(8,128)(2,1)S(1)}, bf16[128,3712]{1,0:T(8,128)(2,1)S(1)}, u32[]{:S(2)}, u32[]{:S(2)}) collective-permute-start(bf16[128,3712]{1,0:T(8,128)(2,1)S(1)} %broadcast_select_fusion.1.refs_2_), channel_id=1, source_target_pairs={{0,1},{1,0},{2,3},{3,2},{4,5},{5,4},{6,7},{7,6},{8,9},{9,8},{10,11... | collective-permute-start | bytes 2850824 | tf_op jit(solution)/shard_map/ppermute | solution.py:19
  60.7 25.9 %collective-permute-start.14 = (bf16[128,3712]{1,0:T(8,128)(2,1)S(1)}, bf16[128,3712]{1,0:T(8,128)(2,1)S(1)}, u32[]{:S(2)}, u32[]{:S(2)}) collective-permute-start(bf16[128,3712]{1,0:T(8,128)(2,1)S(1)} %broadcast_select_fusion.1.refs_2_), channel_id=1, source_target_pairs={{0,2},{1,3},{2,0},{3,1},{4,6},{5,7},{6,4},{7,5},{8,10},{9,11},{10,... | collective-permute-start | bytes 2850824 | tf_op jit(solution)/shard_map/ppermute | solution.py:19
  61.9 27.8 %collective-permute-start.16 = (bf16[128,3712]{1,0:T(8,128)(2,1)}, bf16[128,3712]{1,0:T(8,128)(2,1)S(1)}, u32[]{:S(2)}, u32[]{:S(2)}) collective-permute-start(bf16[128,3712]{1,0:T(8,128)(2,1)} %collective-permute-done.10), channel_id=1, source_target_pairs={{4,0},{5,1},{6,2},{7,3},{8,12},{9,13},{10,14},{11,15},{20,16},{21,... | collective-permute-start | bytes 2850824 | tf_op jit(solution)/shard_map/ppermute | solution.py:233
  67.8 21.8 %collective-permute-start.15 = (bf16[256,1792]{1,0:T(8,128)(2,1)S(1)}, bf16[256,1792]{1,0:T(8,128)(2,1)S(1)}, u32[]{:S(2)}, u32[]{:S(2)}) collective-permute-start(bf16[256,1792]{1,0:T(8,128)(2,1)S(1)} %fusion), channel_id=1, source_target_pairs={{0,16},{16,0},{1,17},{17,1},{2,18},{18,2},{3,19},{19,3},{4,20},{20... | collective-permute-start | bytes 2752520 | tf_op jit(solution)/shard_map/ppermute | solution.py:19
  89.7 4.1 %collective-permute-start.21 = (bf16[2,256,1792]{2,1,0:T(8,128)(2,1)S(1)}, bf16[2,256,1792]{2,1,0:T(8,128)(2,1)S(1)}, u32[]{:S(2)}, u32[]{:S(2)}) collective-permute-start(bf16[2,256,1792]{2,1,0:T(8,128)(2,1)S(1)} %get-tuple-element.76), channel_id=1, source_target_pairs={{0,1},{1,0},{2,3},{3,2},{4,5},{5,4},{6,7},{7,6},{8,9},{9,8},{10,11... | collective-permute-start | bytes 5505032 | tf_op jit(solution)/shard_map/ppermute | solution.py:19
  91.0 5.1 %collective-permute-start.18 = (bf16[128,3712]{1,0:T(8,128)(2,1)S(1)}, bf16[128,3712]{1,0:T(8,128)(2,1)S(1)}, u32[]{:S(2)}, u32[]{:S(2)}) collective-permute-start(bf16[128,3712]{1,0:T(8,128)(2,1)S(1)} %broadcast_select_fusion.refs_2_), channel_id=1, source_target_pairs={{0,1},{1,0},{2,3},{3,2},{4,5},{5,4},{6,7},{7,6},{8,9},{9,8},{10,11... | collective-permute-start | bytes 2850824 | tf_op jit(solution)/shard_map/ppermute | solution.py:19
  91.6 23.0 %collective-permute-start.19 = (bf16[128,3712]{1,0:T(8,128)(2,1)S(1)}, bf16[128,3712]{1,0:T(8,128)(2,1)S(1)}, u32[]{:S(2)}, u32[]{:S(2)}) collective-permute-start(bf16[128,3712]{1,0:T(8,128)(2,1)S(1)} %broadcast_select_fusion.refs_2_), channel_id=1, source_target_pairs={{0,2},{1,3},{2,0},{3,1},{4,6},{5,7},{6,4},{7,5},{8,10},{9,11},{10,... | collective-permute-start | bytes 2850824 | tf_op jit(solution)/shard_map/ppermute | solution.py:19
  93.7 19.7 %collective-permute-start.20 = (bf16[128,1792]{1,0:T(8,128)(2,1)S(1)}, bf16[128,1792]{1,0:T(8,128)(2,1)S(1)}, u32[]{:S(2)}, u32[]{:S(2)}) collective-permute-start(bf16[128,1792]{1,0:T(8,128)(2,1)S(1)} %fusion.14), channel_id=1, source_target_pairs={{0,4},{1,5},{2,6},{3,7},{4,0},{5,1},{6,2},{7,3},{8,12},{9,13},{10,... | collective-permute-start | bytes 1376264 | tf_op jit(solution)/shard_map/ppermute | solution.py:19
  94.0 22.8 %collective-permute-start.22 = (bf16[256,1792]{1,0:T(8,128)(2,1)S(1)}, bf16[256,1792]{1,0:T(8,128)(2,1)S(1)}, u32[]{:S(2)}, u32[]{:S(2)}) collective-permute-start(bf16[256,1792]{1,0:T(8,128)(2,1)S(1)} %fusion.1), channel_id=1, source_target_pairs={{0,16},{16,0},{1,17},{17,1},{2,18},{18,2},{3,19},{19,3},{4,20},{20... | collective-permute-start | bytes 2752520 | tf_op jit(solution)/shard_map/ppermute | solution.py:19
  116.9 3.8 %collective-permute-start.25 = (bf16[2,256,1792]{2,1,0:T(8,128)(2,1)S(1)}, bf16[2,256,1792]{2,1,0:T(8,128)(2,1)S(1)}, u32[]{:S(2)}, u32[]{:S(2)}) collective-permute-start(bf16[2,256,1792]{2,1,0:T(8,128)(2,1)S(1)} %get-tuple-element.82), channel_id=1, source_target_pairs={{0,1},{1,0},{2,3},{3,2},{4,5},{5,4},{6,7},{7,6},{8,9},{9,8},{10,11... | collective-permute-start | bytes 5505032 | tf_op jit(solution)/shard_map/ppermute | solution.py:19
  116.9 5.6 %collective-permute-start.23 = (bf16[128,3712]{1,0:T(8,128)(2,1)S(1)}, bf16[128,3712]{1,0:T(8,128)(2,1)S(1)}, u32[]{:S(2)}, u32[]{:S(2)}) collective-permute-start(bf16[128,3712]{1,0:T(8,128)(2,1)S(1)} %collective-permute-done.19.refs_1_), channel_id=1, source_target_pairs={{0,1},{1,0},{2,3},{3,2},{4,5},{5,4},{6,7},{7,6},{8,9},{9,8},{10,11... | collective-permute-start | bytes 2850824 | tf_op jit(solution)/shard_map/ppermute | solution.py:19
  117.7 17.6 %collective-permute-start.24 = (bf16[96,1792]{1,0:T(8,128)(2,1)S(1)}, bf16[96,1792]{1,0:T(8,128)(2,1)S(1)}, u32[]{:S(2)}, u32[]{:S(2)}) collective-permute-start(bf16[96,1792]{1,0:T(8,128)(2,1)S(1)} %slice.144), channel_id=1, source_target_pairs={{0,8},{1,9},{2,10},{3,11},{4,12},{5,13},{6,14},{7,15},{8,0},{9,1},... | collective-permute-start | bytes 1032200 | tf_op jit(solution)/shard_map/ppermute | solution.py:19
  120.9 14.4 %collective-permute-start.26 = (bf16[128,1792]{1,0:T(8,128)(2,1)S(1)}, bf16[128,1792]{1,0:T(8,128)(2,1)S(1)}, u32[]{:S(2)}, u32[]{:S(2)}) collective-permute-start(bf16[128,1792]{1,0:T(8,128)(2,1)S(1)} %get-tuple-element.98), channel_id=1, source_target_pairs={{0,16},{16,0},{1,17},{17,1},{2,18},{18,2},{3,19},{19,3},{4,20},{20... | collective-permute-start | bytes 1376264 | tf_op jit(solution)/shard_map/ppermute | solution.py:19
  135.3 3.8 %collective-permute-start.27 = (bf16[2,128,1792]{2,1,0:T(8,128)(2,1)S(1)}, bf16[2,128,1792]{2,1,0:T(8,128)(2,1)S(1)}, u32[]{:S(2)}, u32[]{:S(2)}) collective-permute-start(bf16[2,128,1792]{2,1,0:T(8,128)(2,1)S(1)} %get-tuple-element.84), channel_id=1, source_target_pairs={{0,1},{1,0},{2,3},{3,2},{4,5},{5,4},{6,7},{7,6},{8,9},{9,8},{10,11... | collective-permute-start | bytes 2752520 | tf_op jit(solution)/shard_map/ppermute | solution.py:19
  135.3 22.3 %collective-permute-start.30 = (bf16[128,1792]{1,0:T(8,128)(2,1)S(1)}, bf16[128,1792]{1,0:T(8,128)(2,1)S(1)}, u32[]{:S(2)}, u32[]{:S(2)}) collective-permute-start(bf16[128,1792]{1,0:T(8,128)(2,1)S(1)} %get-tuple-element.95), channel_id=1, source_target_pairs={{0,4},{1,5},{2,6},{3,7},{4,0},{5,1},{6,2},{7,3},{8,12},{9,13},{10,... | collective-permute-start | bytes 1376264 | tf_op jit(solution)/shard_map/ppermute | solution.py:19
  138.1 26.2 %collective-permute-start.31 = (bf16[160,1792]{1,0:T(8,128)(2,1)S(1)}, bf16[160,1792]{1,0:T(8,128)(2,1)S(1)}, u32[]{:S(2)}, u32[]{:S(2)}) collective-permute-start(bf16[160,1792]{1,0:T(8,128)(2,1)S(1)} %pad_maximum_fusion), channel_id=1, source_target_pairs={{0,8},{1,9},{2,10},{3,11},{4,12},{5,13},{6,14},{7,15},{8,0},{9,1},... | collective-permute-start | bytes 1720328 | tf_op jit(solution)/shard_map/ppermute | solution.py:19
  139.3 25.0 %collective-permute-start.28 = (bf16[128,1792]{1,0:T(8,128)(2,1)S(1)}, bf16[128,1792]{1,0:T(8,128)(2,1)S(1)}, u32[]{:S(2)}, u32[]{:S(2)}) collective-permute-start(bf16[128,1792]{1,0:T(8,128)(2,1)S(1)} %get-tuple-element.100), channel_id=1, source_target_pairs={{0,2},{1,3},{2,0},{3,1},{4,6},{5,7},{6,4},{7,5},{8,10},{9,11},{10,... | collective-permute-start | bytes 1376264 | tf_op jit(solution)/shard_map/ppermute | solution.py:19
  140.8 23.6 %collective-permute-start.29 = (bf16[128,1792]{1,0:T(8,128)(2,1)S(1)}, bf16[128,1792]{1,0:T(8,128)(2,1)S(1)}, u32[]{:S(2)}, u32[]{:S(2)}) collective-permute-start(bf16[128,1792]{1,0:T(8,128)(2,1)S(1)} %get-tuple-element.99), channel_id=1, source_target_pairs={{0,18},{1,19},{2,16},{3,17},{4,22},{5,23},{6,20},{7,21},{8,26},{9,... | collective-permute-start | bytes 1376264 | tf_op jit(solution)/shard_map/ppermute | solution.py:230
  142.3 22.0 %collective-permute-start.32 = (bf16[128,1792]{1,0:T(8,128)(2,1)S(1)}, bf16[128,1792]{1,0:T(8,128)(2,1)S(1)}, u32[]{:S(2)}, u32[]{:S(2)}) collective-permute-start(bf16[128,1792]{1,0:T(8,128)(2,1)S(1)} %get-tuple-element.86), channel_id=1, source_target_pairs={{0,16},{16,0},{1,17},{17,1},{2,18},{18,2},{3,19},{19,3},{4,20},{20... | collective-permute-start | bytes 1376264 | tf_op jit(solution)/shard_map/ppermute | solution.py:19
  164.7 22.0 %collective-permute-start.34 = (bf16[128,1792]{1,0:T(8,128)(2,1)S(1)}, bf16[128,1792]{1,0:T(8,128)(2,1)S(1)}, u32[]{:S(2)}, u32[]{:S(2)}) collective-permute-start(bf16[128,1792]{1,0:T(8,128)(2,1)S(1)} %fusion.10), channel_id=1, source_target_pairs={{0,12},{1,13},{2,14},{3,15},{4,8},{5,9},{6,10},{7,11},{8,4},{9,5},... | collective-permute-start | bytes 1376264 | tf_op jit(solution)/shard_map/ppermute | solution.py:19
  166.6 20.1 %collective-permute-start.33 = (bf16[128,1792]{1,0:T(8,128)(2,1)S(1)}, bf16[128,1792]{1,0:T(8,128)(2,1)S(1)}, u32[]{:S(2)}, u32[]{:S(2)}) collective-permute-start(bf16[128,1792]{1,0:T(8,128)(2,1)S(1)} %fusion.16), channel_id=1, source_target_pairs={{0,2},{1,3},{2,0},{3,1},{4,6},{5,7},{6,4},{7,5},{8,10},{9,11},{10,... | collective-permute-start | bytes 1376264 | tf_op jit(solution)/shard_map/ppermute | solution.py:19
  (10 other events, 55.5 us)

commit v4 on v3

--- a/solution.py
+++ b/solution.py
@@ -274,27 +274,27 @@
         row_own = over_row(wide)
         near = over_planes(wide, ((0, 1), (1, 0), (2, 3), (3, 2)))
         opposite = over_planes(wide, middle)
-        shared_part = shared(tokens)
         kept_0, sent_0 = routed([wide, over_core(wide)])
         kept_0, near, opposite = together(kept_0, near, opposite)
-        kept_0, sent_0, row_own, shared_part = together(kept_0, sent_0, row_own, shared_part)
+        met_0 = over_core(sent_0)
+        kept_0, met_0, row_own = together(kept_0, met_0, row_own)
 
         inputs = [row_own, near, over_core(row_own), over_core(near)]
         row_near = over_row(near)
-        from_outer, from_inner = over_planes(opposite, outward), over_planes(near, middle)
-        met_0 = over_core(sent_0)
-        own = kept_0.astype(f32) + met_0.astype(f32) + shared_part
-        came_0 = over_dp([own[k].astype(bf16) for k in range(1, n_dp)])
+        relay = jnp.where(inner, opposite, wide)
+        next_ = over_planes(relay, ((0, 2), (3, 1), (1, 0), (2, 3)))
+        came_0 = over_dp(to_dp(kept_0, met_0))
+        *inputs, _ = together(*inputs, relay)
         kept_1, sent_1 = routed(inputs)
-        kept_1, sent_1, row_near, *came_0 = together(kept_1, sent_1, row_near, *came_0)
-        kept_1, from_outer, from_inner = together(kept_1, from_outer, from_inner)
-
-        next_ = jnp.where(inner, from_inner, from_outer)
+        kept_1, sent_1, row_near, next_, *came_0 = together(kept_1, sent_1, row_near, next_, *came_0)
+
         inputs = [row_near, next_, over_core(row_near), over_core(next_)]
         row_next = over_row(next_)
-        last = over_planes(from_inner, outward)
         met_1 = over_core(sent_1)
-        came_1 = over_dp(to_dp(kept_1, met_1))
+        sends = to_dp(kept_1, met_1)
+        came_1 = over_dp(sends)
+        relayed, *_ = together(next_, *sends)
+        last = over_planes(relayed, outward)
         kept_2, sent_2 = routed(inputs)
         kept_2, sent_2, row_next, *came_1 = together(kept_2, sent_2, row_next, *came_1)
         kept_2, last = together(kept_2, last)
@@ -303,14 +303,16 @@
         inputs = [row_next, far, over_core(row_next), over_core(far)]
         row_far = over_row(far)
         met_2 = over_core(sent_2)
-        home_1 = exchange(owned(kept_1, met_1, of(came_1, lower), lower).astype(bf16), "expert", 4)
-        came_2 = over_dp(to_dp(kept_2, met_2))
+        sends = to_dp(kept_2, met_2)
+        came_2 = over_dp(sends)
+        total_1, *_ = together(owned(kept_1, met_1, of(came_1, lower), lower).astype(bf16), *sends)
+        home_1 = exchange(total_1, "expert", 4)
         kept_3, sent_3 = routed(inputs)
         kept_3, sent_3, row_far, home_1, *came_2 = together(kept_3, sent_3, row_far, home_1, *came_2)
 
         inputs = [row_far, over_core(row_far)]
         met_3 = over_core(sent_3)
-        cross_1 = exchange(owned(kept_2, met_2, of(came_2, upper), upper).astype(bf16), "expert", 4)
+        cross_1 = owned(kept_2, met_2, of(came_2, upper), upper).astype(bf16)
         total_2 = owned(kept_2, met_2, of(came_2, lower), lower).astype(bf16)
         home_2 = exchange(total_2[:cut], "expert", 8)
         came_3 = over_dp(to_dp(kept_3, met_3, upper))
@@ -318,22 +320,25 @@
         kept_4, sent_4, home_2, *came_3 = together(kept_4, sent_4, home_2, *came_3)
 
         met_4 = over_core(sent_4)
-        sends = [(kept_4[k].astype(f32) + met_4[k].astype(f32)).astype(bf16) for k in range(n_dp)]
+        last_rows = sends = [(kept_4[k].astype(f32) + met_4[k].astype(f32)).astype(bf16) for k in range(n_dp)]
         back_3 = [over_row(sends[0])] + [across_both(send, k) for k, send in enumerate(sends) if k]
         cross_2 = owned(kept_3, met_3, came_3, upper).astype(bf16)
         cross_2 = exchange(jnp.concatenate([cross_2, total_2[cut:]], axis=0), "expert", 8)
-        *sends, _ = together(*to_dp(kept_3, met_3, lower), sends[0])
+        *sends, cross_1, _ = together(*to_dp(kept_3, met_3, lower), cross_1, sends[0])
+        cross_1 = exchange(cross_1, "expert", 4)
         came_far = over_dp(sends)
-        back_3[0], back_3[1], cross_1, cross_2, *came_far = together(*back_3[:2], cross_1, cross_2, *came_far)
-        total_3 = owned(kept_3, met_3, came_far + back_3, lower)
-        home_3 = exchange(total_3.astype(bf16), "expert", 12)
+        rows, *_ = together(tokens, *last_rows)
+        shared_part, cross_1, cross_2, *came = together(shared(rows), cross_1, cross_2, *back_3, *came_far)
+        total_3 = owned(kept_3, met_3, came, lower)
+        total_3 = total_3.astype(bf16)
+        home_3 = exchange(total_3, "expert", 12)
+        *sends, _ = together(*[shared_part[k].astype(bf16) for k in range(1, n_dp)], total_3)
+        came_shared = over_dp(sends)
         cross = cross_1.astype(f32) + cross_2[:count].astype(f32)
         back_0 = over_row((owned(kept_1, met_1, of(came_1, upper), upper) + cross).astype(bf16))
         home_2 = jnp.concatenate([home_2, cross_2[count:]], axis=0)
         homes = [home_1, home_2, home_3]
-        answer = own[0] + back_0.astype(f32)
-        for value in came_0:
-            answer = answer + value.astype(f32)
+        answer = owned(kept_0, met_0, came_0 + came_shared) + shared_part[0] + back_0.astype(f32)
     else:
         totals = []
         for s in range(planes):

time: 188 us -> 183 us (0.973)
  starting transfers between devices: 39.4 us -> 34.6 us
    ppermute x5 -> x4, waiting for transfers between devices: 1 us -> 11.1 us  [over_planes(): lax.ppermute(value, 'expert', [(4 * s + k, 4 * t + k) for s, t in pairs f...]
    ppermute x29 -> x30, waiting for transfers between devices: 48.8 us -> 38.8 us  [exchange(): return lax.ppermute(value, axis, pairs)]
    ppermute x5 -> x4, starting transfers between devices: 14 us -> 7.1 us  [over_planes(): lax.ppermute(value, 'expert', [(4 * s + k, 4 * t + k) for s, t in pairs f...]
    ppermute x29 -> x30, starting transfers between devices: 23.8 us -> 26.3 us  [exchange(): return lax.ppermute(value, axis, pairs)]
  transfers between devices with their start and end apart: 35 -> 35, of which waited for: 10 -> 15; matrix products, arithmetic and copies ran while one was open for 5% -> 4% of each run, Pallas kernels for 45% -> 46%
where the time goes in v4:
time: 183 us; the launch traced here: 182 us
  Pallas kernels  84.6 us (46%)
  waiting for transfers between devices  49.9 us (27%)
  starting transfers between devices  34.6 us (19%)
  other arithmetic  9.1 us (5%)
  local copies, waits for them, and re-layouts  3.25 us (2%)
    pallas_call x6, Pallas kernels, ffn(): pl.pallas_call(body, out_shape=[jax.ShapeDtypeStruct((blocks, count, widt...  83.7 us
    ppermute x30, waiting for transfers between devices, exchange(): return lax.ppermute(value, axis, pairs)  38.8 us
    ppermute x30, starting transfers between devices, exchange(): return lax.ppermute(value, axis, pairs)  26.3 us
    ppermute x4, waiting for transfers between devices, over_planes(): lax.ppermute(value, 'expert', [(4 * s + k, 4 * t + k) for s, t in pairs f...  11.1 us
    ppermute x4, starting transfers between devices, over_planes(): lax.ppermute(value, 'expert', [(4 * s + k, 4 * t + k) for s, t in pairs f...  7.1 us
  transfers between devices with their start and end apart: 35, of which 15 were waited for; matrix products, arithmetic and copies ran while one was open for 4% of the time, Pallas kernels for 46%

profile of v4, /device:TPU:8, one launch (start us, length us, event | category | flops | bytes accessed | tf_op | source)
XLA Modules:
  0.0 182.4 jit_solution(11203252202532640278)
XLA Ops:
  3.6 5.0 %collective-permute-start.2 = (bf16[128,3712]{1,0:T(8,128)(2,1)S(1)}, bf16[128,3712]{1,0:T(8,128)(2,1)}, u32[]{:S(2)}, u32[]{:S(2)}) collective-permute-start(bf16[128,3712]{1,0:T(8,128)(2,1)S(1)} %widen.1.refs_1_), channel_id=1, source_target_pairs={{4,8},{5,9},{6,10},{7,11},{8,4},{9,5},{10,6},{11,7},{20,24},{21,25... | collective-permute-start | bytes 2850824 | tf_op jit(solution)/shard_map/ppermute | solution.py:233
  8.7 1.6 collective-permute-start.4
  11.6 11.5 %routed_expert.5 = (bf16[2,128,1792]{2,1,0:T(8,128)(2,1)S(1)}, bf16[2,128,1792]{2,1,0:T(8,128)(2,1)}) custom-call(s32[2]{0:T(128)S(1)} %pad_add_fusion.refs_0_, bf16[128,3712]{1,0:T(8,128)(2,1)S(1)} %widen.1.refs_1_, bf16[128,3712]{1,0:T(8,128)(2,1)S(1)} %collective-permute-done.refs_2_, bf16[3584,1024]{1,0:T(8,128)(2,1)} %bitcast.74, ...), custom_call_target="tpu_custom_call" | custom-call | flops 5637144576 | bytes 25690112 | tf_op jit(solution)/shard_map/routed_expert/pallas_call | solution.py:179
  23.2 3.9 %collective-permute-done.1.refs_2_ = bf16[128,3712]{1,0:T(8,128)(2,1)} collective-permute-done((bf16[128,3712]{1,0:T(8,128)(2,1)S(1)}, bf16[128,3712]{1,0:T(8,128)(2,1)}, u32[]{:S(2)}, u32[]{:S(2)}) %collective-permute-start.1) | collective-permute-done | bytes 950304 | tf_op jit(solution)/shard_map/ppermute | solution.py:233
  27.1 3.0 %collective-permute-done.2 = bf16[128,3712]{1,0:T(8,128)(2,1)} collective-permute-done((bf16[128,3712]{1,0:T(8,128)(2,1)S(1)}, bf16[128,3712]{1,0:T(8,128)(2,1)}, u32[]{:S(2)}, u32[]{:S(2)}) %collective-permute-start.2) | collective-permute-done | bytes 950304 | tf_op jit(solution)/shard_map/ppermute | solution.py:233
  30.1 1.5 collective-permute-start.7
  31.9 1.3 broadcast_select_fusion.1
  34.4 1.6 collective-permute-start.9
  35.9 16.9 %routed_expert.6 = (bf16[2,256,1792]{2,1,0:T(8,128)(2,1)S(1)}, bf16[2,256,1792]{2,1,0:T(8,128)(2,1)S(1)}) custom-call(s32[2]{0:T(128)S(1)} %pad_add_fusion.refs_0_, bf16[128,3712]{1,0:T(8,128)(2,1)} %collective-permute-done.4.refs_1_, bf16[128,3712]{1,0:T(8,128)(2,1)} %collective-permute-done.1.refs_2_, ...), custom_call_target="tpu_custom_call" | custom-call | flops 11274289152 | bytes 29360128 | tf_op jit(solution)/shard_map/routed_expert/pallas_call | solution.py:179
  53.8 3.6 %collective-permute-done.8.refs_2_ = bf16[128,3712]{1,0:T(8,128)(2,1)S(1)} collective-permute-done((bf16[128,3712]{1,0:T(8,128)(2,1)S(1)}, bf16[128,3712]{1,0:T(8,128)(2,1)S(1)}, u32[]{:S(2)}, u32[]{:S(2)}) %collective-permute-start.8) | collective-permute-done | bytes 950304 | tf_op jit(solution)/shard_map/ppermute | solution.py:233
  57.9 1.5 collective-permute-start.12
  59.4 1.8 collective-permute-done.13
  61.4 1.6 collective-permute-start.14
  63.0 1.9 %collective-permute-start.15 = (bf16[128,3712]{1,0:T(8,128)(2,1)S(1)}, bf16[128,3712]{1,0:T(8,128)(2,1)S(1)}, u32[]{:S(2)}, u32[]{:S(2)}) collective-permute-start(bf16[128,3712]{1,0:T(8,128)(2,1)S(1)} %collective-permute-done.8.refs_2_), channel_id=1, source_target_pairs={{4,0},{5,1},{6,2},{7,3},{8,12},{9,13},{10,14},{11,15},{20,16},{21,... | collective-permute-start | bytes 2850824 | tf_op jit(solution)/shard_map/ppermute | solution.py:233
  64.9 17.2 %routed_expert.7 = (bf16[2,256,1792]{2,1,0:T(8,128)(2,1)S(1)}, bf16[2,256,1792]{2,1,0:T(8,128)(2,1)S(1)}) custom-call(s32[2]{0:T(128)S(1)} %pad_add_fusion.refs_0_, bf16[128,3712]{1,0:T(8,128)(2,1)S(1)} %collective-permute-done.7.refs_1_, bf16[128,3712]{1,0:T(8,128)(2,1)S(1)} %collective-permute-done.8.refs_2_, ...), custom_call_target="tpu_custom_call" | custom-call | flops 11274289152 | bytes 29360128 | tf_op jit(solution)/shard_map/routed_expert/pallas_call | solution.py:179
  82.2 1.7 collective-permute-done.14
  85.0 1.4 broadcast_select_fusion.refs_2_
  86.6 1.4 collective-permute-start.18
  90.4 17.2 %routed_expert.8 = (bf16[2,256,1792]{2,1,0:T(8,128)(2,1)S(1)}, bf16[2,256,1792]{2,1,0:T(8,128)(2,1)S(1)}) custom-call(s32[2]{0:T(128)S(1)} %pad_add_fusion.refs_0_, bf16[128,3712]{1,0:T(8,128)(2,1)S(1)} %collective-permute-done.12.refs_1_, bf16[128,3712]{1,0:T(8,128)(2,1)S(1)} %broadcast_select_fusion.refs_2_, ...), custom_call_target="tpu_custom_call" | custom-call | flops 11274289152 | bytes 29360128 | tf_op jit(solution)/shard_map/routed_expert/pallas_call | solution.py:179
  107.6 2.5 %collective-permute-done.18.refs_1_ = bf16[128,3712]{1,0:T(8,128)(2,1)S(1)} collective-permute-done((bf16[128,3712]{1,0:T(8,128)(2,1)S(1)}, bf16[128,3712]{1,0:T(8,128)(2,1)S(1)}, u32[]{:S(2)}, u32[]{:S(2)}) %collective-permute-start.18) | collective-permute-done | bytes 950304 | tf_op jit(solution)/shard_map/ppermute | solution.py:19
  112.4 1.7 collective-permute-start.23
  115.9 11.3 %routed_expert.9 = (bf16[2,128,1792]{2,1,0:T(8,128)(2,1)S(1)}, bf16[2,128,1792]{2,1,0:T(8,128)(2,1)S(1)}) custom-call(s32[2]{0:T(128)S(1)} %pad_add_fusion.refs_0_, bf16[128,3712]{1,0:T(8,128)(2,1)S(1)} %collective-permute-done.18.refs_1_, bf16[128,3712]{1,0:T(8,128)(2,1)S(1)} %collective-permute-done.22.refs_2_, bf16[3584,1024]{1,0:T(8,128)(2,1)} %bitcast.78, ...), custom_call_target="tpu_custom_call" | custom-call | flops 5637144576 | bytes 25690112 | tf_op jit(solution)/shard_map/routed_expert/pallas_call | solution.py:179
  127.3 1.8 collective-permute-done.23
  129.3 3.4 %collective-permute-start.28 = (bf16[160,1792]{1,0:T(8,128)(2,1)S(1)}, bf16[160,1792]{1,0:T(8,128)(2,1)S(1)}, u32[]{:S(2)}, u32[]{:S(2)}) collective-permute-start(bf16[160,1792]{1,0:T(8,128)(2,1)S(1)} %pad_maximum_fusion), channel_id=1, source_target_pairs={{0,8},{1,9},{2,10},{3,11},{4,12},{5,13},{6,14},{7,15},{8,0},{9,1},... | collective-permute-start | bytes 1720328 | tf_op jit(solution)/shard_map/ppermute | solution.py:19
  133.0 1.3 collective-permute-start.29
  134.3 1.2 collective-permute-start.27
  136.8 1.5 collective-permute-start.31
  138.3 9.5 %shared_expert.1 = f32[2,128,1792]{2,1,0:T(8,128)S(1)} custom-call(s32[2]{0:T(128)S(1)} %pad_add_fusion.refs_0_, bf16[128,3584]{1,0:T(8,128)(2,1)S(1)} %copy-done.1, bf16[3584,1024]{1,0:T(8,128)(2,1)} %refs_2_.1, bf16[3584,1024]{1,0:T(8,128)(2,1)} %refs_3_.1, bf16[1024,3584]{1,0:T(8,128)(2,1)} %refs_4_.1), custom_call_target="tpu_custom_call" | custom-call | flops 2818572288 | bytes 23855104 | tf_op jit(solution)/shard_map/shared_expert/pallas_call | solution.py:179
  147.8 9.5 %collective-permute-done.28 = bf16[160,1792]{1,0:T(8,128)(2,1)S(1)} collective-permute-done((bf16[160,1792]{1,0:T(8,128)(2,1)S(1)}, bf16[160,1792]{1,0:T(8,128)(2,1)S(1)}, u32[]{:S(2)}, u32[]{:S(2)}) %collective-permute-start.28) | collective-permute-done | bytes 573472 | tf_op jit(solution)/shard_map/ppermute | solution.py:19
  159.7 1.3 collective-permute-start.33
  161.7 18.3 %collective-permute-done.34 = bf16[128,1792]{1,0:T(8,128)(2,1)S(1)} collective-permute-done((bf16[128,1792]{1,0:T(8,128)(2,1)S(1)}, bf16[128,1792]{1,0:T(8,128)(2,1)S(1)}, u32[]{:S(2)}, u32[]{:S(2)}) %collective-permute-start.34) | collective-permute-done | bytes 458784 | tf_op jit(solution)/shard_map/ppermute | solution.py:19
  180.0 2.3 %fusion.8 = bf16[128,1792]{1,0:T(8,128)(2,1)} fusion(bf16[128,1792]{1,0:T(8,128)(2,1)S(1)} %collective-permute-done.34, bf16[128,1792]{1,0:T(8,128)(2,1)S(1)} %collective-permute-done.20, bf16[128,1792]{1,0:T(8,128)(2,1)S(1)} %collective-permute-done.33, f32[2,128,1792]{2,1,0:T(8,128)S(1)} %shared_expert.1, ...), kind=kLoop, calls=%fused_computation.15 | loop fusion | flops 4587520 | bytes 5046272 | tf_op jit(solution)/shard_map/convert_element_type | solution.py:358
  (77 shorter events, 20.0 us)
Async XLA Ops:
  3.5 8.1 %collective-permute-start = (bf16[128,3712]{1,0:T(8,128)(2,1)S(1)}, bf16[128,3712]{1,0:T(8,128)(2,1)S(1)}, u32[]{:S(2)}, u32[]{:S(2)}) collective-permute-start(bf16[128,3712]{1,0:T(8,128)(2,1)S(1)} %widen.1.refs_1_), channel_id=1, source_target_pairs={{0,1},{1,0},{2,3},{3,2},{4,5},{5,4},{6,7},{7,6},{8,9},{9,8},{10,11... | collective-permute-start | bytes 2850824 | tf_op jit(solution)/shard_map/ppermute | solution.py:19
  3.5 23.6 %collective-permute-start.1 = (bf16[128,3712]{1,0:T(8,128)(2,1)S(1)}, bf16[128,3712]{1,0:T(8,128)(2,1)}, u32[]{:S(2)}, u32[]{:S(2)}) collective-permute-start(bf16[128,3712]{1,0:T(8,128)(2,1)S(1)} %widen.1.refs_1_), channel_id=1, source_target_pairs={{0,4},{1,5},{2,6},{3,7},{4,0},{5,1},{6,2},{7,3},{8,12},{9,13},{10,... | collective-permute-start | bytes 2850824 | tf_op jit(solution)/shard_map/ppermute | solution.py:233
  3.6 26.5 %collective-permute-start.2 = (bf16[128,3712]{1,0:T(8,128)(2,1)S(1)}, bf16[128,3712]{1,0:T(8,128)(2,1)}, u32[]{:S(2)}, u32[]{:S(2)}) collective-permute-start(bf16[128,3712]{1,0:T(8,128)(2,1)S(1)} %widen.1.refs_1_), channel_id=1, source_target_pairs={{4,8},{5,9},{6,10},{7,11},{8,4},{9,5},{10,6},{11,7},{20,24},{21,25... | collective-permute-start | bytes 2850824 | tf_op jit(solution)/shard_map/ppermute | solution.py:233
  8.7 23.0 %collective-permute-start.4 = (bf16[128,3712]{1,0:T(8,128)(2,1)S(1)}, bf16[128,3712]{1,0:T(8,128)(2,1)}, u32[]{:S(2)}, u32[]{:S(2)}) collective-permute-start(bf16[128,3712]{1,0:T(8,128)(2,1)S(1)} %widen.1.refs_1_), channel_id=1, source_target_pairs={{0,2},{1,3},{2,0},{3,1},{4,6},{5,7},{6,4},{7,5},{8,10},{9,11},{10,... | collective-permute-start | bytes 2850824 | tf_op jit(solution)/shard_map/ppermute | solution.py:19
  23.1 8.5 %collective-permute-start.3 = (bf16[2,128,1792]{2,1,0:T(8,128)(2,1)}, bf16[2,128,1792]{2,1,0:T(8,128)(2,1)}, u32[]{:S(2)}, u32[]{:S(2)}) collective-permute-start(bf16[2,128,1792]{2,1,0:T(8,128)(2,1)} %get-tuple-element.59), channel_id=1, source_target_pairs={{0,1},{1,0},{2,3},{3,2},{4,5},{5,4},{6,7},{7,6},{8,9},{9,8},{10,11... | collective-permute-start | bytes 2752520 | tf_op jit(solution)/shard_map/ppermute | solution.py:19
  30.1 5.8 %collective-permute-start.6 = (bf16[128,3712]{1,0:T(8,128)(2,1)}, bf16[128,3712]{1,0:T(8,128)(2,1)S(1)}, u32[]{:S(2)}, u32[]{:S(2)}) collective-permute-start(bf16[128,3712]{1,0:T(8,128)(2,1)} %collective-permute-done.1.refs_2_), channel_id=1, source_target_pairs={{0,1},{1,0},{2,3},{3,2},{4,5},{5,4},{6,7},{7,6},{8,9},{9,8},{10,11... | collective-permute-start | bytes 2850824 | tf_op jit(solution)/shard_map/ppermute | solution.py:19
  30.1 23.7 %collective-permute-start.7 = (bf16[128,3712]{1,0:T(8,128)(2,1)}, bf16[128,3712]{1,0:T(8,128)(2,1)S(1)}, u32[]{:S(2)}, u32[]{:S(2)}) collective-permute-start(bf16[128,3712]{1,0:T(8,128)(2,1)} %collective-permute-done.1.refs_2_), channel_id=1, source_target_pairs={{0,2},{1,3},{2,0},{3,1},{4,6},{5,7},{6,4},{7,5},{8,10},{9,11},{10,... | collective-permute-start | bytes 2850824 | tf_op jit(solution)/shard_map/ppermute | solution.py:19
  31.7 4.3 %collective-permute-start.5 = (bf16[128,3712]{1,0:T(8,128)(2,1)}, bf16[128,3712]{1,0:T(8,128)(2,1)S(1)}, u32[]{:S(2)}, u32[]{:S(2)}) collective-permute-start(bf16[128,3712]{1,0:T(8,128)(2,1)} %collective-permute-done.4.refs_1_), channel_id=1, source_target_pairs={{0,1},{1,0},{2,3},{3,2},{4,5},{5,4},{6,7},{7,6},{8,9},{9,8},{10,11... | collective-permute-start | bytes 2850824 | tf_op jit(solution)/shard_map/ppermute | solution.py:19
  33.2 24.2 %collective-permute-start.8 = (bf16[128,3712]{1,0:T(8,128)(2,1)S(1)}, bf16[128,3712]{1,0:T(8,128)(2,1)S(1)}, u32[]{:S(2)}, u32[]{:S(2)}) collective-permute-start(bf16[128,3712]{1,0:T(8,128)(2,1)S(1)} %broadcast_select_fusion.1), channel_id=1, source_target_pairs={{0,8},{1,9},{2,10},{3,11},{12,4},{13,5},{14,6},{15,7},{4,0},{5,1},... | collective-permute-start | bytes 2850824 | tf_op jit(solution)/shard_map/ppermute | solution.py:233
  34.4 23.0 %collective-permute-start.9 = (bf16[128,1792]{1,0:T(8,128)(2,1)S(1)}, bf16[128,1792]{1,0:T(8,128)(2,1)S(1)}, u32[]{:S(2)}, u32[]{:S(2)}) collective-permute-start(bf16[128,1792]{1,0:T(8,128)(2,1)S(1)} %fusion.17), channel_id=1, source_target_pairs={{0,16},{16,0},{1,17},{17,1},{2,18},{18,2},{3,19},{19,3},{4,20},{20... | collective-permute-start | bytes 1376264 | tf_op jit(solution)/shard_map/ppermute | solution.py:19
  57.4 7.5 %collective-permute-start.10 = (bf16[128,3712]{1,0:T(8,128)(2,1)S(1)}, bf16[128,3712]{1,0:T(8,128)(2,1)S(1)}, u32[]{:S(2)}, u32[]{:S(2)}) collective-permute-start(bf16[128,3712]{1,0:T(8,128)(2,1)S(1)} %collective-permute-done.7.refs_1_), channel_id=1, source_target_pairs={{0,1},{1,0},{2,3},{3,2},{4,5},{5,4},{6,7},{7,6},{8,9},{9,8},{10,11... | collective-permute-start | bytes 2850824 | tf_op jit(solution)/shard_map/ppermute | solution.py:19
  57.9 7.0 %collective-permute-start.11 = (bf16[128,3712]{1,0:T(8,128)(2,1)S(1)}, bf16[128,3712]{1,0:T(8,128)(2,1)S(1)}, u32[]{:S(2)}, u32[]{:S(2)}) collective-permute-start(bf16[128,3712]{1,0:T(8,128)(2,1)S(1)} %collective-permute-done.8.refs_2_), channel_id=1, source_target_pairs={{0,1},{1,0},{2,3},{3,2},{4,5},{5,4},{6,7},{7,6},{8,9},{9,8},{10,11... | collective-permute-start | bytes 2850824 | tf_op jit(solution)/shard_map/ppermute | solution.py:19
  57.9 24.2 %collective-permute-start.12 = (bf16[128,3712]{1,0:T(8,128)(2,1)S(1)}, bf16[128,3712]{1,0:T(8,128)(2,1)S(1)}, u32[]{:S(2)}, u32[]{:S(2)}) collective-permute-start(bf16[128,3712]{1,0:T(8,128)(2,1)S(1)} %collective-permute-done.8.refs_2_), channel_id=1, source_target_pairs={{0,2},{1,3},{2,0},{3,1},{4,6},{5,7},{6,4},{7,5},{8,10},{9,11},{10,... | collective-permute-start | bytes 2850824 | tf_op jit(solution)/shard_map/ppermute | solution.py:19
  61.4 22.5 %collective-permute-start.14 = (bf16[256,1792]{1,0:T(8,128)(2,1)S(1)}, bf16[256,1792]{1,0:T(8,128)(2,1)S(1)}, u32[]{:S(2)}, u32[]{:S(2)}) collective-permute-start(bf16[256,1792]{1,0:T(8,128)(2,1)S(1)} %fusion), channel_id=1, source_target_pairs={{0,16},{16,0},{1,17},{17,1},{2,18},{18,2},{3,19},{19,3},{4,20},{20... | collective-permute-start | bytes 2752520 | tf_op jit(solution)/shard_map/ppermute | solution.py:19
  63.0 22.0 %collective-permute-start.15 = (bf16[128,3712]{1,0:T(8,128)(2,1)S(1)}, bf16[128,3712]{1,0:T(8,128)(2,1)S(1)}, u32[]{:S(2)}, u32[]{:S(2)}) collective-permute-start(bf16[128,3712]{1,0:T(8,128)(2,1)S(1)} %collective-permute-done.8.refs_2_), channel_id=1, source_target_pairs={{4,0},{5,1},{6,2},{7,3},{8,12},{9,13},{10,14},{11,15},{20,16},{21,... | collective-permute-start | bytes 2850824 | tf_op jit(solution)/shard_map/ppermute | solution.py:233
  83.9 4.2 %collective-permute-start.19 = (bf16[2,256,1792]{2,1,0:T(8,128)(2,1)S(1)}, bf16[2,256,1792]{2,1,0:T(8,128)(2,1)S(1)}, u32[]{:S(2)}, u32[]{:S(2)}) collective-permute-start(bf16[2,256,1792]{2,1,0:T(8,128)(2,1)S(1)} %get-tuple-element.86), channel_id=1, source_target_pairs={{0,1},{1,0},{2,3},{3,2},{4,5},{5,4},{6,7},{7,6},{8,9},{9,8},{10,11... | collective-permute-start | bytes 5505032 | tf_op jit(solution)/shard_map/ppermute | solution.py:19
  83.9 6.3 %collective-permute-start.16 = (bf16[128,3712]{1,0:T(8,128)(2,1)S(1)}, bf16[128,3712]{1,0:T(8,128)(2,1)S(1)}, u32[]{:S(2)}, u32[]{:S(2)}) collective-permute-start(bf16[128,3712]{1,0:T(8,128)(2,1)S(1)} %collective-permute-done.12.refs_1_), channel_id=1, source_target_pairs={{0,1},{1,0},{2,3},{3,2},{4,5},{5,4},{6,7},{7,6},{8,9},{9,8},{10,11... | collective-permute-start | bytes 2850824 | tf_op jit(solution)/shard_map/ppermute | solution.py:19
  86.3 4.0 %collective-permute-start.17 = (bf16[128,3712]{1,0:T(8,128)(2,1)S(1)}, bf16[128,3712]{1,0:T(8,128)(2,1)S(1)}, u32[]{:S(2)}, u32[]{:S(2)}) collective-permute-start(bf16[128,3712]{1,0:T(8,128)(2,1)S(1)} %broadcast_select_fusion.refs_2_), channel_id=1, source_target_pairs={{0,1},{1,0},{2,3},{3,2},{4,5},{5,4},{6,7},{7,6},{8,9},{9,8},{10,11... | collective-permute-start | bytes 2850824 | tf_op jit(solution)/shard_map/ppermute | solution.py:19
  86.6 23.5 %collective-permute-start.18 = (bf16[128,3712]{1,0:T(8,128)(2,1)S(1)}, bf16[128,3712]{1,0:T(8,128)(2,1)S(1)}, u32[]{:S(2)}, u32[]{:S(2)}) collective-permute-start(bf16[128,3712]{1,0:T(8,128)(2,1)S(1)} %broadcast_select_fusion.refs_2_), channel_id=1, source_target_pairs={{0,2},{1,3},{2,0},{3,1},{4,6},{5,7},{6,4},{7,5},{8,10},{9,11},{10,... | collective-permute-start | bytes 2850824 | tf_op jit(solution)/shard_map/ppermute | solution.py:19
  88.3 22.5 %collective-permute-start.21 = (bf16[256,1792]{1,0:T(8,128)(2,1)S(1)}, bf16[256,1792]{1,0:T(8,128)(2,1)S(1)}, u32[]{:S(2)}, u32[]{:S(2)}) collective-permute-start(bf16[256,1792]{1,0:T(8,128)(2,1)S(1)} %fusion.1), channel_id=1, source_target_pairs={{0,16},{16,0},{1,17},{17,1},{2,18},{18,2},{3,19},{19,3},{4,20},{20... | collective-permute-start | bytes 2752520 | tf_op jit(solution)/shard_map/ppermute | solution.py:19
  89.4 20.7 %collective-permute-start.20 = (bf16[128,1792]{1,0:T(8,128)(2,1)S(1)}, bf16[128,1792]{1,0:T(8,128)(2,1)S(1)}, u32[]{:S(2)}, u32[]{:S(2)}) collective-permute-start(bf16[128,1792]{1,0:T(8,128)(2,1)S(1)} %fusion.15), channel_id=1, source_target_pairs={{0,4},{1,5},{2,6},{3,7},{4,0},{5,1},{6,2},{7,3},{8,12},{9,13},{10,... | collective-permute-start | bytes 1376264 | tf_op jit(solution)/shard_map/ppermute | solution.py:19
  110.8 5.1 %collective-permute-start.22 = (bf16[128,3712]{1,0:T(8,128)(2,1)S(1)}, bf16[128,3712]{1,0:T(8,128)(2,1)S(1)}, u32[]{:S(2)}, u32[]{:S(2)}) collective-permute-start(bf16[128,3712]{1,0:T(8,128)(2,1)S(1)} %collective-permute-done.18.refs_1_), channel_id=1, source_target_pairs={{0,1},{1,0},{2,3},{3,2},{4,5},{5,4},{6,7},{7,6},{8,9},{9,8},{10,11... | collective-permute-start | bytes 2850824 | tf_op jit(solution)/shard_map/ppermute | solution.py:19
  112.4 16.6 %collective-permute-start.23 = (bf16[96,1792]{1,0:T(8,128)(2,1)S(1)}, bf16[96,1792]{1,0:T(8,128)(2,1)S(1)}, u32[]{:S(2)}, u32[]{:S(2)}) collective-permute-start(bf16[96,1792]{1,0:T(8,128)(2,1)S(1)} %slice.157), channel_id=1, source_target_pairs={{0,8},{1,9},{2,10},{3,11},{4,12},{5,13},{6,14},{7,15},{8,0},{9,1},... | collective-permute-start | bytes 1032200 | tf_op jit(solution)/shard_map/ppermute | solution.py:19
  114.8 14.3 %collective-permute-start.25 = (bf16[128,1792]{1,0:T(8,128)(2,1)S(1)}, bf16[128,1792]{1,0:T(8,128)(2,1)S(1)}, u32[]{:S(2)}, u32[]{:S(2)}) collective-permute-start(bf16[128,1792]{1,0:T(8,128)(2,1)S(1)} %get-tuple-element.112), channel_id=1, source_target_pairs={{0,16},{16,0},{1,17},{17,1},{2,18},{18,2},{3,19},{19,3},{4,20},{20... | collective-permute-start | bytes 1376264 | tf_op jit(solution)/shard_map/ppermute | solution.py:19
  129.3 28.0 %collective-permute-start.28 = (bf16[160,1792]{1,0:T(8,128)(2,1)S(1)}, bf16[160,1792]{1,0:T(8,128)(2,1)S(1)}, u32[]{:S(2)}, u32[]{:S(2)}) collective-permute-start(bf16[160,1792]{1,0:T(8,128)(2,1)S(1)} %pad_maximum_fusion), channel_id=1, source_target_pairs={{0,8},{1,9},{2,10},{3,11},{4,12},{5,13},{6,14},{7,15},{8,0},{9,1},... | collective-permute-start | bytes 1720328 | tf_op jit(solution)/shard_map/ppermute | solution.py:19
  133.0 24.4 %collective-permute-start.29 = (bf16[128,1792]{1,0:T(8,128)(2,1)S(1)}, bf16[128,1792]{1,0:T(8,128)(2,1)S(1)}, u32[]{:S(2)}, u32[]{:S(2)}) collective-permute-start(bf16[128,1792]{1,0:T(8,128)(2,1)S(1)} %get-tuple-element.114), channel_id=1, source_target_pairs={{0,2},{1,3},{2,0},{3,1},{4,6},{5,7},{6,4},{7,5},{8,10},{9,11},{10,... | collective-permute-start | bytes 1376264 | tf_op jit(solution)/shard_map/ppermute | solution.py:19
  134.3 23.0 %collective-permute-start.27 = (bf16[128,1792]{1,0:T(8,128)(2,1)S(1)}, bf16[128,1792]{1,0:T(8,128)(2,1)S(1)}, u32[]{:S(2)}, u32[]{:S(2)}) collective-permute-start(bf16[128,1792]{1,0:T(8,128)(2,1)S(1)} %copy-done.4), channel_id=1, source_target_pairs={{0,4},{1,5},{2,6},{3,7},{4,0},{5,1},{6,2},{7,3},{8,12},{9,13},{10,... | collective-permute-start | bytes 1376264 | tf_op jit(solution)/shard_map/ppermute | solution.py:19
  135.6 21.8 %collective-permute-start.30 = (bf16[128,1792]{1,0:T(8,128)(2,1)S(1)}, bf16[128,1792]{1,0:T(8,128)(2,1)S(1)}, u32[]{:S(2)}, u32[]{:S(2)}) collective-permute-start(bf16[128,1792]{1,0:T(8,128)(2,1)S(1)} %get-tuple-element.113), channel_id=1, source_target_pairs={{0,18},{1,19},{2,16},{3,17},{4,22},{5,23},{6,20},{7,21},{8,26},{9,... | collective-permute-start | bytes 1376264 | tf_op jit(solution)/shard_map/ppermute | solution.py:230
  136.8 21.3 %collective-permute-start.31 = (bf16[128,1792]{1,0:T(8,128)(2,1)S(1)}, bf16[128,1792]{1,0:T(8,128)(2,1)S(1)}, u32[]{:S(2)}, u32[]{:S(2)}) collective-permute-start(bf16[128,1792]{1,0:T(8,128)(2,1)S(1)} %get-tuple-element.99), channel_id=1, source_target_pairs={{0,16},{16,0},{1,17},{17,1},{2,18},{18,2},{3,19},{19,3},{4,20},{20... | collective-permute-start | bytes 1376264 | tf_op jit(solution)/shard_map/ppermute | solution.py:19
  158.4 21.6 %collective-permute-start.34 = (bf16[128,1792]{1,0:T(8,128)(2,1)S(1)}, bf16[128,1792]{1,0:T(8,128)(2,1)S(1)}, u32[]{:S(2)}, u32[]{:S(2)}) collective-permute-start(bf16[128,1792]{1,0:T(8,128)(2,1)S(1)} %fusion.11), channel_id=1, source_target_pairs={{0,12},{1,13},{2,14},{3,15},{4,8},{5,9},{6,10},{7,11},{8,4},{9,5},... | collective-permute-start | bytes 1376264 | tf_op jit(solution)/shard_map/ppermute | solution.py:19
  159.7 20.3 %collective-permute-start.33 = (bf16[128,1792]{1,0:T(8,128)(2,1)S(1)}, bf16[128,1792]{1,0:T(8,128)(2,1)S(1)}, u32[]{:S(2)}, u32[]{:S(2)}) collective-permute-start(bf16[128,1792]{1,0:T(8,128)(2,1)S(1)} %fusion.3), channel_id=1, source_target_pairs={{0,2},{1,3},{2,0},{3,1},{4,6},{5,7},{6,4},{7,5},{8,10},{9,11},{10,... | collective-permute-start | bytes 1376264 | tf_op jit(solution)/shard_map/ppermute | solution.py:19
  161.1 18.9 %collective-permute-start.32 = (bf16[128,1792]{1,0:T(8,128)(2,1)S(1)}, bf16[128,1792]{1,0:T(8,128)(2,1)S(1)}, u32[]{:S(2)}, u32[]{:S(2)}) collective-permute-start(bf16[128,1792]{1,0:T(8,128)(2,1)S(1)} %fusion.22), channel_id=1, source_target_pairs={{0,16},{16,0},{1,17},{17,1},{2,18},{18,2},{3,19},{19,3},{4,20},{20... | collective-permute-start | bytes 1376264 | tf_op jit(solution)/shard_map/ppermute | solution.py:19
  (9 other events, 38.2 us)

commit v5 on v4

--- a/solution.py
+++ b/solution.py
@@ -47,7 +47,7 @@
         out_specs=pl.BlockSpec((count, width + LANES), lambda i: (0, 0)),
         compiler_params=pltpu.CompilerParams(vmem_limit_bytes=16 * 1024 * 1024),
         name="widen",
-    )(tokens, ids.T, weight.T)
+    )(*[pltpu.with_memory_space_constraint(array, pltpu.HBM) for array in (tokens, ids.T, weight.T)])
 
 
 def ffn_body(experts, blocks, out_rows, scaled, n_in, n_out, *refs):
@@ -324,11 +324,13 @@
         back_3 = [over_row(sends[0])] + [across_both(send, k) for k, send in enumerate(sends) if k]
         cross_2 = owned(kept_3, met_3, came_3, upper).astype(bf16)
         cross_2 = exchange(jnp.concatenate([cross_2, total_2[cut:]], axis=0), "expert", 8)
-        *sends, cross_1, _ = together(*to_dp(kept_3, met_3, lower), cross_1, sends[0])
+        cross_1, _ = together(cross_1, sends[0])
+        sends = to_dp(kept_3, met_3, lower)
         cross_1 = exchange(cross_1, "expert", 4)
         came_far = over_dp(sends)
         rows, *_ = together(tokens, *last_rows)
-        shared_part, cross_1, cross_2, *came = together(shared(rows), cross_1, cross_2, *back_3, *came_far)
+        early = owned(kept_0, met_0, came_0) + home_1.astype(f32)
+        early, shared_part, cross_1, cross_2, *came = together(early, shared(rows), cross_1, cross_2, *back_3, *came_far)
         total_3 = owned(kept_3, met_3, came, lower)
         total_3 = total_3.astype(bf16)
         home_3 = exchange(total_3, "expert", 12)
@@ -337,8 +339,10 @@
         cross = cross_1.astype(f32) + cross_2[:count].astype(f32)
         back_0 = over_row((owned(kept_1, met_1, of(came_1, upper), upper) + cross).astype(bf16))
         home_2 = jnp.concatenate([home_2, cross_2[count:]], axis=0)
-        homes = [home_1, home_2, home_3]
-        answer = owned(kept_0, met_0, came_0 + came_shared) + shared_part[0] + back_0.astype(f32)
+        homes = [home_2, home_3]
+        answer = early + shared_part[0] + back_0.astype(f32)
+        for value in came_shared:
+            answer = answer + value.astype(f32)
     else:
         totals = []
         for s in range(planes):

time: 183 us -> 180 us (0.984)
  local copies, waits for them, and re-layouts: 3.25 us -> 0.77 us
    unnamed x12 -> x8, local copies, waits for them, and re-layouts: 2.58 us -> 0.1 us
  transfers between devices with their start and end apart: 35 -> 35, of which waited for: 15 -> 15; matrix products, arithmetic and copies ran while one was open for 4% -> 4% of each run, Pallas kernels for 46% -> 47%
where the time goes in v5:
time: 180 us; the launch traced here: 179 us
  Pallas kernels  85.9 us (48%)
  waiting for transfers between devices  49 us (27%)
  starting transfers between devices  34.4 us (19%)
  other arithmetic  8.3 us (5%)
    pallas_call x6, Pallas kernels, ffn(): pl.pallas_call(body, out_shape=[jax.ShapeDtypeStruct((blocks, count, widt...  83.7 us
    ppermute x30, waiting for transfers between devices, exchange(): return lax.ppermute(value, axis, pairs)  37.9 us
    ppermute x30, starting transfers between devices, exchange(): return lax.ppermute(value, axis, pairs)  26.3 us
    ppermute x4, waiting for transfers between devices, over_planes(): lax.ppermute(value, 'expert', [(4 * s + k, 4 * t + k) for s, t in pairs f...  11.1 us
    ppermute x4, starting transfers between devices, over_planes(): lax.ppermute(value, 'expert', [(4 * s + k, 4 * t + k) for s, t in pairs f...  7.1 us
  transfers between devices with their start and end apart: 35, of which 15 were waited for; matrix products, arithmetic and copies ran while one was open for 4% of the time, Pallas kernels for 47%

profile of v5, /device:TPU:8, one launch (start us, length us, event | category | flops | bytes accessed | tf_op | source)
XLA Modules:
  0.0 179.4 jit_solution(3153504193107664896)
XLA Ops:
  0.0 2.2 %widen.1.refs_1_ = bf16[128,3712]{1,0:T(8,128)(2,1)S(1)} custom-call(bf16[128,3584]{1,0:T(8,128)(2,1)} %refs_1_, s32[8,128]{1,0:T(8,128)} %bitcast.85, f32[8,128]{1,0:T(8,128)} %bitcast.86), custom_call_target="tpu_custom_call" | custom-call | tf_op jit(solution)/shard_map/widen/pallas_call | solution.py:42
  2.3 5.0 %collective-permute-start.2 = (bf16[128,3712]{1,0:T(8,128)(2,1)S(1)}, bf16[128,3712]{1,0:T(8,128)(2,1)}, u32[]{:S(2)}, u32[]{:S(2)}) collective-permute-start(bf16[128,3712]{1,0:T(8,128)(2,1)S(1)} %widen.1.refs_1_), channel_id=1, source_target_pairs={{4,8},{5,9},{6,10},{7,11},{8,4},{9,5},{10,6},{11,7},{20,24},{21,25... | collective-permute-start | bytes 2850824 | tf_op jit(solution)/shard_map/ppermute | solution.py:233
  7.4 1.6 collective-permute-start.4
  10.3 11.5 %routed_expert.5 = (bf16[2,128,1792]{2,1,0:T(8,128)(2,1)S(1)}, bf16[2,128,1792]{2,1,0:T(8,128)(2,1)}) custom-call(s32[2]{0:T(128)S(1)} %pad_add_fusion.refs_0_, bf16[128,3712]{1,0:T(8,128)(2,1)S(1)} %widen.1.refs_1_, bf16[128,3712]{1,0:T(8,128)(2,1)S(1)} %collective-permute-done.refs_2_, bf16[3584,1024]{1,0:T(8,128)(2,1)} %bitcast.70, ...), custom_call_target="tpu_custom_call" | custom-call | flops 5637144576 | bytes 25690112 | tf_op jit(solution)/shard_map/routed_expert/pallas_call | solution.py:179
  22.0 3.9 %collective-permute-done.1.refs_2_ = bf16[128,3712]{1,0:T(8,128)(2,1)} collective-permute-done((bf16[128,3712]{1,0:T(8,128)(2,1)S(1)}, bf16[128,3712]{1,0:T(8,128)(2,1)}, u32[]{:S(2)}, u32[]{:S(2)}) %collective-permute-start.1) | collective-permute-done | bytes 950304 | tf_op jit(solution)/shard_map/ppermute | solution.py:233
  25.8 3.0 %collective-permute-done.2 = bf16[128,3712]{1,0:T(8,128)(2,1)} collective-permute-done((bf16[128,3712]{1,0:T(8,128)(2,1)S(1)}, bf16[128,3712]{1,0:T(8,128)(2,1)}, u32[]{:S(2)}, u32[]{:S(2)}) %collective-permute-start.2) | collective-permute-done | bytes 950304 | tf_op jit(solution)/shard_map/ppermute | solution.py:233
  28.9 1.5 collective-permute-start.7
  30.6 1.3 broadcast_select_fusion.1
  33.1 1.6 collective-permute-start.9
  34.7 16.9 %routed_expert.6 = (bf16[2,256,1792]{2,1,0:T(8,128)(2,1)S(1)}, bf16[2,256,1792]{2,1,0:T(8,128)(2,1)S(1)}) custom-call(s32[2]{0:T(128)S(1)} %pad_add_fusion.refs_0_, bf16[128,3712]{1,0:T(8,128)(2,1)} %collective-permute-done.4.refs_1_, bf16[128,3712]{1,0:T(8,128)(2,1)} %collective-permute-done.1.refs_2_, ...), custom_call_target="tpu_custom_call" | custom-call | flops 11274289152 | bytes 29360128 | tf_op jit(solution)/shard_map/routed_expert/pallas_call | solution.py:179
  52.5 3.6 %collective-permute-done.8.refs_2_ = bf16[128,3712]{1,0:T(8,128)(2,1)S(1)} collective-permute-done((bf16[128,3712]{1,0:T(8,128)(2,1)S(1)}, bf16[128,3712]{1,0:T(8,128)(2,1)S(1)}, u32[]{:S(2)}, u32[]{:S(2)}) %collective-permute-start.8) | collective-permute-done | bytes 950304 | tf_op jit(solution)/shard_map/ppermute | solution.py:233
  56.6 1.5 collective-permute-start.12
  58.2 1.8 collective-permute-done.13
  60.1 1.6 collective-permute-start.14
  61.7 1.9 %collective-permute-start.15 = (bf16[128,3712]{1,0:T(8,128)(2,1)S(1)}, bf16[128,3712]{1,0:T(8,128)(2,1)S(1)}, u32[]{:S(2)}, u32[]{:S(2)}) collective-permute-start(bf16[128,3712]{1,0:T(8,128)(2,1)S(1)} %collective-permute-done.8.refs_2_), channel_id=1, source_target_pairs={{4,0},{5,1},{6,2},{7,3},{8,12},{9,13},{10,14},{11,15},{20,16},{21,... | collective-permute-start | bytes 2850824 | tf_op jit(solution)/shard_map/ppermute | solution.py:233
  63.7 17.2 %routed_expert.7 = (bf16[2,256,1792]{2,1,0:T(8,128)(2,1)S(1)}, bf16[2,256,1792]{2,1,0:T(8,128)(2,1)S(1)}) custom-call(s32[2]{0:T(128)S(1)} %pad_add_fusion.refs_0_, bf16[128,3712]{1,0:T(8,128)(2,1)S(1)} %collective-permute-done.7.refs_1_, bf16[128,3712]{1,0:T(8,128)(2,1)S(1)} %collective-permute-done.8.refs_2_, ...), custom_call_target="tpu_custom_call" | custom-call | flops 11274289152 | bytes 29360128 | tf_op jit(solution)/shard_map/routed_expert/pallas_call | solution.py:179
  80.9 1.7 collective-permute-done.14
  83.7 1.4 broadcast_select_fusion.refs_2_
  85.3 1.4 collective-permute-start.18
  89.1 17.2 %routed_expert.8 = (bf16[2,256,1792]{2,1,0:T(8,128)(2,1)S(1)}, bf16[2,256,1792]{2,1,0:T(8,128)(2,1)S(1)}) custom-call(s32[2]{0:T(128)S(1)} %pad_add_fusion.refs_0_, bf16[128,3712]{1,0:T(8,128)(2,1)S(1)} %collective-permute-done.12.refs_1_, bf16[128,3712]{1,0:T(8,128)(2,1)S(1)} %broadcast_select_fusion.refs_2_, ...), custom_call_target="tpu_custom_call" | custom-call | flops 11274289152 | bytes 29360128 | tf_op jit(solution)/shard_map/routed_expert/pallas_call | solution.py:179
  106.3 2.5 %collective-permute-done.18.refs_1_ = bf16[128,3712]{1,0:T(8,128)(2,1)S(1)} collective-permute-done((bf16[128,3712]{1,0:T(8,128)(2,1)S(1)}, bf16[128,3712]{1,0:T(8,128)(2,1)S(1)}, u32[]{:S(2)}, u32[]{:S(2)}) %collective-permute-start.18) | collective-permute-done | bytes 950304 | tf_op jit(solution)/shard_map/ppermute | solution.py:19
  110.5 2.4 %collective-permute-start.23 = (bf16[96,1792]{1,0:T(8,128)(2,1)S(1)}, bf16[96,1792]{1,0:T(8,128)(2,1)S(1)}, u32[]{:S(2)}, u32[]{:S(2)}) collective-permute-start(bf16[96,1792]{1,0:T(8,128)(2,1)S(1)} %slice.157), channel_id=1, source_target_pairs={{0,8},{1,9},{2,10},{3,11},{4,12},{5,13},{6,14},{7,15},{8,0},{9,1},... | collective-permute-start | bytes 1032200 | tf_op jit(solution)/shard_map/ppermute | solution.py:19
  114.7 11.3 %routed_expert.9 = (bf16[2,128,1792]{2,1,0:T(8,128)(2,1)S(1)}, bf16[2,128,1792]{2,1,0:T(8,128)(2,1)S(1)}) custom-call(s32[2]{0:T(128)S(1)} %pad_add_fusion.refs_0_, bf16[128,3712]{1,0:T(8,128)(2,1)S(1)} %collective-permute-done.18.refs_1_, bf16[128,3712]{1,0:T(8,128)(2,1)S(1)} %collective-permute-done.22.refs_2_, bf16[3584,1024]{1,0:T(8,128)(2,1)} %bitcast.74, ...), custom_call_target="tpu_custom_call" | custom-call | flops 5637144576 | bytes 25690112 | tf_op jit(solution)/shard_map/routed_expert/pallas_call | solution.py:179
  126.1 1.6 collective-permute-done.23
  128.6 3.4 %collective-permute-start.28 = (bf16[160,1792]{1,0:T(8,128)(2,1)S(1)}, bf16[160,1792]{1,0:T(8,128)(2,1)S(1)}, u32[]{:S(2)}, u32[]{:S(2)}) collective-permute-start(bf16[160,1792]{1,0:T(8,128)(2,1)S(1)} %pad_maximum_fusion), channel_id=1, source_target_pairs={{0,8},{1,9},{2,10},{3,11},{4,12},{5,13},{6,14},{7,15},{8,0},{9,1},... | collective-permute-start | bytes 1720328 | tf_op jit(solution)/shard_map/ppermute | solution.py:19
  132.9 1.4 collective-permute-start.27
  135.3 1.2 fusion.16
  136.5 9.5 %shared_expert.1 = f32[2,128,1792]{2,1,0:T(8,128)S(1)} custom-call(s32[2]{0:T(128)S(1)} %pad_add_fusion.refs_0_, bf16[128,3584]{1,0:T(8,128)(2,1)S(1)} %copy-done, bf16[3584,1024]{1,0:T(8,128)(2,1)} %refs_2_.1, bf16[3584,1024]{1,0:T(8,128)(2,1)} %refs_3_.1, bf16[1024,3584]{1,0:T(8,128)(2,1)} %refs_4_.1), custom_call_target="tpu_custom_call" | custom-call | flops 2818572288 | bytes 23855104 | tf_op jit(solution)/shard_map/shared_expert/pallas_call | solution.py:179
  146.1 9.6 %collective-permute-done.28 = bf16[160,1792]{1,0:T(8,128)(2,1)S(1)} collective-permute-done((bf16[160,1792]{1,0:T(8,128)(2,1)S(1)}, bf16[160,1792]{1,0:T(8,128)(2,1)S(1)}, u32[]{:S(2)}, u32[]{:S(2)}) %collective-permute-start.28) | collective-permute-done | bytes 573472 | tf_op jit(solution)/shard_map/ppermute | solution.py:19
  155.9 1.6 collective-permute-start.34
  157.6 1.6 collective-permute-start.33
  160.1 18.2 %collective-permute-done.34 = bf16[128,1792]{1,0:T(8,128)(2,1)S(1)} collective-permute-done((bf16[128,1792]{1,0:T(8,128)(2,1)S(1)}, bf16[128,1792]{1,0:T(8,128)(2,1)S(1)}, u32[]{:S(2)}, u32[]{:S(2)}) %collective-permute-start.34) | collective-permute-done | bytes 458784 | tf_op jit(solution)/shard_map/ppermute | solution.py:19
  (74 shorter events, 16.3 us)
Async XLA Ops:
  2.2 8.1 %collective-permute-start = (bf16[128,3712]{1,0:T(8,128)(2,1)S(1)}, bf16[128,3712]{1,0:T(8,128)(2,1)S(1)}, u32[]{:S(2)}, u32[]{:S(2)}) collective-permute-start(bf16[128,3712]{1,0:T(8,128)(2,1)S(1)} %widen.1.refs_1_), channel_id=1, source_target_pairs={{0,1},{1,0},{2,3},{3,2},{4,5},{5,4},{6,7},{7,6},{8,9},{9,8},{10,11... | collective-permute-start | bytes 2850824 | tf_op jit(solution)/shard_map/ppermute | solution.py:19
  2.3 23.6 %collective-permute-start.1 = (bf16[128,3712]{1,0:T(8,128)(2,1)S(1)}, bf16[128,3712]{1,0:T(8,128)(2,1)}, u32[]{:S(2)}, u32[]{:S(2)}) collective-permute-start(bf16[128,3712]{1,0:T(8,128)(2,1)S(1)} %widen.1.refs_1_), channel_id=1, source_target_pairs={{0,4},{1,5},{2,6},{3,7},{4,0},{5,1},{6,2},{7,3},{8,12},{9,13},{10,... | collective-permute-start | bytes 2850824 | tf_op jit(solution)/shard_map/ppermute | solution.py:233
  2.3 26.5 %collective-permute-start.2 = (bf16[128,3712]{1,0:T(8,128)(2,1)S(1)}, bf16[128,3712]{1,0:T(8,128)(2,1)}, u32[]{:S(2)}, u32[]{:S(2)}) collective-permute-start(bf16[128,3712]{1,0:T(8,128)(2,1)S(1)} %widen.1.refs_1_), channel_id=1, source_target_pairs={{4,8},{5,9},{6,10},{7,11},{8,4},{9,5},{10,6},{11,7},{20,24},{21,25... | collective-permute-start | bytes 2850824 | tf_op jit(solution)/shard_map/ppermute | solution.py:233
  7.4 23.0 %collective-permute-start.4 = (bf16[128,3712]{1,0:T(8,128)(2,1)S(1)}, bf16[128,3712]{1,0:T(8,128)(2,1)}, u32[]{:S(2)}, u32[]{:S(2)}) collective-permute-start(bf16[128,3712]{1,0:T(8,128)(2,1)S(1)} %widen.1.refs_1_), channel_id=1, source_target_pairs={{0,2},{1,3},{2,0},{3,1},{4,6},{5,7},{6,4},{7,5},{8,10},{9,11},{10,... | collective-permute-start | bytes 2850824 | tf_op jit(solution)/shard_map/ppermute | solution.py:19
  21.9 8.5 %collective-permute-start.3 = (bf16[2,128,1792]{2,1,0:T(8,128)(2,1)}, bf16[2,128,1792]{2,1,0:T(8,128)(2,1)}, u32[]{:S(2)}, u32[]{:S(2)}) collective-permute-start(bf16[2,128,1792]{2,1,0:T(8,128)(2,1)} %get-tuple-element.59), channel_id=1, source_target_pairs={{0,1},{1,0},{2,3},{3,2},{4,5},{5,4},{6,7},{7,6},{8,9},{9,8},{10,11... | collective-permute-start | bytes 2752520 | tf_op jit(solution)/shard_map/ppermute | solution.py:19
  28.9 5.8 %collective-permute-start.6 = (bf16[128,3712]{1,0:T(8,128)(2,1)}, bf16[128,3712]{1,0:T(8,128)(2,1)S(1)}, u32[]{:S(2)}, u32[]{:S(2)}) collective-permute-start(bf16[128,3712]{1,0:T(8,128)(2,1)} %collective-permute-done.1.refs_2_), channel_id=1, source_target_pairs={{0,1},{1,0},{2,3},{3,2},{4,5},{5,4},{6,7},{7,6},{8,9},{9,8},{10,11... | collective-permute-start | bytes 2850824 | tf_op jit(solution)/shard_map/ppermute | solution.py:19
  28.9 23.7 %collective-permute-start.7 = (bf16[128,3712]{1,0:T(8,128)(2,1)}, bf16[128,3712]{1,0:T(8,128)(2,1)S(1)}, u32[]{:S(2)}, u32[]{:S(2)}) collective-permute-start(bf16[128,3712]{1,0:T(8,128)(2,1)} %collective-permute-done.1.refs_2_), channel_id=1, source_target_pairs={{0,2},{1,3},{2,0},{3,1},{4,6},{5,7},{6,4},{7,5},{8,10},{9,11},{10,... | collective-permute-start | bytes 2850824 | tf_op jit(solution)/shard_map/ppermute | solution.py:19
  30.4 4.3 %collective-permute-start.5 = (bf16[128,3712]{1,0:T(8,128)(2,1)}, bf16[128,3712]{1,0:T(8,128)(2,1)S(1)}, u32[]{:S(2)}, u32[]{:S(2)}) collective-permute-start(bf16[128,3712]{1,0:T(8,128)(2,1)} %collective-permute-done.4.refs_1_), channel_id=1, source_target_pairs={{0,1},{1,0},{2,3},{3,2},{4,5},{5,4},{6,7},{7,6},{8,9},{9,8},{10,11... | collective-permute-start | bytes 2850824 | tf_op jit(solution)/shard_map/ppermute | solution.py:19
  31.9 24.2 %collective-permute-start.8 = (bf16[128,3712]{1,0:T(8,128)(2,1)S(1)}, bf16[128,3712]{1,0:T(8,128)(2,1)S(1)}, u32[]{:S(2)}, u32[]{:S(2)}) collective-permute-start(bf16[128,3712]{1,0:T(8,128)(2,1)S(1)} %broadcast_select_fusion.1), channel_id=1, source_target_pairs={{0,8},{1,9},{2,10},{3,11},{12,4},{13,5},{14,6},{15,7},{4,0},{5,1},... | collective-permute-start | bytes 2850824 | tf_op jit(solution)/shard_map/ppermute | solution.py:233
  33.1 23.0 %collective-permute-start.9 = (bf16[128,1792]{1,0:T(8,128)(2,1)S(1)}, bf16[128,1792]{1,0:T(8,128)(2,1)S(1)}, u32[]{:S(2)}, u32[]{:S(2)}) collective-permute-start(bf16[128,1792]{1,0:T(8,128)(2,1)S(1)} %fusion.17), channel_id=1, source_target_pairs={{0,16},{16,0},{1,17},{17,1},{2,18},{18,2},{3,19},{19,3},{4,20},{20... | collective-permute-start | bytes 1376264 | tf_op jit(solution)/shard_map/ppermute | solution.py:19
  56.1 7.5 %collective-permute-start.10 = (bf16[128,3712]{1,0:T(8,128)(2,1)S(1)}, bf16[128,3712]{1,0:T(8,128)(2,1)S(1)}, u32[]{:S(2)}, u32[]{:S(2)}) collective-permute-start(bf16[128,3712]{1,0:T(8,128)(2,1)S(1)} %collective-permute-done.7.refs_1_), channel_id=1, source_target_pairs={{0,1},{1,0},{2,3},{3,2},{4,5},{5,4},{6,7},{7,6},{8,9},{9,8},{10,11... | collective-permute-start | bytes 2850824 | tf_op jit(solution)/shard_map/ppermute | solution.py:19
  56.6 7.0 %collective-permute-start.11 = (bf16[128,3712]{1,0:T(8,128)(2,1)S(1)}, bf16[128,3712]{1,0:T(8,128)(2,1)S(1)}, u32[]{:S(2)}, u32[]{:S(2)}) collective-permute-start(bf16[128,3712]{1,0:T(8,128)(2,1)S(1)} %collective-permute-done.8.refs_2_), channel_id=1, source_target_pairs={{0,1},{1,0},{2,3},{3,2},{4,5},{5,4},{6,7},{7,6},{8,9},{9,8},{10,11... | collective-permute-start | bytes 2850824 | tf_op jit(solution)/shard_map/ppermute | solution.py:19
  56.6 24.2 %collective-permute-start.12 = (bf16[128,3712]{1,0:T(8,128)(2,1)S(1)}, bf16[128,3712]{1,0:T(8,128)(2,1)S(1)}, u32[]{:S(2)}, u32[]{:S(2)}) collective-permute-start(bf16[128,3712]{1,0:T(8,128)(2,1)S(1)} %collective-permute-done.8.refs_2_), channel_id=1, source_target_pairs={{0,2},{1,3},{2,0},{3,1},{4,6},{5,7},{6,4},{7,5},{8,10},{9,11},{10,... | collective-permute-start | bytes 2850824 | tf_op jit(solution)/shard_map/ppermute | solution.py:19
  60.1 22.5 %collective-permute-start.14 = (bf16[256,1792]{1,0:T(8,128)(2,1)S(1)}, bf16[256,1792]{1,0:T(8,128)(2,1)S(1)}, u32[]{:S(2)}, u32[]{:S(2)}) collective-permute-start(bf16[256,1792]{1,0:T(8,128)(2,1)S(1)} %fusion), channel_id=1, source_target_pairs={{0,16},{16,0},{1,17},{17,1},{2,18},{18,2},{3,19},{19,3},{4,20},{20... | collective-permute-start | bytes 2752520 | tf_op jit(solution)/shard_map/ppermute | solution.py:19
  61.7 22.0 %collective-permute-start.15 = (bf16[128,3712]{1,0:T(8,128)(2,1)S(1)}, bf16[128,3712]{1,0:T(8,128)(2,1)S(1)}, u32[]{:S(2)}, u32[]{:S(2)}) collective-permute-start(bf16[128,3712]{1,0:T(8,128)(2,1)S(1)} %collective-permute-done.8.refs_2_), channel_id=1, source_target_pairs={{4,0},{5,1},{6,2},{7,3},{8,12},{9,13},{10,14},{11,15},{20,16},{21,... | collective-permute-start | bytes 2850824 | tf_op jit(solution)/shard_map/ppermute | solution.py:233
  82.6 4.2 %collective-permute-start.19 = (bf16[2,256,1792]{2,1,0:T(8,128)(2,1)S(1)}, bf16[2,256,1792]{2,1,0:T(8,128)(2,1)S(1)}, u32[]{:S(2)}, u32[]{:S(2)}) collective-permute-start(bf16[2,256,1792]{2,1,0:T(8,128)(2,1)S(1)} %get-tuple-element.86), channel_id=1, source_target_pairs={{0,1},{1,0},{2,3},{3,2},{4,5},{5,4},{6,7},{7,6},{8,9},{9,8},{10,11... | collective-permute-start | bytes 5505032 | tf_op jit(solution)/shard_map/ppermute | solution.py:19
  82.6 6.3 %collective-permute-start.16 = (bf16[128,3712]{1,0:T(8,128)(2,1)S(1)}, bf16[128,3712]{1,0:T(8,128)(2,1)S(1)}, u32[]{:S(2)}, u32[]{:S(2)}) collective-permute-start(bf16[128,3712]{1,0:T(8,128)(2,1)S(1)} %collective-permute-done.12.refs_1_), channel_id=1, source_target_pairs={{0,1},{1,0},{2,3},{3,2},{4,5},{5,4},{6,7},{7,6},{8,9},{9,8},{10,11... | collective-permute-start | bytes 2850824 | tf_op jit(solution)/shard_map/ppermute | solution.py:19
  85.3 23.5 %collective-permute-start.18 = (bf16[128,3712]{1,0:T(8,128)(2,1)S(1)}, bf16[128,3712]{1,0:T(8,128)(2,1)S(1)}, u32[]{:S(2)}, u32[]{:S(2)}) collective-permute-start(bf16[128,3712]{1,0:T(8,128)(2,1)S(1)} %broadcast_select_fusion.refs_2_), channel_id=1, source_target_pairs={{0,2},{1,3},{2,0},{3,1},{4,6},{5,7},{6,4},{7,5},{8,10},{9,11},{10,... | collective-permute-start | bytes 2850824 | tf_op jit(solution)/shard_map/ppermute | solution.py:19
  87.0 22.5 %collective-permute-start.21 = (bf16[256,1792]{1,0:T(8,128)(2,1)S(1)}, bf16[256,1792]{1,0:T(8,128)(2,1)S(1)}, u32[]{:S(2)}, u32[]{:S(2)}) collective-permute-start(bf16[256,1792]{1,0:T(8,128)(2,1)S(1)} %fusion.1), channel_id=1, source_target_pairs={{0,16},{16,0},{1,17},{17,1},{2,18},{18,2},{3,19},{19,3},{4,20},{20... | collective-permute-start | bytes 2752520 | tf_op jit(solution)/shard_map/ppermute | solution.py:19
  88.2 20.7 %collective-permute-start.20 = (bf16[128,1792]{1,0:T(8,128)(2,1)S(1)}, bf16[128,1792]{1,0:T(8,128)(2,1)S(1)}, u32[]{:S(2)}, u32[]{:S(2)}) collective-permute-start(bf16[128,1792]{1,0:T(8,128)(2,1)S(1)} %fusion.15), channel_id=1, source_target_pairs={{0,4},{1,5},{2,6},{3,7},{4,0},{5,1},{6,2},{7,3},{8,12},{9,13},{10,... | collective-permute-start | bytes 1376264 | tf_op jit(solution)/shard_map/ppermute | solution.py:19
  109.6 5.1 %collective-permute-start.22 = (bf16[128,3712]{1,0:T(8,128)(2,1)S(1)}, bf16[128,3712]{1,0:T(8,128)(2,1)S(1)}, u32[]{:S(2)}, u32[]{:S(2)}) collective-permute-start(bf16[128,3712]{1,0:T(8,128)(2,1)S(1)} %collective-permute-done.18.refs_1_), channel_id=1, source_target_pairs={{0,1},{1,0},{2,3},{3,2},{4,5},{5,4},{6,7},{7,6},{8,9},{9,8},{10,11... | collective-permute-start | bytes 2850824 | tf_op jit(solution)/shard_map/ppermute | solution.py:19
  110.5 17.2 %collective-permute-start.23 = (bf16[96,1792]{1,0:T(8,128)(2,1)S(1)}, bf16[96,1792]{1,0:T(8,128)(2,1)S(1)}, u32[]{:S(2)}, u32[]{:S(2)}) collective-permute-start(bf16[96,1792]{1,0:T(8,128)(2,1)S(1)} %slice.157), channel_id=1, source_target_pairs={{0,8},{1,9},{2,10},{3,11},{4,12},{5,13},{6,14},{7,15},{8,0},{9,1},... | collective-permute-start | bytes 1032200 | tf_op jit(solution)/shard_map/ppermute | solution.py:19
  113.6 14.1 %collective-permute-start.25 = (bf16[128,1792]{1,0:T(8,128)(2,1)S(1)}, bf16[128,1792]{1,0:T(8,128)(2,1)S(1)}, u32[]{:S(2)}, u32[]{:S(2)}) collective-permute-start(bf16[128,1792]{1,0:T(8,128)(2,1)S(1)} %get-tuple-element.112), channel_id=1, source_target_pairs={{0,16},{16,0},{1,17},{17,1},{2,18},{18,2},{3,19},{19,3},{4,20},{20... | collective-permute-start | bytes 1376264 | tf_op jit(solution)/shard_map/ppermute | solution.py:19
  127.7 4.3 %collective-permute-start.26 = (bf16[2,128,1792]{2,1,0:T(8,128)(2,1)S(1)}, bf16[2,128,1792]{2,1,0:T(8,128)(2,1)S(1)}, u32[]{:S(2)}, u32[]{:S(2)}) collective-permute-start(bf16[2,128,1792]{2,1,0:T(8,128)(2,1)S(1)} %get-tuple-element.96), channel_id=1, source_target_pairs={{0,1},{1,0},{2,3},{3,2},{4,5},{5,4},{6,7},{7,6},{8,9},{9,8},{10,11... | collective-permute-start | bytes 2752520 | tf_op jit(solution)/shard_map/ppermute | solution.py:19
  127.7 18.3 %collective-permute-start.31 = (bf16[128,1792]{1,0:T(8,128)(2,1)S(1)}, bf16[128,1792]{1,0:T(8,128)(2,1)S(1)}, u32[]{:S(2)}, u32[]{:S(2)}) collective-permute-start(bf16[128,1792]{1,0:T(8,128)(2,1)S(1)} %get-tuple-element.111), channel_id=1, source_target_pairs={{0,16},{16,0},{1,17},{17,1},{2,18},{18,2},{3,19},{19,3},{4,20},{20... | collective-permute-start | bytes 1376264 | tf_op jit(solution)/shard_map/ppermute | solution.py:19
  128.6 27.1 %collective-permute-start.28 = (bf16[160,1792]{1,0:T(8,128)(2,1)S(1)}, bf16[160,1792]{1,0:T(8,128)(2,1)S(1)}, u32[]{:S(2)}, u32[]{:S(2)}) collective-permute-start(bf16[160,1792]{1,0:T(8,128)(2,1)S(1)} %pad_maximum_fusion), channel_id=1, source_target_pairs={{0,8},{1,9},{2,10},{3,11},{4,12},{5,13},{6,14},{7,15},{8,0},{9,1},... | collective-permute-start | bytes 1720328 | tf_op jit(solution)/shard_map/ppermute | solution.py:19
  132.2 23.4 %collective-permute-start.29 = (bf16[128,1792]{1,0:T(8,128)(2,1)S(1)}, bf16[128,1792]{1,0:T(8,128)(2,1)S(1)}, u32[]{:S(2)}, u32[]{:S(2)}) collective-permute-start(bf16[128,1792]{1,0:T(8,128)(2,1)S(1)} %get-tuple-element.114), channel_id=1, source_target_pairs={{0,2},{1,3},{2,0},{3,1},{4,6},{5,7},{6,4},{7,5},{8,10},{9,11},{10,... | collective-permute-start | bytes 1376264 | tf_op jit(solution)/shard_map/ppermute | solution.py:19
  132.9 22.8 %collective-permute-start.27 = (bf16[128,1792]{1,0:T(8,128)(2,1)S(1)}, bf16[128,1792]{1,0:T(8,128)(2,1)S(1)}, u32[]{:S(2)}, u32[]{:S(2)}) collective-permute-start(bf16[128,1792]{1,0:T(8,128)(2,1)S(1)} %get-tuple-element.98), channel_id=1, source_target_pairs={{0,4},{1,5},{2,6},{3,7},{4,0},{5,1},{6,2},{7,3},{8,12},{9,13},{10,... | collective-permute-start | bytes 1376264 | tf_op jit(solution)/shard_map/ppermute | solution.py:19
  134.2 21.4 %collective-permute-start.30 = (bf16[128,1792]{1,0:T(8,128)(2,1)S(1)}, bf16[128,1792]{1,0:T(8,128)(2,1)S(1)}, u32[]{:S(2)}, u32[]{:S(2)}) collective-permute-start(bf16[128,1792]{1,0:T(8,128)(2,1)S(1)} %get-tuple-element.113), channel_id=1, source_target_pairs={{0,18},{1,19},{2,16},{3,17},{4,22},{5,23},{6,20},{7,21},{8,26},{9,... | collective-permute-start | bytes 1376264 | tf_op jit(solution)/shard_map/ppermute | solution.py:230
  155.9 22.4 %collective-permute-start.34 = (bf16[128,1792]{1,0:T(8,128)(2,1)S(1)}, bf16[128,1792]{1,0:T(8,128)(2,1)S(1)}, u32[]{:S(2)}, u32[]{:S(2)}) collective-permute-start(bf16[128,1792]{1,0:T(8,128)(2,1)S(1)} %fusion.4), channel_id=1, source_target_pairs={{0,12},{1,13},{2,14},{3,15},{4,8},{5,9},{6,10},{7,11},{8,4},{9,5},... | collective-permute-start | bytes 1376264 | tf_op jit(solution)/shard_map/ppermute | solution.py:19
  157.6 20.7 %collective-permute-start.33 = (bf16[128,1792]{1,0:T(8,128)(2,1)S(1)}, bf16[128,1792]{1,0:T(8,128)(2,1)S(1)}, u32[]{:S(2)}, u32[]{:S(2)}) collective-permute-start(bf16[128,1792]{1,0:T(8,128)(2,1)S(1)} %fusion.22), channel_id=1, source_target_pairs={{0,16},{16,0},{1,17},{17,1},{2,18},{18,2},{3,19},{19,3},{4,20},{20... | collective-permute-start | bytes 1376264 | tf_op jit(solution)/shard_map/ppermute | solution.py:19
  159.5 18.8 %collective-permute-start.32 = (bf16[128,1792]{1,0:T(8,128)(2,1)S(1)}, bf16[128,1792]{1,0:T(8,128)(2,1)S(1)}, u32[]{:S(2)}, u32[]{:S(2)}) collective-permute-start(bf16[128,1792]{1,0:T(8,128)(2,1)S(1)} %fusion.6), channel_id=1, source_target_pairs={{0,2},{1,3},{2,0},{3,1},{4,6},{5,7},{6,4},{7,5},{8,10},{9,11},{10,... | collective-permute-start | bytes 1376264 | tf_op jit(solution)/shard_map/ppermute | solution.py:19
  (7 other events, 32.4 us)

commit v6 on v5

--- a/solution.py
+++ b/solution.py
@@ -317,7 +317,8 @@
         home_2 = exchange(total_2[:cut], "expert", 8)
         came_3 = over_dp(to_dp(kept_3, met_3, upper))
         kept_4, sent_4 = routed(inputs)
-        kept_4, sent_4, home_2, *came_3 = together(kept_4, sent_4, home_2, *came_3)
+        kept_4, sent_4, *came_3 = together(kept_4, sent_4, *came_3)
+        home_2, *came_3 = together(home_2, *came_3)
 
         met_4 = over_core(sent_4)
         last_rows = sends = [(kept_4[k].astype(f32) + met_4[k].astype(f32)).astype(bf16) for k in range(n_dp)]

time: 180 us -> 179 us (level)
    ppermute x30, starting transfers between devices: 26.3 us -> 24.4 us  [exchange(): return lax.ppermute(value, axis, pairs)]
  transfers between devices with their start and end apart: 35 -> 35, of which waited for: 15 -> 16; matrix products, arithmetic and copies ran while one was open for 4% -> 4% of each run, Pallas kernels for 47% -> 47%
where the time goes in v6:
time: 179 us
  Pallas kernels  85.9 us (48%)
  waiting for transfers between devices  49.9 us (28%)
  starting transfers between devices  33 us (18%)
  other arithmetic  8.3 us (5%)
    pallas_call x6, Pallas kernels, ffn(): pl.pallas_call(body, out_shape=[jax.ShapeDtypeStruct((blocks, count, widt...  83.7 us
    ppermute x30, waiting for transfers between devices, exchange(): return lax.ppermute(value, axis, pairs)  38.8 us
    ppermute x30, starting transfers between devices, exchange(): return lax.ppermute(value, axis, pairs)  24.4 us
    ppermute x4, waiting for transfers between devices, over_planes(): lax.ppermute(value, 'expert', [(4 * s + k, 4 * t + k) for s, t in pairs f...  11.1 us
    ppermute x4, starting transfers between devices, over_planes(): lax.ppermute(value, 'expert', [(4 * s + k, 4 * t + k) for s, t in pairs f...  7.1 us
  transfers between devices with their start and end apart: 35, of which 16 were waited for; matrix products, arithmetic and copies ran while one was open for 4% of the time, Pallas kernels for 47%

profile of v6, /device:TPU:8, one launch (start us, length us, event | category | flops | bytes accessed | tf_op | source)
XLA Modules:
  0.0 178.8 jit_solution(11242004708239741936)
XLA Ops:
  0.0 2.2 %widen.1.refs_1_ = bf16[128,3712]{1,0:T(8,128)(2,1)S(1)} custom-call(bf16[128,3584]{1,0:T(8,128)(2,1)} %refs_1_, s32[8,128]{1,0:T(8,128)} %bitcast.85, f32[8,128]{1,0:T(8,128)} %bitcast.86), custom_call_target="tpu_custom_call" | custom-call | tf_op jit(solution)/shard_map/widen/pallas_call | solution.py:42
  2.3 5.0 %collective-permute-start.2 = (bf16[128,3712]{1,0:T(8,128)(2,1)S(1)}, bf16[128,3712]{1,0:T(8,128)(2,1)}, u32[]{:S(2)}, u32[]{:S(2)}) collective-permute-start(bf16[128,3712]{1,0:T(8,128)(2,1)S(1)} %widen.1.refs_1_), channel_id=1, source_target_pairs={{4,8},{5,9},{6,10},{7,11},{8,4},{9,5},{10,6},{11,7},{20,24},{21,25... | collective-permute-start | bytes 2850824 | tf_op jit(solution)/shard_map/ppermute | solution.py:233
  7.4 1.6 collective-permute-start.4
  10.3 11.5 %routed_expert.5 = (bf16[2,128,1792]{2,1,0:T(8,128)(2,1)S(1)}, bf16[2,128,1792]{2,1,0:T(8,128)(2,1)}) custom-call(s32[2]{0:T(128)S(1)} %pad_add_fusion.refs_0_, bf16[128,3712]{1,0:T(8,128)(2,1)S(1)} %widen.1.refs_1_, bf16[128,3712]{1,0:T(8,128)(2,1)S(1)} %collective-permute-done.refs_2_, bf16[3584,1024]{1,0:T(8,128)(2,1)} %bitcast.70, ...), custom_call_target="tpu_custom_call" | custom-call | flops 5637144576 | bytes 25690112 | tf_op jit(solution)/shard_map/routed_expert/pallas_call | solution.py:179
  22.0 3.9 %collective-permute-done.1.refs_2_ = bf16[128,3712]{1,0:T(8,128)(2,1)} collective-permute-done((bf16[128,3712]{1,0:T(8,128)(2,1)S(1)}, bf16[128,3712]{1,0:T(8,128)(2,1)}, u32[]{:S(2)}, u32[]{:S(2)}) %collective-permute-start.1) | collective-permute-done | bytes 950304 | tf_op jit(solution)/shard_map/ppermute | solution.py:233
  25.8 3.0 %collective-permute-done.2 = bf16[128,3712]{1,0:T(8,128)(2,1)} collective-permute-done((bf16[128,3712]{1,0:T(8,128)(2,1)S(1)}, bf16[128,3712]{1,0:T(8,128)(2,1)}, u32[]{:S(2)}, u32[]{:S(2)}) %collective-permute-start.2) | collective-permute-done | bytes 950304 | tf_op jit(solution)/shard_map/ppermute | solution.py:233
  28.9 1.5 collective-permute-start.7
  30.6 1.3 broadcast_select_fusion.1
  33.1 1.6 collective-permute-start.9
  34.7 16.9 %routed_expert.6 = (bf16[2,256,1792]{2,1,0:T(8,128)(2,1)S(1)}, bf16[2,256,1792]{2,1,0:T(8,128)(2,1)S(1)}) custom-call(s32[2]{0:T(128)S(1)} %pad_add_fusion.refs_0_, bf16[128,3712]{1,0:T(8,128)(2,1)} %collective-permute-done.4.refs_1_, bf16[128,3712]{1,0:T(8,128)(2,1)} %collective-permute-done.1.refs_2_, ...), custom_call_target="tpu_custom_call" | custom-call | flops 11274289152 | bytes 29360128 | tf_op jit(solution)/shard_map/routed_expert/pallas_call | solution.py:179
  52.5 3.6 %collective-permute-done.8.refs_2_ = bf16[128,3712]{1,0:T(8,128)(2,1)S(1)} collective-permute-done((bf16[128,3712]{1,0:T(8,128)(2,1)S(1)}, bf16[128,3712]{1,0:T(8,128)(2,1)S(1)}, u32[]{:S(2)}, u32[]{:S(2)}) %collective-permute-start.8) | collective-permute-done | bytes 950304 | tf_op jit(solution)/shard_map/ppermute | solution.py:233
  56.6 1.5 collective-permute-start.12
  58.2 1.8 collective-permute-done.13
  60.1 1.6 collective-permute-start.14
  61.7 1.9 %collective-permute-start.15 = (bf16[128,3712]{1,0:T(8,128)(2,1)S(1)}, bf16[128,3712]{1,0:T(8,128)(2,1)S(1)}, u32[]{:S(2)}, u32[]{:S(2)}) collective-permute-start(bf16[128,3712]{1,0:T(8,128)(2,1)S(1)} %collective-permute-done.8.refs_2_), channel_id=1, source_target_pairs={{4,0},{5,1},{6,2},{7,3},{8,12},{9,13},{10,14},{11,15},{20,16},{21,... | collective-permute-start | bytes 2850824 | tf_op jit(solution)/shard_map/ppermute | solution.py:233
  63.7 17.2 %routed_expert.7 = (bf16[2,256,1792]{2,1,0:T(8,128)(2,1)S(1)}, bf16[2,256,1792]{2,1,0:T(8,128)(2,1)S(1)}) custom-call(s32[2]{0:T(128)S(1)} %pad_add_fusion.refs_0_, bf16[128,3712]{1,0:T(8,128)(2,1)S(1)} %collective-permute-done.7.refs_1_, bf16[128,3712]{1,0:T(8,128)(2,1)S(1)} %collective-permute-done.8.refs_2_, ...), custom_call_target="tpu_custom_call" | custom-call | flops 11274289152 | bytes 29360128 | tf_op jit(solution)/shard_map/routed_expert/pallas_call | solution.py:179
  80.9 1.7 collective-permute-done.14
  83.7 1.4 broadcast_select_fusion.refs_2_
  85.3 1.4 collective-permute-start.18
  87.0 1.2 collective-permute-start.21
  89.1 17.2 %routed_expert.8 = (bf16[2,256,1792]{2,1,0:T(8,128)(2,1)S(1)}, bf16[2,256,1792]{2,1,0:T(8,128)(2,1)S(1)}) custom-call(s32[2]{0:T(128)S(1)} %pad_add_fusion.refs_0_, bf16[128,3712]{1,0:T(8,128)(2,1)S(1)} %collective-permute-done.12.refs_1_, bf16[128,3712]{1,0:T(8,128)(2,1)S(1)} %broadcast_select_fusion.refs_2_, ...), custom_call_target="tpu_custom_call" | custom-call | flops 11274289152 | bytes 29360128 | tf_op jit(solution)/shard_map/routed_expert/pallas_call | solution.py:179
  106.3 2.5 %collective-permute-done.18.refs_1_ = bf16[128,3712]{1,0:T(8,128)(2,1)S(1)} collective-permute-done((bf16[128,3712]{1,0:T(8,128)(2,1)S(1)}, bf16[128,3712]{1,0:T(8,128)(2,1)S(1)}, u32[]{:S(2)}, u32[]{:S(2)}) %collective-permute-start.18) | collective-permute-done | bytes 950304 | tf_op jit(solution)/shard_map/ppermute | solution.py:19
  110.5 2.4 %collective-permute-start.27 = (bf16[96,1792]{1,0:T(8,128)(2,1)S(1)}, bf16[96,1792]{1,0:T(8,128)(2,1)S(1)}, u32[]{:S(2)}, u32[]{:S(2)}) collective-permute-start(bf16[96,1792]{1,0:T(8,128)(2,1)S(1)} %slice.162), channel_id=1, source_target_pairs={{0,8},{1,9},{2,10},{3,11},{4,12},{5,13},{6,14},{7,15},{8,0},{9,1},... | collective-permute-start | bytes 1032200 | tf_op jit(solution)/shard_map/ppermute | solution.py:19
  114.7 11.3 %routed_expert.9 = (bf16[2,128,1792]{2,1,0:T(8,128)(2,1)S(1)}, bf16[2,128,1792]{2,1,0:T(8,128)(2,1)S(1)}) custom-call(s32[2]{0:T(128)S(1)} %pad_add_fusion.refs_0_, bf16[128,3712]{1,0:T(8,128)(2,1)S(1)} %collective-permute-done.18.refs_1_, bf16[128,3712]{1,0:T(8,128)(2,1)S(1)} %collective-permute-done.22.refs_2_, bf16[3584,1024]{1,0:T(8,128)(2,1)} %bitcast.74, ...), custom_call_target="tpu_custom_call" | custom-call | flops 5637144576 | bytes 25690112 | tf_op jit(solution)/shard_map/routed_expert/pallas_call | solution.py:179
  127.9 3.4 %collective-permute-start.28 = (bf16[160,1792]{1,0:T(8,128)(2,1)S(1)}, bf16[160,1792]{1,0:T(8,128)(2,1)S(1)}, u32[]{:S(2)}, u32[]{:S(2)}) collective-permute-start(bf16[160,1792]{1,0:T(8,128)(2,1)S(1)} %pad_maximum_fusion), channel_id=1, source_target_pairs={{0,8},{1,9},{2,10},{3,11},{4,12},{5,13},{6,14},{7,15},{8,0},{9,1},... | collective-permute-start | bytes 1720328 | tf_op jit(solution)/shard_map/ppermute | solution.py:19
  132.3 1.4 collective-permute-start.30
  133.7 1.2 fusion.16
  134.9 9.5 %shared_expert.1 = f32[2,128,1792]{2,1,0:T(8,128)S(1)} custom-call(s32[2]{0:T(128)S(1)} %pad_add_fusion.refs_0_, bf16[128,3584]{1,0:T(8,128)(2,1)S(1)} %copy-done, bf16[3584,1024]{1,0:T(8,128)(2,1)} %refs_2_.1, bf16[3584,1024]{1,0:T(8,128)(2,1)} %refs_3_.1, bf16[1024,3584]{1,0:T(8,128)(2,1)} %refs_4_.1), custom_call_target="tpu_custom_call" | custom-call | flops 2818572288 | bytes 23855104 | tf_op jit(solution)/shard_map/shared_expert/pallas_call | solution.py:179
  144.5 10.6 %collective-permute-done.28 = bf16[160,1792]{1,0:T(8,128)(2,1)S(1)} collective-permute-done((bf16[160,1792]{1,0:T(8,128)(2,1)S(1)}, bf16[160,1792]{1,0:T(8,128)(2,1)S(1)}, u32[]{:S(2)}, u32[]{:S(2)}) %collective-permute-start.28) | collective-permute-done | bytes 573472 | tf_op jit(solution)/shard_map/ppermute | solution.py:19
  155.4 1.2 collective-permute-start.34
  157.3 1.3 collective-permute-start.32
  158.6 19.1 %collective-permute-done.34 = bf16[128,1792]{1,0:T(8,128)(2,1)S(1)} collective-permute-done((bf16[128,1792]{1,0:T(8,128)(2,1)S(1)}, bf16[128,1792]{1,0:T(8,128)(2,1)S(1)}, u32[]{:S(2)}, u32[]{:S(2)}) %collective-permute-start.34) | collective-permute-done | bytes 458784 | tf_op jit(solution)/shard_map/ppermute | solution.py:19
  (74 shorter events, 14.8 us)
Async XLA Ops:
  2.2 8.1 %collective-permute-start = (bf16[128,3712]{1,0:T(8,128)(2,1)S(1)}, bf16[128,3712]{1,0:T(8,128)(2,1)S(1)}, u32[]{:S(2)}, u32[]{:S(2)}) collective-permute-start(bf16[128,3712]{1,0:T(8,128)(2,1)S(1)} %widen.1.refs_1_), channel_id=1, source_target_pairs={{0,1},{1,0},{2,3},{3,2},{4,5},{5,4},{6,7},{7,6},{8,9},{9,8},{10,11... | collective-permute-start | bytes 2850824 | tf_op jit(solution)/shard_map/ppermute | solution.py:19
  2.3 23.6 %collective-permute-start.1 = (bf16[128,3712]{1,0:T(8,128)(2,1)S(1)}, bf16[128,3712]{1,0:T(8,128)(2,1)}, u32[]{:S(2)}, u32[]{:S(2)}) collective-permute-start(bf16[128,3712]{1,0:T(8,128)(2,1)S(1)} %widen.1.refs_1_), channel_id=1, source_target_pairs={{0,4},{1,5},{2,6},{3,7},{4,0},{5,1},{6,2},{7,3},{8,12},{9,13},{10,... | collective-permute-start | bytes 2850824 | tf_op jit(solution)/shard_map/ppermute | solution.py:233
  2.3 26.5 %collective-permute-start.2 = (bf16[128,3712]{1,0:T(8,128)(2,1)S(1)}, bf16[128,3712]{1,0:T(8,128)(2,1)}, u32[]{:S(2)}, u32[]{:S(2)}) collective-permute-start(bf16[128,3712]{1,0:T(8,128)(2,1)S(1)} %widen.1.refs_1_), channel_id=1, source_target_pairs={{4,8},{5,9},{6,10},{7,11},{8,4},{9,5},{10,6},{11,7},{20,24},{21,25... | collective-permute-start | bytes 2850824 | tf_op jit(solution)/shard_map/ppermute | solution.py:233
  7.4 23.0 %collective-permute-start.4 = (bf16[128,3712]{1,0:T(8,128)(2,1)S(1)}, bf16[128,3712]{1,0:T(8,128)(2,1)}, u32[]{:S(2)}, u32[]{:S(2)}) collective-permute-start(bf16[128,3712]{1,0:T(8,128)(2,1)S(1)} %widen.1.refs_1_), channel_id=1, source_target_pairs={{0,2},{1,3},{2,0},{3,1},{4,6},{5,7},{6,4},{7,5},{8,10},{9,11},{10,... | collective-permute-start | bytes 2850824 | tf_op jit(solution)/shard_map/ppermute | solution.py:19
  21.9 8.5 %collective-permute-start.3 = (bf16[2,128,1792]{2,1,0:T(8,128)(2,1)}, bf16[2,128,1792]{2,1,0:T(8,128)(2,1)}, u32[]{:S(2)}, u32[]{:S(2)}) collective-permute-start(bf16[2,128,1792]{2,1,0:T(8,128)(2,1)} %get-tuple-element.60), channel_id=1, source_target_pairs={{0,1},{1,0},{2,3},{3,2},{4,5},{5,4},{6,7},{7,6},{8,9},{9,8},{10,11... | collective-permute-start | bytes 2752520 | tf_op jit(solution)/shard_map/ppermute | solution.py:19
  28.9 5.8 %collective-permute-start.6 = (bf16[128,3712]{1,0:T(8,128)(2,1)}, bf16[128,3712]{1,0:T(8,128)(2,1)S(1)}, u32[]{:S(2)}, u32[]{:S(2)}) collective-permute-start(bf16[128,3712]{1,0:T(8,128)(2,1)} %collective-permute-done.1.refs_2_), channel_id=1, source_target_pairs={{0,1},{1,0},{2,3},{3,2},{4,5},{5,4},{6,7},{7,6},{8,9},{9,8},{10,11... | collective-permute-start | bytes 2850824 | tf_op jit(solution)/shard_map/ppermute | solution.py:19
  28.9 23.7 %collective-permute-start.7 = (bf16[128,3712]{1,0:T(8,128)(2,1)}, bf16[128,3712]{1,0:T(8,128)(2,1)S(1)}, u32[]{:S(2)}, u32[]{:S(2)}) collective-permute-start(bf16[128,3712]{1,0:T(8,128)(2,1)} %collective-permute-done.1.refs_2_), channel_id=1, source_target_pairs={{0,2},{1,3},{2,0},{3,1},{4,6},{5,7},{6,4},{7,5},{8,10},{9,11},{10,... | collective-permute-start | bytes 2850824 | tf_op jit(solution)/shard_map/ppermute | solution.py:19
  30.4 4.3 %collective-permute-start.5 = (bf16[128,3712]{1,0:T(8,128)(2,1)}, bf16[128,3712]{1,0:T(8,128)(2,1)S(1)}, u32[]{:S(2)}, u32[]{:S(2)}) collective-permute-start(bf16[128,3712]{1,0:T(8,128)(2,1)} %collective-permute-done.4.refs_1_), channel_id=1, source_target_pairs={{0,1},{1,0},{2,3},{3,2},{4,5},{5,4},{6,7},{7,6},{8,9},{9,8},{10,11... | collective-permute-start | bytes 2850824 | tf_op jit(solution)/shard_map/ppermute | solution.py:19
  31.9 24.2 %collective-permute-start.8 = (bf16[128,3712]{1,0:T(8,128)(2,1)S(1)}, bf16[128,3712]{1,0:T(8,128)(2,1)S(1)}, u32[]{:S(2)}, u32[]{:S(2)}) collective-permute-start(bf16[128,3712]{1,0:T(8,128)(2,1)S(1)} %broadcast_select_fusion.1), channel_id=1, source_target_pairs={{0,8},{1,9},{2,10},{3,11},{12,4},{13,5},{14,6},{15,7},{4,0},{5,1},... | collective-permute-start | bytes 2850824 | tf_op jit(solution)/shard_map/ppermute | solution.py:233
  33.1 23.0 %collective-permute-start.9 = (bf16[128,1792]{1,0:T(8,128)(2,1)S(1)}, bf16[128,1792]{1,0:T(8,128)(2,1)S(1)}, u32[]{:S(2)}, u32[]{:S(2)}) collective-permute-start(bf16[128,1792]{1,0:T(8,128)(2,1)S(1)} %fusion.17), channel_id=1, source_target_pairs={{0,16},{16,0},{1,17},{17,1},{2,18},{18,2},{3,19},{19,3},{4,20},{20... | collective-permute-start | bytes 1376264 | tf_op jit(solution)/shard_map/ppermute | solution.py:19
  56.1 7.5 %collective-permute-start.10 = (bf16[128,3712]{1,0:T(8,128)(2,1)S(1)}, bf16[128,3712]{1,0:T(8,128)(2,1)S(1)}, u32[]{:S(2)}, u32[]{:S(2)}) collective-permute-start(bf16[128,3712]{1,0:T(8,128)(2,1)S(1)} %collective-permute-done.7.refs_1_), channel_id=1, source_target_pairs={{0,1},{1,0},{2,3},{3,2},{4,5},{5,4},{6,7},{7,6},{8,9},{9,8},{10,11... | collective-permute-start | bytes 2850824 | tf_op jit(solution)/shard_map/ppermute | solution.py:19
  56.6 7.0 %collective-permute-start.11 = (bf16[128,3712]{1,0:T(8,128)(2,1)S(1)}, bf16[128,3712]{1,0:T(8,128)(2,1)S(1)}, u32[]{:S(2)}, u32[]{:S(2)}) collective-permute-start(bf16[128,3712]{1,0:T(8,128)(2,1)S(1)} %collective-permute-done.8.refs_2_), channel_id=1, source_target_pairs={{0,1},{1,0},{2,3},{3,2},{4,5},{5,4},{6,7},{7,6},{8,9},{9,8},{10,11... | collective-permute-start | bytes 2850824 | tf_op jit(solution)/shard_map/ppermute | solution.py:19
  56.6 24.2 %collective-permute-start.12 = (bf16[128,3712]{1,0:T(8,128)(2,1)S(1)}, bf16[128,3712]{1,0:T(8,128)(2,1)S(1)}, u32[]{:S(2)}, u32[]{:S(2)}) collective-permute-start(bf16[128,3712]{1,0:T(8,128)(2,1)S(1)} %collective-permute-done.8.refs_2_), channel_id=1, source_target_pairs={{0,2},{1,3},{2,0},{3,1},{4,6},{5,7},{6,4},{7,5},{8,10},{9,11},{10,... | collective-permute-start | bytes 2850824 | tf_op jit(solution)/shard_map/ppermute | solution.py:19
  60.1 22.5 %collective-permute-start.14 = (bf16[256,1792]{1,0:T(8,128)(2,1)S(1)}, bf16[256,1792]{1,0:T(8,128)(2,1)S(1)}, u32[]{:S(2)}, u32[]{:S(2)}) collective-permute-start(bf16[256,1792]{1,0:T(8,128)(2,1)S(1)} %fusion), channel_id=1, source_target_pairs={{0,16},{16,0},{1,17},{17,1},{2,18},{18,2},{3,19},{19,3},{4,20},{20... | collective-permute-start | bytes 2752520 | tf_op jit(solution)/shard_map/ppermute | solution.py:19
  61.7 22.0 %collective-permute-start.15 = (bf16[128,3712]{1,0:T(8,128)(2,1)S(1)}, bf16[128,3712]{1,0:T(8,128)(2,1)S(1)}, u32[]{:S(2)}, u32[]{:S(2)}) collective-permute-start(bf16[128,3712]{1,0:T(8,128)(2,1)S(1)} %collective-permute-done.8.refs_2_), channel_id=1, source_target_pairs={{4,0},{5,1},{6,2},{7,3},{8,12},{9,13},{10,14},{11,15},{20,16},{21,... | collective-permute-start | bytes 2850824 | tf_op jit(solution)/shard_map/ppermute | solution.py:233
  82.6 4.2 %collective-permute-start.19 = (bf16[2,256,1792]{2,1,0:T(8,128)(2,1)S(1)}, bf16[2,256,1792]{2,1,0:T(8,128)(2,1)S(1)}, u32[]{:S(2)}, u32[]{:S(2)}) collective-permute-start(bf16[2,256,1792]{2,1,0:T(8,128)(2,1)S(1)} %get-tuple-element.87), channel_id=1, source_target_pairs={{0,1},{1,0},{2,3},{3,2},{4,5},{5,4},{6,7},{7,6},{8,9},{9,8},{10,11... | collective-permute-start | bytes 5505032 | tf_op jit(solution)/shard_map/ppermute | solution.py:19
  82.6 6.3 %collective-permute-start.16 = (bf16[128,3712]{1,0:T(8,128)(2,1)S(1)}, bf16[128,3712]{1,0:T(8,128)(2,1)S(1)}, u32[]{:S(2)}, u32[]{:S(2)}) collective-permute-start(bf16[128,3712]{1,0:T(8,128)(2,1)S(1)} %collective-permute-done.12.refs_1_), channel_id=1, source_target_pairs={{0,1},{1,0},{2,3},{3,2},{4,5},{5,4},{6,7},{7,6},{8,9},{9,8},{10,11... | collective-permute-start | bytes 2850824 | tf_op jit(solution)/shard_map/ppermute | solution.py:19
  85.3 23.5 %collective-permute-start.18 = (bf16[128,3712]{1,0:T(8,128)(2,1)S(1)}, bf16[128,3712]{1,0:T(8,128)(2,1)S(1)}, u32[]{:S(2)}, u32[]{:S(2)}) collective-permute-start(bf16[128,3712]{1,0:T(8,128)(2,1)S(1)} %broadcast_select_fusion.refs_2_), channel_id=1, source_target_pairs={{0,2},{1,3},{2,0},{3,1},{4,6},{5,7},{6,4},{7,5},{8,10},{9,11},{10,... | collective-permute-start | bytes 2850824 | tf_op jit(solution)/shard_map/ppermute | solution.py:19
  87.0 22.5 %collective-permute-start.21 = (bf16[256,1792]{1,0:T(8,128)(2,1)S(1)}, bf16[256,1792]{1,0:T(8,128)(2,1)S(1)}, u32[]{:S(2)}, u32[]{:S(2)}) collective-permute-start(bf16[256,1792]{1,0:T(8,128)(2,1)S(1)} %fusion.1), channel_id=1, source_target_pairs={{0,16},{16,0},{1,17},{17,1},{2,18},{18,2},{3,19},{19,3},{4,20},{20... | collective-permute-start | bytes 2752520 | tf_op jit(solution)/shard_map/ppermute | solution.py:19
  88.2 20.7 %collective-permute-start.20 = (bf16[128,1792]{1,0:T(8,128)(2,1)S(1)}, bf16[128,1792]{1,0:T(8,128)(2,1)S(1)}, u32[]{:S(2)}, u32[]{:S(2)}) collective-permute-start(bf16[128,1792]{1,0:T(8,128)(2,1)S(1)} %fusion.15), channel_id=1, source_target_pairs={{0,4},{1,5},{2,6},{3,7},{4,0},{5,1},{6,2},{7,3},{8,12},{9,13},{10,... | collective-permute-start | bytes 1376264 | tf_op jit(solution)/shard_map/ppermute | solution.py:19
  109.6 5.1 %collective-permute-start.22 = (bf16[128,3712]{1,0:T(8,128)(2,1)S(1)}, bf16[128,3712]{1,0:T(8,128)(2,1)S(1)}, u32[]{:S(2)}, u32[]{:S(2)}) collective-permute-start(bf16[128,3712]{1,0:T(8,128)(2,1)S(1)} %collective-permute-done.18.refs_1_), channel_id=1, source_target_pairs={{0,1},{1,0},{2,3},{3,2},{4,5},{5,4},{6,7},{7,6},{8,9},{9,8},{10,11... | collective-permute-start | bytes 2850824 | tf_op jit(solution)/shard_map/ppermute | solution.py:19
  110.5 17.2 %collective-permute-start.27 = (bf16[96,1792]{1,0:T(8,128)(2,1)S(1)}, bf16[96,1792]{1,0:T(8,128)(2,1)S(1)}, u32[]{:S(2)}, u32[]{:S(2)}) collective-permute-start(bf16[96,1792]{1,0:T(8,128)(2,1)S(1)} %slice.162), channel_id=1, source_target_pairs={{0,8},{1,9},{2,10},{3,11},{4,12},{5,13},{6,14},{7,15},{8,0},{9,1},... | collective-permute-start | bytes 1032200 | tf_op jit(solution)/shard_map/ppermute | solution.py:19
  113.6 12.6 %collective-permute-start.24 = (bf16[128,1792]{1,0:T(8,128)(2,1)S(1)}, bf16[128,1792]{1,0:T(8,128)(2,1)S(1)}, u32[]{:S(2)}, u32[]{:S(2)}) collective-permute-start(bf16[128,1792]{1,0:T(8,128)(2,1)S(1)} %get-tuple-element.114), channel_id=1, source_target_pairs={{0,16},{16,0},{1,17},{17,1},{2,18},{18,2},{3,19},{19,3},{4,20},{20... | collective-permute-start | bytes 1376264 | tf_op jit(solution)/shard_map/ppermute | solution.py:19
  126.2 5.2 %collective-permute-start.25 = (bf16[2,128,1792]{2,1,0:T(8,128)(2,1)S(1)}, bf16[2,128,1792]{2,1,0:T(8,128)(2,1)S(1)}, u32[]{:S(2)}, u32[]{:S(2)}) collective-permute-start(bf16[2,128,1792]{2,1,0:T(8,128)(2,1)S(1)} %get-tuple-element.96), channel_id=1, source_target_pairs={{0,1},{1,0},{2,3},{3,2},{4,5},{5,4},{6,7},{7,6},{8,9},{9,8},{10,11... | collective-permute-start | bytes 2752520 | tf_op jit(solution)/shard_map/ppermute | solution.py:19
  126.3 18.2 %collective-permute-start.31 = (bf16[128,1792]{1,0:T(8,128)(2,1)S(1)}, bf16[128,1792]{1,0:T(8,128)(2,1)S(1)}, u32[]{:S(2)}, u32[]{:S(2)}) collective-permute-start(bf16[128,1792]{1,0:T(8,128)(2,1)S(1)} %get-tuple-element.113), channel_id=1, source_target_pairs={{0,16},{16,0},{1,17},{17,1},{2,18},{18,2},{3,19},{19,3},{4,20},{20... | collective-permute-start | bytes 1376264 | tf_op jit(solution)/shard_map/ppermute | solution.py:19
  127.9 27.2 %collective-permute-start.28 = (bf16[160,1792]{1,0:T(8,128)(2,1)S(1)}, bf16[160,1792]{1,0:T(8,128)(2,1)S(1)}, u32[]{:S(2)}, u32[]{:S(2)}) collective-permute-start(bf16[160,1792]{1,0:T(8,128)(2,1)S(1)} %pad_maximum_fusion), channel_id=1, source_target_pairs={{0,8},{1,9},{2,10},{3,11},{4,12},{5,13},{6,14},{7,15},{8,0},{9,1},... | collective-permute-start | bytes 1720328 | tf_op jit(solution)/shard_map/ppermute | solution.py:19
  131.6 23.5 %collective-permute-start.29 = (bf16[128,1792]{1,0:T(8,128)(2,1)S(1)}, bf16[128,1792]{1,0:T(8,128)(2,1)S(1)}, u32[]{:S(2)}, u32[]{:S(2)}) collective-permute-start(bf16[128,1792]{1,0:T(8,128)(2,1)S(1)} %get-tuple-element.116), channel_id=1, source_target_pairs={{0,2},{1,3},{2,0},{3,1},{4,6},{5,7},{6,4},{7,5},{8,10},{9,11},{10,... | collective-permute-start | bytes 1376264 | tf_op jit(solution)/shard_map/ppermute | solution.py:19
  132.3 22.8 %collective-permute-start.26 = (bf16[128,1792]{1,0:T(8,128)(2,1)S(1)}, bf16[128,1792]{1,0:T(8,128)(2,1)S(1)}, u32[]{:S(2)}, u32[]{:S(2)}) collective-permute-start(bf16[128,1792]{1,0:T(8,128)(2,1)S(1)} %get-tuple-element.99), channel_id=1, source_target_pairs={{0,4},{1,5},{2,6},{3,7},{4,0},{5,1},{6,2},{7,3},{8,12},{9,13},{10,... | collective-permute-start | bytes 1376264 | tf_op jit(solution)/shard_map/ppermute | solution.py:19
  132.3 22.8 %collective-permute-start.30 = (bf16[128,1792]{1,0:T(8,128)(2,1)S(1)}, bf16[128,1792]{1,0:T(8,128)(2,1)S(1)}, u32[]{:S(2)}, u32[]{:S(2)}) collective-permute-start(bf16[128,1792]{1,0:T(8,128)(2,1)S(1)} %get-tuple-element.115), channel_id=1, source_target_pairs={{0,18},{1,19},{2,16},{3,17},{4,22},{5,23},{6,20},{7,21},{8,26},{9,... | collective-permute-start | bytes 1376264 | tf_op jit(solution)/shard_map/ppermute | solution.py:230
  155.4 22.3 %collective-permute-start.34 = (bf16[128,1792]{1,0:T(8,128)(2,1)S(1)}, bf16[128,1792]{1,0:T(8,128)(2,1)S(1)}, u32[]{:S(2)}, u32[]{:S(2)}) collective-permute-start(bf16[128,1792]{1,0:T(8,128)(2,1)S(1)} %fusion.4), channel_id=1, source_target_pairs={{0,12},{1,13},{2,14},{3,15},{4,8},{5,9},{6,10},{7,11},{8,4},{9,5},... | collective-permute-start | bytes 1376264 | tf_op jit(solution)/shard_map/ppermute | solution.py:19
  156.6 21.1 %collective-permute-start.33 = (bf16[128,1792]{1,0:T(8,128)(2,1)S(1)}, bf16[128,1792]{1,0:T(8,128)(2,1)S(1)}, u32[]{:S(2)}, u32[]{:S(2)}) collective-permute-start(bf16[128,1792]{1,0:T(8,128)(2,1)S(1)} %fusion.22), channel_id=1, source_target_pairs={{0,16},{16,0},{1,17},{17,1},{2,18},{18,2},{3,19},{19,3},{4,20},{20... | collective-permute-start | bytes 1376264 | tf_op jit(solution)/shard_map/ppermute | solution.py:19
  157.3 20.5 %collective-permute-start.32 = (bf16[128,1792]{1,0:T(8,128)(2,1)S(1)}, bf16[128,1792]{1,0:T(8,128)(2,1)S(1)}, u32[]{:S(2)}, u32[]{:S(2)}) collective-permute-start(bf16[128,1792]{1,0:T(8,128)(2,1)S(1)} %fusion.6), channel_id=1, source_target_pairs={{0,2},{1,3},{2,0},{3,1},{4,6},{5,7},{6,4},{7,5},{8,10},{9,11},{10,... | collective-permute-start | bytes 1376264 | tf_op jit(solution)/shard_map/ppermute | solution.py:19
  (7 other events, 30.5 us)

commit v7 on v6

--- a/solution.py
+++ b/solution.py
@@ -308,7 +308,8 @@
         total_1, *_ = together(owned(kept_1, met_1, of(came_1, lower), lower).astype(bf16), *sends)
         home_1 = exchange(total_1, "expert", 4)
         kept_3, sent_3 = routed(inputs)
-        kept_3, sent_3, row_far, home_1, *came_2 = together(kept_3, sent_3, row_far, home_1, *came_2)
+        kept_3, sent_3, home_1, *came_2 = together(kept_3, sent_3, home_1, *came_2)
+        row_far, *came_2 = together(row_far, *came_2)
 
         inputs = [row_far, over_core(row_far)]
         met_3 = over_core(sent_3)

time: 179 us -> 201 us (1.12)
  waiting for transfers between devices: 49.9 us -> 72.9 us
    ppermute x30, waiting for transfers between devices: 38.8 us -> 61.8 us  [exchange(): return lax.ppermute(value, axis, pairs)]
  transfers between devices with their start and end apart: 35 -> 35, of which waited for: 16 -> 15; matrix products, arithmetic and copies ran while one was open for 4% -> 4% of each run, Pallas kernels for 47% -> 42%
where the time goes in v7:
time: 201 us; the launch traced here: 200 us
  Pallas kernels  85.9 us (43%)
  waiting for transfers between devices  72.9 us (36%)
  starting transfers between devices  31.7 us (16%)
  other arithmetic  8.3 us (4%)
    pallas_call x6, Pallas kernels, ffn(): pl.pallas_call(body, out_shape=[jax.ShapeDtypeStruct((blocks, count, widt...  83.7 us
    ppermute x30, waiting for transfers between devices, exchange(): return lax.ppermute(value, axis, pairs)  61.8 us
    ppermute x30, starting transfers between devices, exchange(): return lax.ppermute(value, axis, pairs)  23.1 us
    ppermute x4, waiting for transfers between devices, over_planes(): lax.ppermute(value, 'expert', [(4 * s + k, 4 * t + k) for s, t in pairs f...  11.1 us
    ppermute x4, starting transfers between devices, over_planes(): lax.ppermute(value, 'expert', [(4 * s + k, 4 * t + k) for s, t in pairs f...  7.1 us
  transfers between devices with their start and end apart: 35, of which 15 were waited for; matrix products, arithmetic and copies ran while one was open for 4% of the time, Pallas kernels for 42%

profile of v7, /device:TPU:8, one launch (start us, length us, event | category | flops | bytes accessed | tf_op | source)
XLA Modules:
  0.0 200.5 jit_solution(4616888967907248683)
XLA Ops:
  0.0 2.2 %widen.1.refs_1_ = bf16[128,3712]{1,0:T(8,128)(2,1)S(1)} custom-call(bf16[128,3584]{1,0:T(8,128)(2,1)} %refs_1_, s32[8,128]{1,0:T(8,128)} %bitcast.85, f32[8,128]{1,0:T(8,128)} %bitcast.86), custom_call_target="tpu_custom_call" | custom-call | tf_op jit(solution)/shard_map/widen/pallas_call | solution.py:42
  2.3 5.0 %collective-permute-start.2 = (bf16[128,3712]{1,0:T(8,128)(2,1)S(1)}, bf16[128,3712]{1,0:T(8,128)(2,1)}, u32[]{:S(2)}, u32[]{:S(2)}) collective-permute-start(bf16[128,3712]{1,0:T(8,128)(2,1)S(1)} %widen.1.refs_1_), channel_id=1, source_target_pairs={{4,8},{5,9},{6,10},{7,11},{8,4},{9,5},{10,6},{11,7},{20,24},{21,25... | collective-permute-start | bytes 2850824 | tf_op jit(solution)/shard_map/ppermute | solution.py:233
  7.4 1.6 collective-permute-start.4
  10.3 11.5 %routed_expert.5 = (bf16[2,128,1792]{2,1,0:T(8,128)(2,1)S(1)}, bf16[2,128,1792]{2,1,0:T(8,128)(2,1)}) custom-call(s32[2]{0:T(128)S(1)} %pad_add_fusion.refs_0_, bf16[128,3712]{1,0:T(8,128)(2,1)S(1)} %widen.1.refs_1_, bf16[128,3712]{1,0:T(8,128)(2,1)S(1)} %collective-permute-done.refs_2_, bf16[3584,1024]{1,0:T(8,128)(2,1)} %bitcast.70, ...), custom_call_target="tpu_custom_call" | custom-call | flops 5637144576 | bytes 25690112 | tf_op jit(solution)/shard_map/routed_expert/pallas_call | solution.py:179
  22.0 3.9 %collective-permute-done.1.refs_2_ = bf16[128,3712]{1,0:T(8,128)(2,1)} collective-permute-done((bf16[128,3712]{1,0:T(8,128)(2,1)S(1)}, bf16[128,3712]{1,0:T(8,128)(2,1)}, u32[]{:S(2)}, u32[]{:S(2)}) %collective-permute-start.1) | collective-permute-done | bytes 950304 | tf_op jit(solution)/shard_map/ppermute | solution.py:233
  25.8 3.0 %collective-permute-done.2 = bf16[128,3712]{1,0:T(8,128)(2,1)} collective-permute-done((bf16[128,3712]{1,0:T(8,128)(2,1)S(1)}, bf16[128,3712]{1,0:T(8,128)(2,1)}, u32[]{:S(2)}, u32[]{:S(2)}) %collective-permute-start.2) | collective-permute-done | bytes 950304 | tf_op jit(solution)/shard_map/ppermute | solution.py:233
  28.9 1.5 collective-permute-start.7
  33.1 1.6 collective-permute-start.9
  34.7 16.9 %routed_expert.6 = (bf16[2,256,1792]{2,1,0:T(8,128)(2,1)S(1)}, bf16[2,256,1792]{2,1,0:T(8,128)(2,1)S(1)}) custom-call(s32[2]{0:T(128)S(1)} %pad_add_fusion.refs_0_, bf16[128,3712]{1,0:T(8,128)(2,1)} %collective-permute-done.4.refs_1_, bf16[128,3712]{1,0:T(8,128)(2,1)} %collective-permute-done.1.refs_2_, ...), custom_call_target="tpu_custom_call" | custom-call | flops 11274289152 | bytes 29360128 | tf_op jit(solution)/shard_map/routed_expert/pallas_call | solution.py:179
  52.5 3.6 %collective-permute-done.8.refs_2_ = bf16[128,3712]{1,0:T(8,128)(2,1)S(1)} collective-permute-done((bf16[128,3712]{1,0:T(8,128)(2,1)S(1)}, bf16[128,3712]{1,0:T(8,128)(2,1)S(1)}, u32[]{:S(2)}, u32[]{:S(2)}) %collective-permute-start.8) | collective-permute-done | bytes 950304 | tf_op jit(solution)/shard_map/ppermute | solution.py:233
  56.6 1.5 collective-permute-start.12
  58.2 1.8 collective-permute-done.13
  60.1 1.6 collective-permute-start.14
  61.7 1.9 collective-permute-start.15
  63.7 17.2 %routed_expert.7 = (bf16[2,256,1792]{2,1,0:T(8,128)(2,1)S(1)}, bf16[2,256,1792]{2,1,0:T(8,128)(2,1)S(1)}) custom-call(s32[2]{0:T(128)S(1)} %pad_add_fusion.refs_0_, bf16[128,3712]{1,0:T(8,128)(2,1)S(1)} %collective-permute-done.7.refs_1_, bf16[128,3712]{1,0:T(8,128)(2,1)S(1)} %collective-permute-done.8.refs_2_, ...), custom_call_target="tpu_custom_call" | custom-call | flops 11274289152 | bytes 29360128 | tf_op jit(solution)/shard_map/routed_expert/pallas_call | solution.py:179
  80.9 1.7 collective-permute-done.14
  83.7 1.4 broadcast_select_fusion.refs_2_
  86.6 1.6 collective-permute-start.20
  89.1 17.2 %routed_expert.8 = (bf16[2,256,1792]{2,1,0:T(8,128)(2,1)S(1)}, bf16[2,256,1792]{2,1,0:T(8,128)(2,1)S(1)}) custom-call(s32[2]{0:T(128)S(1)} %pad_add_fusion.refs_0_, bf16[128,3712]{1,0:T(8,128)(2,1)S(1)} %collective-permute-done.12.refs_1_, bf16[128,3712]{1,0:T(8,128)(2,1)S(1)} %broadcast_select_fusion.refs_2_, ...), custom_call_target="tpu_custom_call" | custom-call | flops 11274289152 | bytes 29360128 | tf_op jit(solution)/shard_map/routed_expert/pallas_call | solution.py:179
  106.3 2.7 %collective-permute-done.20 = bf16[256,1792]{1,0:T(8,128)(2,1)S(1)} collective-permute-done((bf16[256,1792]{1,0:T(8,128)(2,1)S(1)}, bf16[256,1792]{1,0:T(8,128)(2,1)S(1)}, u32[]{:S(2)}, u32[]{:S(2)}) %collective-permute-start.20) | collective-permute-done | bytes 917536 | tf_op jit(solution)/shard_map/ppermute | solution.py:19
  109.1 1.5 collective-permute-start.21
  110.6 21.9 %collective-permute-done.21.refs_1_ = bf16[128,3712]{1,0:T(8,128)(2,1)S(1)} collective-permute-done((bf16[128,3712]{1,0:T(8,128)(2,1)S(1)}, bf16[128,3712]{1,0:T(8,128)(2,1)S(1)}, u32[]{:S(2)}, u32[]{:S(2)}) %collective-permute-start.21) | collective-permute-done | bytes 950304 | tf_op jit(solution)/shard_map/ppermute | solution.py:19
  132.9 1.7 collective-permute-start.27
  135.4 11.3 %routed_expert.9 = (bf16[2,128,1792]{2,1,0:T(8,128)(2,1)S(1)}, bf16[2,128,1792]{2,1,0:T(8,128)(2,1)S(1)}) custom-call(s32[2]{0:T(128)S(1)} %pad_add_fusion.refs_0_, bf16[128,3712]{1,0:T(8,128)(2,1)S(1)} %collective-permute-done.21.refs_1_, bf16[128,3712]{1,0:T(8,128)(2,1)S(1)} %collective-permute-done.22.refs_2_, bf16[3584,1024]{1,0:T(8,128)(2,1)} %bitcast.74, ...), custom_call_target="tpu_custom_call" | custom-call | flops 5637144576 | bytes 25690112 | tf_op jit(solution)/shard_map/routed_expert/pallas_call | solution.py:179
  148.4 1.5 collective-permute-done.27
  150.2 3.4 %collective-permute-start.28 = (bf16[160,1792]{1,0:T(8,128)(2,1)S(1)}, bf16[160,1792]{1,0:T(8,128)(2,1)S(1)}, u32[]{:S(2)}, u32[]{:S(2)}) collective-permute-start(bf16[160,1792]{1,0:T(8,128)(2,1)S(1)} %pad_maximum_fusion), channel_id=1, source_target_pairs={{0,8},{1,9},{2,10},{3,11},{4,12},{5,13},{6,14},{7,15},{8,0},{9,1},... | collective-permute-start | bytes 1720328 | tf_op jit(solution)/shard_map/ppermute | solution.py:19
  154.4 1.5 collective-permute-start.30
  157.2 9.5 %shared_expert.1 = f32[2,128,1792]{2,1,0:T(8,128)S(1)} custom-call(s32[2]{0:T(128)S(1)} %pad_add_fusion.refs_0_, bf16[128,3584]{1,0:T(8,128)(2,1)S(1)} %copy-done, bf16[3584,1024]{1,0:T(8,128)(2,1)} %refs_2_.1, bf16[3584,1024]{1,0:T(8,128)(2,1)} %refs_3_.1, bf16[1024,3584]{1,0:T(8,128)(2,1)} %refs_4_.1), custom_call_target="tpu_custom_call" | custom-call | flops 2818572288 | bytes 23855104 | tf_op jit(solution)/shard_map/shared_expert/pallas_call | solution.py:179
  166.7 10.0 %collective-permute-done.28 = bf16[160,1792]{1,0:T(8,128)(2,1)S(1)} collective-permute-done((bf16[160,1792]{1,0:T(8,128)(2,1)S(1)}, bf16[160,1792]{1,0:T(8,128)(2,1)S(1)}, u32[]{:S(2)}, u32[]{:S(2)}) %collective-permute-start.28) | collective-permute-done | bytes 573472 | tf_op jit(solution)/shard_map/ppermute | solution.py:19
  177.0 1.6 collective-permute-start.34
  179.6 1.4 collective-permute-start.32
  181.1 18.3 %collective-permute-done.34 = bf16[128,1792]{1,0:T(8,128)(2,1)S(1)} collective-permute-done((bf16[128,1792]{1,0:T(8,128)(2,1)S(1)}, bf16[128,1792]{1,0:T(8,128)(2,1)S(1)}, u32[]{:S(2)}, u32[]{:S(2)}) %collective-permute-start.34) | collective-permute-done | bytes 458784 | tf_op jit(solution)/shard_map/ppermute | solution.py:19
  (74 shorter events, 16.3 us)
Async XLA Ops:
  2.2 8.1 %collective-permute-start = (bf16[128,3712]{1,0:T(8,128)(2,1)S(1)}, bf16[128,3712]{1,0:T(8,128)(2,1)S(1)}, u32[]{:S(2)}, u32[]{:S(2)}) collective-permute-start(bf16[128,3712]{1,0:T(8,128)(2,1)S(1)} %widen.1.refs_1_), channel_id=1, source_target_pairs={{0,1},{1,0},{2,3},{3,2},{4,5},{5,4},{6,7},{7,6},{8,9},{9,8},{10,11... | collective-permute-start | bytes 2850824 | tf_op jit(solution)/shard_map/ppermute | solution.py:19
  2.3 23.6 %collective-permute-start.1 = (bf16[128,3712]{1,0:T(8,128)(2,1)S(1)}, bf16[128,3712]{1,0:T(8,128)(2,1)}, u32[]{:S(2)}, u32[]{:S(2)}) collective-permute-start(bf16[128,3712]{1,0:T(8,128)(2,1)S(1)} %widen.1.refs_1_), channel_id=1, source_target_pairs={{0,4},{1,5},{2,6},{3,7},{4,0},{5,1},{6,2},{7,3},{8,12},{9,13},{10,... | collective-permute-start | bytes 2850824 | tf_op jit(solution)/shard_map/ppermute | solution.py:233
  2.3 26.5 %collective-permute-start.2 = (bf16[128,3712]{1,0:T(8,128)(2,1)S(1)}, bf16[128,3712]{1,0:T(8,128)(2,1)}, u32[]{:S(2)}, u32[]{:S(2)}) collective-permute-start(bf16[128,3712]{1,0:T(8,128)(2,1)S(1)} %widen.1.refs_1_), channel_id=1, source_target_pairs={{4,8},{5,9},{6,10},{7,11},{8,4},{9,5},{10,6},{11,7},{20,24},{21,25... | collective-permute-start | bytes 2850824 | tf_op jit(solution)/shard_map/ppermute | solution.py:233
  7.4 23.0 %collective-permute-start.4 = (bf16[128,3712]{1,0:T(8,128)(2,1)S(1)}, bf16[128,3712]{1,0:T(8,128)(2,1)}, u32[]{:S(2)}, u32[]{:S(2)}) collective-permute-start(bf16[128,3712]{1,0:T(8,128)(2,1)S(1)} %widen.1.refs_1_), channel_id=1, source_target_pairs={{0,2},{1,3},{2,0},{3,1},{4,6},{5,7},{6,4},{7,5},{8,10},{9,11},{10,... | collective-permute-start | bytes 2850824 | tf_op jit(solution)/shard_map/ppermute | solution.py:19
  21.9 8.5 %collective-permute-start.3 = (bf16[2,128,1792]{2,1,0:T(8,128)(2,1)}, bf16[2,128,1792]{2,1,0:T(8,128)(2,1)}, u32[]{:S(2)}, u32[]{:S(2)}) collective-permute-start(bf16[2,128,1792]{2,1,0:T(8,128)(2,1)} %get-tuple-element.61), channel_id=1, source_target_pairs={{0,1},{1,0},{2,3},{3,2},{4,5},{5,4},{6,7},{7,6},{8,9},{9,8},{10,11... | collective-permute-start | bytes 2752520 | tf_op jit(solution)/shard_map/ppermute | solution.py:19
  28.9 5.8 %collective-permute-start.6 = (bf16[128,3712]{1,0:T(8,128)(2,1)}, bf16[128,3712]{1,0:T(8,128)(2,1)S(1)}, u32[]{:S(2)}, u32[]{:S(2)}) collective-permute-start(bf16[128,3712]{1,0:T(8,128)(2,1)} %collective-permute-done.1.refs_2_), channel_id=1, source_target_pairs={{0,1},{1,0},{2,3},{3,2},{4,5},{5,4},{6,7},{7,6},{8,9},{9,8},{10,11... | collective-permute-start | bytes 2850824 | tf_op jit(solution)/shard_map/ppermute | solution.py:19
  28.9 23.7 %collective-permute-start.7 = (bf16[128,3712]{1,0:T(8,128)(2,1)}, bf16[128,3712]{1,0:T(8,128)(2,1)S(1)}, u32[]{:S(2)}, u32[]{:S(2)}) collective-permute-start(bf16[128,3712]{1,0:T(8,128)(2,1)} %collective-permute-done.1.refs_2_), channel_id=1, source_target_pairs={{0,2},{1,3},{2,0},{3,1},{4,6},{5,7},{6,4},{7,5},{8,10},{9,11},{10,... | collective-permute-start | bytes 2850824 | tf_op jit(solution)/shard_map/ppermute | solution.py:19
  30.4 4.3 %collective-permute-start.5 = (bf16[128,3712]{1,0:T(8,128)(2,1)}, bf16[128,3712]{1,0:T(8,128)(2,1)S(1)}, u32[]{:S(2)}, u32[]{:S(2)}) collective-permute-start(bf16[128,3712]{1,0:T(8,128)(2,1)} %collective-permute-done.4.refs_1_), channel_id=1, source_target_pairs={{0,1},{1,0},{2,3},{3,2},{4,5},{5,4},{6,7},{7,6},{8,9},{9,8},{10,11... | collective-permute-start | bytes 2850824 | tf_op jit(solution)/shard_map/ppermute | solution.py:19
  31.9 24.2 %collective-permute-start.8 = (bf16[128,3712]{1,0:T(8,128)(2,1)S(1)}, bf16[128,3712]{1,0:T(8,128)(2,1)S(1)}, u32[]{:S(2)}, u32[]{:S(2)}) collective-permute-start(bf16[128,3712]{1,0:T(8,128)(2,1)S(1)} %broadcast_select_fusion.1), channel_id=1, source_target_pairs={{0,8},{1,9},{2,10},{3,11},{12,4},{13,5},{14,6},{15,7},{4,0},{5,1},... | collective-permute-start | bytes 2850824 | tf_op jit(solution)/shard_map/ppermute | solution.py:233
  33.1 23.0 %collective-permute-start.9 = (bf16[128,1792]{1,0:T(8,128)(2,1)S(1)}, bf16[128,1792]{1,0:T(8,128)(2,1)S(1)}, u32[]{:S(2)}, u32[]{:S(2)}) collective-permute-start(bf16[128,1792]{1,0:T(8,128)(2,1)S(1)} %fusion.17), channel_id=1, source_target_pairs={{0,16},{16,0},{1,17},{17,1},{2,18},{18,2},{3,19},{19,3},{4,20},{20... | collective-permute-start | bytes 1376264 | tf_op jit(solution)/shard_map/ppermute | solution.py:19
  56.1 7.5 %collective-permute-start.10 = (bf16[128,3712]{1,0:T(8,128)(2,1)S(1)}, bf16[128,3712]{1,0:T(8,128)(2,1)S(1)}, u32[]{:S(2)}, u32[]{:S(2)}) collective-permute-start(bf16[128,3712]{1,0:T(8,128)(2,1)S(1)} %collective-permute-done.7.refs_1_), channel_id=1, source_target_pairs={{0,1},{1,0},{2,3},{3,2},{4,5},{5,4},{6,7},{7,6},{8,9},{9,8},{10,11... | collective-permute-start | bytes 2850824 | tf_op jit(solution)/shard_map/ppermute | solution.py:19
  56.6 7.0 %collective-permute-start.11 = (bf16[128,3712]{1,0:T(8,128)(2,1)S(1)}, bf16[128,3712]{1,0:T(8,128)(2,1)S(1)}, u32[]{:S(2)}, u32[]{:S(2)}) collective-permute-start(bf16[128,3712]{1,0:T(8,128)(2,1)S(1)} %collective-permute-done.8.refs_2_), channel_id=1, source_target_pairs={{0,1},{1,0},{2,3},{3,2},{4,5},{5,4},{6,7},{7,6},{8,9},{9,8},{10,11... | collective-permute-start | bytes 2850824 | tf_op jit(solution)/shard_map/ppermute | solution.py:19
  56.6 24.2 %collective-permute-start.12 = (bf16[128,3712]{1,0:T(8,128)(2,1)S(1)}, bf16[128,3712]{1,0:T(8,128)(2,1)S(1)}, u32[]{:S(2)}, u32[]{:S(2)}) collective-permute-start(bf16[128,3712]{1,0:T(8,128)(2,1)S(1)} %collective-permute-done.8.refs_2_), channel_id=1, source_target_pairs={{0,2},{1,3},{2,0},{3,1},{4,6},{5,7},{6,4},{7,5},{8,10},{9,11},{10,... | collective-permute-start | bytes 2850824 | tf_op jit(solution)/shard_map/ppermute | solution.py:19
  60.1 22.5 %collective-permute-start.14 = (bf16[256,1792]{1,0:T(8,128)(2,1)S(1)}, bf16[256,1792]{1,0:T(8,128)(2,1)S(1)}, u32[]{:S(2)}, u32[]{:S(2)}) collective-permute-start(bf16[256,1792]{1,0:T(8,128)(2,1)S(1)} %fusion), channel_id=1, source_target_pairs={{0,16},{16,0},{1,17},{17,1},{2,18},{18,2},{3,19},{19,3},{4,20},{20... | collective-permute-start | bytes 2752520 | tf_op jit(solution)/shard_map/ppermute | solution.py:19
  61.7 22.0 %collective-permute-start.15 = (bf16[128,3712]{1,0:T(8,128)(2,1)S(1)}, bf16[128,3712]{1,0:T(8,128)(2,1)S(1)}, u32[]{:S(2)}, u32[]{:S(2)}) collective-permute-start(bf16[128,3712]{1,0:T(8,128)(2,1)S(1)} %collective-permute-done.8.refs_2_), channel_id=1, source_target_pairs={{4,0},{5,1},{6,2},{7,3},{8,12},{9,13},{10,14},{11,15},{20,16},{21,... | collective-permute-start | bytes 2850824 | tf_op jit(solution)/shard_map/ppermute | solution.py:233
  82.6 5.6 %collective-permute-start.16 = (bf16[128,3712]{1,0:T(8,128)(2,1)S(1)}, bf16[128,3712]{1,0:T(8,128)(2,1)S(1)}, u32[]{:S(2)}, u32[]{:S(2)}) collective-permute-start(bf16[128,3712]{1,0:T(8,128)(2,1)S(1)} %collective-permute-done.12.refs_1_), channel_id=1, source_target_pairs={{0,1},{1,0},{2,3},{3,2},{4,5},{5,4},{6,7},{7,6},{8,9},{9,8},{10,11... | collective-permute-start | bytes 2850824 | tf_op jit(solution)/shard_map/ppermute | solution.py:19
  85.1 4.0 %collective-permute-start.17 = (bf16[128,3712]{1,0:T(8,128)(2,1)S(1)}, bf16[128,3712]{1,0:T(8,128)(2,1)S(1)}, u32[]{:S(2)}, u32[]{:S(2)}) collective-permute-start(bf16[128,3712]{1,0:T(8,128)(2,1)S(1)} %broadcast_select_fusion.refs_2_), channel_id=1, source_target_pairs={{0,1},{1,0},{2,3},{3,2},{4,5},{5,4},{6,7},{7,6},{8,9},{9,8},{10,11... | collective-permute-start | bytes 2850824 | tf_op jit(solution)/shard_map/ppermute | solution.py:19
  86.6 22.5 %collective-permute-start.20 = (bf16[256,1792]{1,0:T(8,128)(2,1)S(1)}, bf16[256,1792]{1,0:T(8,128)(2,1)S(1)}, u32[]{:S(2)}, u32[]{:S(2)}) collective-permute-start(bf16[256,1792]{1,0:T(8,128)(2,1)S(1)} %fusion.1), channel_id=1, source_target_pairs={{0,16},{16,0},{1,17},{17,1},{2,18},{18,2},{3,19},{19,3},{4,20},{20... | collective-permute-start | bytes 2752520 | tf_op jit(solution)/shard_map/ppermute | solution.py:19
  88.2 18.2 %collective-permute-start.19 = (bf16[128,1792]{1,0:T(8,128)(2,1)S(1)}, bf16[128,1792]{1,0:T(8,128)(2,1)S(1)}, u32[]{:S(2)}, u32[]{:S(2)}) collective-permute-start(bf16[128,1792]{1,0:T(8,128)(2,1)S(1)} %fusion.15), channel_id=1, source_target_pairs={{0,4},{1,5},{2,6},{3,7},{4,0},{5,1},{6,2},{7,3},{8,12},{9,13},{10,... | collective-permute-start | bytes 1376264 | tf_op jit(solution)/shard_map/ppermute | solution.py:19
  109.1 25.5 %collective-permute-start.23 = (bf16[2,256,1792]{2,1,0:T(8,128)(2,1)S(1)}, bf16[2,256,1792]{2,1,0:T(8,128)(2,1)S(1)}, u32[]{:S(2)}, u32[]{:S(2)}) collective-permute-start(bf16[2,256,1792]{2,1,0:T(8,128)(2,1)S(1)} %get-tuple-element.96), channel_id=1, source_target_pairs={{0,1},{1,0},{2,3},{3,2},{4,5},{5,4},{6,7},{7,6},{8,9},{9,8},{10,11... | collective-permute-start | bytes 5505032 | tf_op jit(solution)/shard_map/ppermute | solution.py:19
  109.1 23.5 %collective-permute-start.21 = (bf16[128,3712]{1,0:T(8,128)(2,1)S(1)}, bf16[128,3712]{1,0:T(8,128)(2,1)S(1)}, u32[]{:S(2)}, u32[]{:S(2)}) collective-permute-start(bf16[128,3712]{1,0:T(8,128)(2,1)S(1)} %broadcast_select_fusion.refs_2_), channel_id=1, source_target_pairs={{0,2},{1,3},{2,0},{3,1},{4,6},{5,7},{6,4},{7,5},{8,10},{9,11},{10,... | collective-permute-start | bytes 2850824 | tf_op jit(solution)/shard_map/ppermute | solution.py:19
  132.9 17.0 %collective-permute-start.27 = (bf16[96,1792]{1,0:T(8,128)(2,1)S(1)}, bf16[96,1792]{1,0:T(8,128)(2,1)S(1)}, u32[]{:S(2)}, u32[]{:S(2)}) collective-permute-start(bf16[96,1792]{1,0:T(8,128)(2,1)S(1)} %slice.162), channel_id=1, source_target_pairs={{0,8},{1,9},{2,10},{3,11},{4,12},{5,13},{6,14},{7,15},{8,0},{9,1},... | collective-permute-start | bytes 1032200 | tf_op jit(solution)/shard_map/ppermute | solution.py:19
  134.8 12.7 %collective-permute-start.24 = (bf16[128,1792]{1,0:T(8,128)(2,1)S(1)}, bf16[128,1792]{1,0:T(8,128)(2,1)S(1)}, u32[]{:S(2)}, u32[]{:S(2)}) collective-permute-start(bf16[128,1792]{1,0:T(8,128)(2,1)S(1)} %get-tuple-element.116), channel_id=1, source_target_pairs={{0,16},{16,0},{1,17},{17,1},{2,18},{18,2},{3,19},{19,3},{4,20},{20... | collective-permute-start | bytes 1376264 | tf_op jit(solution)/shard_map/ppermute | solution.py:19
  147.5 6.1 %collective-permute-start.25 = (bf16[2,128,1792]{2,1,0:T(8,128)(2,1)S(1)}, bf16[2,128,1792]{2,1,0:T(8,128)(2,1)S(1)}, u32[]{:S(2)}, u32[]{:S(2)}) collective-permute-start(bf16[2,128,1792]{2,1,0:T(8,128)(2,1)S(1)} %get-tuple-element.98), channel_id=1, source_target_pairs={{0,1},{1,0},{2,3},{3,2},{4,5},{5,4},{6,7},{7,6},{8,9},{9,8},{10,11... | collective-permute-start | bytes 2752520 | tf_op jit(solution)/shard_map/ppermute | solution.py:19
  147.5 19.2 %collective-permute-start.31 = (bf16[128,1792]{1,0:T(8,128)(2,1)S(1)}, bf16[128,1792]{1,0:T(8,128)(2,1)S(1)}, u32[]{:S(2)}, u32[]{:S(2)}) collective-permute-start(bf16[128,1792]{1,0:T(8,128)(2,1)S(1)} %get-tuple-element.115), channel_id=1, source_target_pairs={{0,16},{16,0},{1,17},{17,1},{2,18},{18,2},{3,19},{19,3},{4,20},{20... | collective-permute-start | bytes 1376264 | tf_op jit(solution)/shard_map/ppermute | solution.py:19
  150.2 26.6 %collective-permute-start.28 = (bf16[160,1792]{1,0:T(8,128)(2,1)S(1)}, bf16[160,1792]{1,0:T(8,128)(2,1)S(1)}, u32[]{:S(2)}, u32[]{:S(2)}) collective-permute-start(bf16[160,1792]{1,0:T(8,128)(2,1)S(1)} %pad_maximum_fusion), channel_id=1, source_target_pairs={{0,8},{1,9},{2,10},{3,11},{4,12},{5,13},{6,14},{7,15},{8,0},{9,1},... | collective-permute-start | bytes 1720328 | tf_op jit(solution)/shard_map/ppermute | solution.py:19
  153.9 22.9 %collective-permute-start.29 = (bf16[128,1792]{1,0:T(8,128)(2,1)S(1)}, bf16[128,1792]{1,0:T(8,128)(2,1)S(1)}, u32[]{:S(2)}, u32[]{:S(2)}) collective-permute-start(bf16[128,1792]{1,0:T(8,128)(2,1)S(1)} %get-tuple-element.118), channel_id=1, source_target_pairs={{0,2},{1,3},{2,0},{3,1},{4,6},{5,7},{6,4},{7,5},{8,10},{9,11},{10,... | collective-permute-start | bytes 1376264 | tf_op jit(solution)/shard_map/ppermute | solution.py:19
  154.4 22.3 %collective-permute-start.26 = (bf16[128,1792]{1,0:T(8,128)(2,1)S(1)}, bf16[128,1792]{1,0:T(8,128)(2,1)S(1)}, u32[]{:S(2)}, u32[]{:S(2)}) collective-permute-start(bf16[128,1792]{1,0:T(8,128)(2,1)S(1)} %get-tuple-element.101), channel_id=1, source_target_pairs={{0,4},{1,5},{2,6},{3,7},{4,0},{5,1},{6,2},{7,3},{8,12},{9,13},{10,... | collective-permute-start | bytes 1376264 | tf_op jit(solution)/shard_map/ppermute | solution.py:19
  154.4 22.3 %collective-permute-start.30 = (bf16[128,1792]{1,0:T(8,128)(2,1)S(1)}, bf16[128,1792]{1,0:T(8,128)(2,1)S(1)}, u32[]{:S(2)}, u32[]{:S(2)}) collective-permute-start(bf16[128,1792]{1,0:T(8,128)(2,1)S(1)} %get-tuple-element.117), channel_id=1, source_target_pairs={{0,18},{1,19},{2,16},{3,17},{4,22},{5,23},{6,20},{7,21},{8,26},{9,... | collective-permute-start | bytes 1376264 | tf_op jit(solution)/shard_map/ppermute | solution.py:230
  177.0 22.3 %collective-permute-start.34 = (bf16[128,1792]{1,0:T(8,128)(2,1)S(1)}, bf16[128,1792]{1,0:T(8,128)(2,1)S(1)}, u32[]{:S(2)}, u32[]{:S(2)}) collective-permute-start(bf16[128,1792]{1,0:T(8,128)(2,1)S(1)} %fusion.4), channel_id=1, source_target_pairs={{0,12},{1,13},{2,14},{3,15},{4,8},{5,9},{6,10},{7,11},{8,4},{9,5},... | collective-permute-start | bytes 1376264 | tf_op jit(solution)/shard_map/ppermute | solution.py:19
  178.7 20.6 %collective-permute-start.33 = (bf16[128,1792]{1,0:T(8,128)(2,1)S(1)}, bf16[128,1792]{1,0:T(8,128)(2,1)S(1)}, u32[]{:S(2)}, u32[]{:S(2)}) collective-permute-start(bf16[128,1792]{1,0:T(8,128)(2,1)S(1)} %fusion.22), channel_id=1, source_target_pairs={{0,16},{16,0},{1,17},{17,1},{2,18},{18,2},{3,19},{19,3},{4,20},{20... | collective-permute-start | bytes 1376264 | tf_op jit(solution)/shard_map/ppermute | solution.py:19
  179.6 19.8 %collective-permute-start.32 = (bf16[128,1792]{1,0:T(8,128)(2,1)S(1)}, bf16[128,1792]{1,0:T(8,128)(2,1)S(1)}, u32[]{:S(2)}, u32[]{:S(2)}) collective-permute-start(bf16[128,1792]{1,0:T(8,128)(2,1)S(1)} %fusion.6), channel_id=1, source_target_pairs={{0,2},{1,3},{2,0},{3,1},{4,6},{5,7},{6,4},{7,5},{8,10},{9,11},{10,... | collective-permute-start | bytes 1376264 | tf_op jit(solution)/shard_map/ppermute | solution.py:19
  (7 other events, 31.3 us)
